TPU v7x, 256 devices: a whole 4x4x8 slice. The times are simulated.
256 devices in a mesh: band: 32 (over y_lo, z, core), fft: 8 (over y_hi, x).
Axes of the slice: x: 4, y: 4 (y_hi: 2, y_lo: 2; y = y_hi * 2 + y_lo), z: 8, core: 2. Of those that a mesh axis runs over, the one named last changes fastest.
Arguments:
- orbitals: float32 [32, 2, 96, 9216], P('band', None, 'fft'), may hold values from -3 to 3
- serve_order: int32 [32], replicated, may hold values from 0 to 31, each once
Outputs:
- applied: float32 [32, 2, 96, 9216], P('band', None, 'fft')
- serving_exchange: float32 [2, 2, 96, 9216], P(None, None, 'fft', 'band')
Inputs may be any that keep to these rules, and one draw needn't show every extreme that they name: `serve_order`: a permutation of the 32 band numbers.
All inputs are finite; a program needn't handle non-finite values.
Results may differ from a plain program's by a relative error of at most 0.0001.
Values sent between devices are 32-bit elements; how exact they have to be, the bound alone decides.
No kernel may reach another device: no remote copies, remote signals or barrier semaphores. Data moves between devices by JAX's collectives and lax.ppermute only.
A program may use at most 320 MiB of HBM per device.

v0:
```python
import math

import jax
import jax.numpy as jnp
from jax import lax
from jax.sharding import PartitionSpec as P

NX = 96
NY = 96
NZ = 96
SERVE = 2


cell_side = 41.04
mixing = 0.25


def spread(block, axis, source):
    block = jnp.where(lax.axis_index(axis) == source, block, jnp.zeros_like(block))
    return lax.psum(block, axis)


def frequencies(count):
    signed = (jnp.arange(count, dtype=jnp.int32) + count // 2) % count - count // 2
    return signed.astype(jnp.float32) * (2.0 * math.pi / cell_side)


def kernel_columns(start, width):
    freq_x = frequencies(NX)
    freq_y = lax.dynamic_slice_in_dim(frequencies(NY), start, width)
    freq_z = frequencies(NZ)
    squared = freq_x[:, None, None] ** 2 + freq_y[None, :, None] ** 2 + freq_z[None, None, :] ** 2
    radius = cell_side * (3.0 / (4.0 * math.pi)) ** (1.0 / 3.0)
    safe_square = jnp.where(squared > 0, squared, 1.0)
    general = 4.0 * math.pi * (1.0 - jnp.cos(jnp.sqrt(safe_square) * radius)) / safe_square
    return jnp.where(squared > 0, general, 2.0 * math.pi * radius * radius)


def dft_tables(count):
    indices = jnp.arange(count, dtype=jnp.int32)
    product = indices[:, None] * indices[None, :] % count
    angles = product.astype(jnp.float32) * (2.0 * math.pi / count)
    cosine = jnp.cos(angles)
    sine = jnp.sin(angles)
    forward = jnp.stack(
        [jnp.stack([cosine, sine], axis=1), jnp.stack([-sine, cosine], axis=1)], axis=0
    )
    inverse = jnp.stack(
        [jnp.stack([cosine, -sine], axis=1), jnp.stack([sine, cosine], axis=1)], axis=0
    )
    return (forward, inverse)


def transform(field, einsum_form, table):
    return jnp.einsum(einsum_form, table, field, precision=lax.Precision.HIGHEST)


def shards(orbitals, serve_order):
    local_bands = orbitals.shape[0]
    plane_rows = orbitals.shape[2]
    fft_parts = lax.axis_size("fft")
    column_rows = NY // fft_parts
    rank_fft = lax.axis_index("fft")
    table_x = dft_tables(NX)
    table_y = dft_tables(NY)
    table_z = dft_tables(NZ)
    kernel = kernel_columns(rank_fft * column_rows, column_rows)
    scaling = 1.0 / (NX * NY * NZ)
    pieces = []
    for member in range(SERVE):
        band_id = serve_order[member]
        owner = band_id // local_bands
        position = band_id % local_bands
        owned = lax.dynamic_index_in_dim(orbitals, position, 0, keepdims=False)
        pieces.append(spread(owned, "band", owner))
    served = jnp.stack(pieces)
    served = served.reshape(SERVE, 2, plane_rows, NY, NZ)
    served_real = served[:, 0]
    served_imag = served[:, 1]
    fields = orbitals.reshape(local_bands, 2, plane_rows, NY, NZ)
    band_real = fields[:, 0]
    band_imag = fields[:, 1]
    density_real = served_real[None] * band_real[:, None] + served_imag[None] * band_imag[:, None]
    density_imag = served_real[None] * band_imag[:, None] - served_imag[None] * band_real[:, None]
    density = jnp.stack([density_real, density_imag], axis=2)
    results = []
    for member in range(SERVE):
        pair_density = density[0, member][None]
        pair_density = transform(pair_density, "akbz,pbxyz->paxyk", table_z[0])
        pair_density = transform(pair_density, "akby,pbxyz->paxkz", table_y[0])
        spectrum = transform(
            lax.all_to_all(pair_density, "fft", split_axis=3, concat_axis=2, tiled=True),
            "akbx,pbxyz->pakyz",
            table_x[0],
        )
        spectrum = spectrum * kernel[None, None]
        spectrum = transform(spectrum, "akbx,pbxyz->pakyz", table_x[1])
        pair_density = lax.all_to_all(spectrum, "fft", split_axis=2, concat_axis=3, tiled=True)
        pair_density = transform(pair_density, "akby,pbxyz->paxkz", table_y[1])
        pair_density = transform(pair_density, "akbz,pbxyz->paxyk", table_z[1])
        results.append((pair_density * scaling)[0])
    potential = jnp.stack(results).reshape(local_bands, SERVE, 2, plane_rows, NY, NZ)
    pot_real = potential[:, :, 0]
    pot_imag = potential[:, :, 1]
    applied_real = -mixing * jnp.sum(
        served_real[None] * pot_real - served_imag[None] * pot_imag, axis=1
    )
    applied_imag = -mixing * jnp.sum(
        served_real[None] * pot_imag + served_imag[None] * pot_real, axis=1
    )
    applied = jnp.stack([applied_real, applied_imag], axis=1).reshape(
        local_bands, 2, plane_rows, NY * NZ
    )
    terms_real = jnp.sum(band_real[:, None] * pot_real + band_imag[:, None] * pot_imag, axis=0)
    terms_imag = jnp.sum(band_imag[:, None] * pot_real - band_real[:, None] * pot_imag, axis=0)
    terms = jnp.stack([terms_real, terms_imag], axis=1).reshape(SERVE, 2, plane_rows, NY * NZ)
    summed = lax.psum_scatter(terms, "band", scatter_dimension=3, tiled=True)
    serving_exchange = -mixing * summed
    return (applied, serving_exchange)


def solution(mesh):
    return jax.shard_map(
        shards,
        mesh=mesh,
        in_specs=(P("band", None, "fft", None), P()),
        out_specs=(P("band", None, "fft", None), P(None, None, "fft", "band")),
        check_vma=False,
    )
```

profile of v0, /device:TPU:4, one launch (start us, length us, event | category | flops | bytes accessed | tf_op | source)
XLA Modules:
  0.0 679.9 jit_solution(16127234719145530380)
XLA Ops:
  7.2 1.3 fusion.66
  9.8 1.8 broadcast_select_fusion
  11.6 0.8 stack.35
  12.4 1.1 copy.55
  13.6 0.8 stack.34
  14.4 1.1 copy.54
  15.6 1.1 copy-done.2
  16.7 0.8 reshape.481
  17.6 0.2 fusion.48
  17.8 0.2 fusion.45
  18.0 1.3 slice_bitcast_fusion.3
  19.4 228.9 %all-reduce.3.cloned.1.call-done = (f32[1,2,12,96,96]{4,3,2,0,1:T(8,128)}, f32[1,2,12,96,96]{4,3,2,0,1:T(8,128)}) async-done(((f32[1,2,12,96,96]{4,3,2,0,1:T(8,128)}, f32[1,2,12,96,96]{4,3,2,0,1:T(8,128)}), (f32[1,2,12,96,96]{4,3,2,0,1:T(8,128)}, f32[1,2,12,96,96]{4,3,2,0,1:T(8,128)})) %all-reduce.3.cloned.1.call-update) | async-done | bytes 1769488 | tf_op jit(solution)/shard_map/psum | solution.py:20
  248.2 1.4 constant_dynamic-update-slice_fusion.1
  249.7 0.2 copy-done.5
  250.0 1.1 copy-done.3
  251.1 0.4 fusion.14
  251.4 1.1 convolution_bitcast_fusion.5
  252.6 3.0 convolution_bitcast_fusion.4
  255.6 2.4 copy.71
  257.9 7.0 %all-to-all-start.2 = ((f32[1,2,12,96,96]{4,1,2,0,3:T(2,128)}), f32[1,2,12,96,96]{4,1,2,0,3:T(2,128)}, u32[]{:S(2)}, u32[]{:S(2)}) async-start(f32[1,2,12,96,96]{4,1,2,0,3:T(2,128)} %copy.71), calls=%async_computation.2 | async-start | bytes 2359296 | tf_op jit(solution)/shard_map/all_to_all | solution.py:92
  265.1 1.1 convolution_bitcast_fusion.11
  266.2 2.0 convolution_bitcast_fusion.10
  268.2 1.4 copy.61
  269.6 11.6 %all-to-all-done.2 = f32[1,2,12,96,96]{4,1,2,0,3:T(2,128)} async-done(((f32[1,2,12,96,96]{4,1,2,0,3:T(2,128)}), f32[1,2,12,96,96]{4,1,2,0,3:T(2,128)}, u32[]{:S(2)}, u32[]{:S(2)}) %all-to-all-start.2) | async-done | bytes 884768 | tf_op jit(solution)/shard_map/all_to_all | solution.py:92
  281.2 6.3 all-to-all-start
  287.6 2.2 fusion.26
  289.8 1.8 copy.72
  291.8 2.0 fusion.6
  293.8 1.1 convolution_bitcast_fusion.2
  294.9 1.4 copy.75
  296.3 7.4 %all-to-all-done = f32[1,2,12,96,96]{4,1,2,0,3:T(2,128)S(1)} async-done(((f32[1,2,12,96,96]{4,1,2,0,3:T(2,128)}), f32[1,2,12,96,96]{4,1,2,0,3:T(2,128)S(1)}, u32[]{:S(2)}, u32[]{:S(2)}) %all-to-all-start) | async-done | bytes 884768 | tf_op jit(solution)/shard_map/all_to_all | solution.py:92
  303.7 1.0 copy-done.1
  304.7 6.2 all-to-all-start.3
  310.9 1.8 copy.62
  312.8 2.0 fusion.4
  314.8 1.1 convolution_bitcast_fusion.8
  315.9 1.4 copy.65
  317.3 9.6 %all-to-all-done.3 = f32[1,2,96,12,96]{4,1,3,0,2:T(2,128)S(1)} async-done(((f32[1,2,96,12,96]{4,1,3,0,2:T(2,128)}), f32[1,2,96,12,96]{4,1,3,0,2:T(2,128)S(1)}, u32[]{:S(2)}, u32[]{:S(2)}) %all-to-all-start.3) | async-done | bytes 884768 | tf_op jit(solution)/shard_map/all_to_all | solution.py:98
  327.0 6.2 all-to-all-start.1
  333.1 0.2 reduce-scatter.4.cloned.1.call-start
  333.3 2.2 mul.447
  335.6 1.2 mul.450
  336.8 2.1 convolution_bitcast_fusion.1
  338.9 2.0 fusion.7
  341.0 8.2 %all-to-all-done.1 = f32[1,2,96,12,96]{4,1,3,0,2:T(2,128)S(1)} async-done(((f32[1,2,96,12,96]{4,1,3,0,2:T(2,128)}), f32[1,2,96,12,96]{4,1,3,0,2:T(2,128)S(1)}, u32[]{:S(2)}, u32[]{:S(2)}) %all-to-all-start.1) | async-done | bytes 884768 | tf_op jit(solution)/shard_map/all_to_all | solution.py:98
  349.2 0.1 copy.66
  349.3 2.1 convolution_bitcast_fusion.7
  351.4 2.0 fusion.5
  353.5 0.2 maximum_bitcast_fusion
  353.7 1.6 fusion.65
  355.3 2.0 reshape.523
  357.2 3.0 reshape.524
  360.2 3.2 multiply_add_fusion
  363.4 2.1 pad_maximum_fusion
  365.5 73.1 %copy.128 = f32[2,2,12,9216]{0,2,1,3:T(8,128)} copy(f32[2,2,12,9216]{3,0,2,1:T(2,128)} %pad_maximum_fusion) | data formatting | bytes 3538944
  438.5 106.3 %reshape.525 = f32[9216,48]{1,0:T(8,128)} reshape(f32[9216,2,12,2]{3,2,1,0:T(8,128)} %bitcast.105) | data formatting | bytes 3538944
  544.9 2.4 fusion.17
  547.3 0.3 mul.442
  547.7 0.3 mul.446
  548.1 1.6 copy.83
  549.7 113.1 %reduce-scatter.4.cloned.1.call-done = f32[288,48]{1,0:T(8,128)} async-done(((f32[9216,48]{1,0:T(8,128)}), f32[288,48]{1,0:T(8,128)}) %reduce-scatter.4.cloned.1.call-update) | async-done | bytes 55312
  662.8 5.6 reshape.526
  668.4 3.4 copy.129
  671.9 0.7 copy.84
  (24 shorter events, 0.8 us)
Async XLA Ops:
  7.2 241.1 %all-reduce.3.cloned.1.call-start = ((), (), s32[]{:S(2)}) async-start(), calls=%async_computation.6 | async-start | bytes 4718592 | tf_op jit(solution)/shard_map/psum | solution.py:20
  15.5 1.2 copy-start.2
  248.2 1.6 copy-start.5
  249.9 1.2 copy-start.3
  250.0 1.5 copy-start
  257.9 23.3 %all-to-all-start.2 = ((f32[1,2,12,96,96]{4,1,2,0,3:T(2,128)}), f32[1,2,12,96,96]{4,1,2,0,3:T(2,128)}, u32[]{:S(2)}, u32[]{:S(2)}) async-start(f32[1,2,12,96,96]{4,1,2,0,3:T(2,128)} %copy.71), calls=%async_computation.2 | async-start | bytes 2359296 | tf_op jit(solution)/shard_map/all_to_all | solution.py:92
  281.2 22.4 %all-to-all-start = ((f32[1,2,12,96,96]{4,1,2,0,3:T(2,128)}), f32[1,2,12,96,96]{4,1,2,0,3:T(2,128)S(1)}, u32[]{:S(2)}, u32[]{:S(2)}) async-start(f32[1,2,12,96,96]{4,1,2,0,3:T(2,128)} %copy.61), calls=%async_computation | async-start | bytes 2359296 | tf_op jit(solution)/shard_map/all_to_all | solution.py:92
  303.7 1.0 copy-start.1
  304.7 22.3 %all-to-all-start.3 = ((f32[1,2,96,12,96]{4,1,3,0,2:T(2,128)}), f32[1,2,96,12,96]{4,1,3,0,2:T(2,128)S(1)}, u32[]{:S(2)}, u32[]{:S(2)}) async-start(f32[1,2,96,12,96]{4,1,3,0,2:T(2,128)} %copy.75), calls=%async_computation.3 | async-start | bytes 2359296 | tf_op jit(solution)/shard_map/all_to_all | solution.py:98
  327.0 22.3 %all-to-all-start.1 = ((f32[1,2,96,12,96]{4,1,3,0,2:T(2,128)}), f32[1,2,96,12,96]{4,1,3,0,2:T(2,128)S(1)}, u32[]{:S(2)}, u32[]{:S(2)}) async-start(f32[1,2,96,12,96]{4,1,3,0,2:T(2,128)} %copy.65), calls=%async_computation.1 | async-start | bytes 2359296 | tf_op jit(solution)/shard_map/all_to_all | solution.py:98
  333.1 2.5 copy-start.4
  333.1 329.7 %reduce-scatter.4.cloned.1.call-start = ((), (), s32[]{:S(2)}) async-start(), calls=%async_computation.5 | async-start | bytes 4866048
Sparse Core Ops, SparseCore 0:
  15.7 232.4 all-reduce.2
  545.0 117.7 reduce-scatter.3
where the time goes:
time: 692 us; the launch traced here: 680 us
  waiting for transfers between devices  379 us (55%)
  local copies, waits for them, and re-layouts  224 us (32%)
  starting transfers between devices  25.9 us (4%)
  matrix products  21.8 us (3%)
  between operations  16.1 us (2%)
  other arithmetic  13.1 us (2%)
    psum x1, waiting for transfers between devices, spread(): return lax.psum(block, axis)  229 us
    unnamed x20, local copies, waits for them, and re-layouts  197 us
    unnamed x3, waiting for transfers between devices  113 us
    dot_general x12, matrix products, transform(): jnp.einsum(einsum_form, table, field, precision=lax.Precision.HIGHEST)  21.8 us
    all_to_all x2, waiting for transfers between devices, shards(): lax.all_to_all(pair_density, 'fft', split_axis=3, concat_axis=2, tiled=True)  19 us
    all_to_all x2, waiting for transfers between devices, shards(): lax.all_to_all(spectrum, 'fft', split_axis=2, concat_axis=3, tiled=True)  17.9 us
  transfers between devices with their start and end apart: 6, of which 6 were waited for; matrix products, arithmetic and copies ran while one was open for 5% of the time, Pallas kernels for 0%

commit v1 on v0

v1 whole, which is shorter than its diff:
```python
import math

import jax
import jax.numpy as jnp
from jax import lax
from jax.sharding import PartitionSpec as P

NX = 96
NY = 96
NZ = 96
SERVE = 2
CHIPS = 16
ROWS = 24
PLANE = NY * NZ

cell_side = 41.04
mixing = 0.25


def frequencies(count):
    signed = (jnp.arange(count, dtype=jnp.int32) + count // 2) % count - count // 2
    return signed.astype(jnp.float32) * (2.0 * math.pi / cell_side)


def kernel_columns(start, width):
    freq_x = frequencies(NX)
    freq_y = lax.dynamic_slice_in_dim(frequencies(NY), start, width)
    freq_z = frequencies(NZ)
    squared = freq_x[:, None, None] ** 2 + freq_y[None, :, None] ** 2 + freq_z[None, None, :] ** 2
    radius = cell_side * (3.0 / (4.0 * math.pi)) ** (1.0 / 3.0)
    safe_square = jnp.where(squared > 0, squared, 1.0)
    general = 4.0 * math.pi * (1.0 - jnp.cos(jnp.sqrt(safe_square) * radius)) / safe_square
    return jnp.where(squared > 0, general, 2.0 * math.pi * radius * radius)


def dft_tables(count):
    indices = jnp.arange(count, dtype=jnp.int32)
    product = indices[:, None] * indices[None, :] % count
    angles = product.astype(jnp.float32) * (2.0 * math.pi / count)
    cosine = jnp.cos(angles)
    sine = jnp.sin(angles)
    forward = jnp.stack(
        [jnp.stack([cosine, sine], axis=1), jnp.stack([-sine, cosine], axis=1)], axis=0
    )
    inverse = jnp.stack(
        [jnp.stack([cosine, -sine], axis=1), jnp.stack([sine, cosine], axis=1)], axis=0
    )
    return (forward, inverse)


def transform(field, einsum_form, table):
    return jnp.einsum(einsum_form, table, field, precision=lax.Precision.HIGHEST)


def conj_times(left, right):
    lr, li = left[:12], left[12:]
    rr, ri = right[:12], right[12:]
    return jnp.concatenate([lr * rr + li * ri, lr * ri - li * rr], axis=0)


def times(left, right):
    lr, li = left[:12], left[12:]
    rr, ri = right[:12], right[12:]
    return jnp.concatenate([lr * rr - li * ri, lr * ri + li * rr], axis=0)


def shards(orbitals, serve_order):
    rank_fft = lax.axis_index("fft")
    rank_band = lax.axis_index("band")
    core = rank_band % 2
    chip = rank_band // 2
    swap = [(i, i ^ 1) for i in range(32)]
    same_core = [[2 * i + c for i in range(CHIPS)] for c in range(2)]
    table = dft_tables(96)
    kernel = kernel_columns(rank_fft * 12, 12).reshape(NX, 12, NZ) * (1.0 / (NX * NY * NZ))

    def chips_exchange(blocks):
        return lax.all_to_all(blocks, "band", 0, 0, axis_index_groups=same_core, tiled=True)

    def fft_exchange(blocks):
        return lax.all_to_all(blocks, "fft", 0, 0, tiled=True)

    mine = orbitals.reshape(ROWS, PLANE)
    other = lax.ppermute(mine, "band", swap)
    serving = serve_order[core]
    candidate = jnp.where(serving % 2 == core, mine, other)
    blocks = candidate.reshape(ROWS, CHIPS, PLANE // CHIPS).transpose(1, 0, 2)
    blocks = chips_exchange(blocks)
    block = lax.dynamic_index_in_dim(blocks, serving // 2, 0, keepdims=True)
    blocks = chips_exchange(jnp.broadcast_to(block, blocks.shape))
    served = blocks.transpose(1, 0, 2).reshape(ROWS, PLANE)

    density = jnp.stack([conj_times(served, mine), conj_times(served, other)])
    field = density.reshape(2, 2, 12, NY, NZ)
    field = transform(field, "akbz,pbxyz->paxyk", table[0])
    field = transform(field, "akby,pbxyz->paxkz", table[0])
    blocks = field.reshape(2, ROWS, 8, 12 * NZ).transpose(2, 0, 1, 3)
    blocks = fft_exchange(blocks)
    field = blocks.reshape(8, 2, 2, 12, 12, NZ).transpose(1, 2, 0, 3, 4, 5).reshape(2, 2, NX, 12, NZ)
    field = transform(field, "akbx,pbxyz->pakyz", table[0])
    field = field * kernel
    field = transform(field, "akbx,pbxyz->pakyz", table[1])
    blocks = field.reshape(2, 2, 8, 12, 12 * NZ).transpose(2, 0, 1, 3, 4).reshape(8, 2, ROWS, 12 * NZ)
    blocks = fft_exchange(blocks)
    field = blocks.transpose(1, 2, 0, 3).reshape(2, 2, 12, NY, NZ)
    field = transform(field, "akby,pbxyz->paxkz", table[1])
    field = transform(field, "akbz,pbxyz->paxyk", table[1])
    potential = field.reshape(2, ROWS, PLANE)

    sent = lax.ppermute(times(served, potential[1]), "band", swap)
    applied = -mixing * (times(served, potential[0]) + sent)
    terms = conj_times(potential[0], mine) + conj_times(potential[1], other)
    blocks = terms.reshape(ROWS, CHIPS, PLANE // CHIPS).transpose(1, 0, 2)
    blocks = chips_exchange(blocks)
    summed = -mixing * jnp.sum(blocks, axis=0)
    half = PLANE // CHIPS // 2
    keep = lax.dynamic_slice_in_dim(summed, core * half, half, 1)
    give = lax.dynamic_slice_in_dim(summed, (1 - core) * half, half, 1)
    got = lax.ppermute(give, "band", swap)
    first = jnp.where(core == 0, keep, got)
    second = jnp.where(core == 0, got, keep)
    serving_exchange = jnp.stack([first, second]).reshape(SERVE, 2, 12, half)
    return (applied.reshape(1, 2, 12, PLANE), serving_exchange)


def solution(mesh):
    return jax.shard_map(
        shards,
        mesh=mesh,
        in_specs=(P("band", None, "fft", None), P()),
        out_specs=(P("band", None, "fft", None), P(None, None, "fft", "band")),
        check_vma=False,
    )
```

time: 692 us -> 270 us (0.39)
  the two profiles are of different devices: /device:TPU:4 before, /device:TPU:1 now
where the time goes in v1:
time: 270 us; the launch traced here: 266 us
  waiting for transfers between devices  108 us (40%)
  local copies, waits for them, and re-layouts  75.3 us (28%)
  starting transfers between devices  38.9 us (14%)
  matrix products  26.6 us (10%)
  other arithmetic  14 us (5%)
  between operations  3.84 us (1%)
    all_to_all x3, waiting for transfers between devices, chips_exchange(): lax.all_to_all(blocks, 'band', 0, 0, axis_index_groups=same_core, tiled=T...  65.8 us
    all_to_all x2, waiting for transfers between devices, fft_exchange(): return lax.all_to_all(blocks, 'fft', 0, 0, tiled=True)  41.8 us
    dot_general x6, matrix products, transform(): jnp.einsum(einsum_form, table, field, precision=lax.Precision.HIGHEST)  26.6 us
    all_to_all x3, starting transfers between devices, chips_exchange(): lax.all_to_all(blocks, 'band', 0, 0, axis_index_groups=same_core, tiled=T...  20.5 us
    all_to_all x2, starting transfers between devices, fft_exchange(): return lax.all_to_all(blocks, 'fft', 0, 0, tiled=True)  11.1 us
    slice x7, local copies, waits for them, and re-layouts, times(): rr, ri = (right[:12], right[12:])  10.1 us
    transpose x2, local copies, waits for them, and re-layouts, transform(): jnp.einsum(einsum_form, table, field, precision=lax.Precision.HIGHEST)  7.78 us
    reshape x2, local copies, waits for them, and re-layouts, shards(): field.reshape(2, 2, 8, 12, 12 * NZ).transpose(2, 0, 1, 3, 4)  6.15 us
  transfers between devices with their start and end apart: 8, of which 5 were waited for; matrix products, arithmetic and copies ran while one was open for 6% of the time, Pallas kernels for 0%

profile of v1, /device:TPU:1, one launch (start us, length us, event | category | flops | bytes accessed | tf_op | source)
XLA Modules:
  0.0 266.2 jit_solution(3385957570722619570)
XLA Ops:
  0.6 1.4 copy.35
  2.2 3.3 %collective-permute-start = (f32[24,9216]{1,0:T(8,128)S(1)}, f32[24,9216]{1,0:T(8,128)S(1)}, u32[]{:S(2)}, u32[]{:S(2)}) collective-permute-start(f32[24,9216]{1,0:T(8,128)S(1)} %reshape.201), channel_id=1, source_target_pairs={{0,8},{8,0},{16,24},{24,16},{32,40},{40,32},{48,56},{56,48},{64,72... | collective-permute-start | bytes 2654216 | tf_op jit(solution)/shard_map/ppermute | solution.py:84
  8.1 1.0 broadcast_select_fusion
  9.1 1.5 reshape.202
  10.6 1.3 copy.89
  11.9 7.6 %all-to-all-start = ((f32[16,24,576]{2,1,0:T(8,128)}), f32[16,24,576]{2,1,0:T(8,128)S(1)}, u32[]{:S(2)}, u32[]{:S(2)}) async-start(f32[16,24,576]{2,1,0:T(8,128)} %bitcast.155), calls=%async_computation | async-start | bytes 1966080 | tf_op jit(solution)/shard_map/all_to_all | solution.py:78
  20.1 23.4 %all-to-all-done = f32[16,24,576]{2,1,0:T(8,128)S(1)} async-done(((f32[16,24,576]{2,1,0:T(8,128)}), f32[16,24,576]{2,1,0:T(8,128)S(1)}, u32[]{:S(2)}, u32[]{:S(2)}) %all-to-all-start) | async-done | bytes 884768 | tf_op jit(solution)/shard_map/all_to_all | solution.py:78
  43.5 1.0 broadcast_in_dim.10
  44.5 6.5 %all-to-all-start.1 = ((f32[16,24,576]{2,1,0:T(8,128)}), f32[16,24,576]{2,1,0:T(8,128)S(1)}, u32[]{:S(2)}, u32[]{:S(2)}) async-start(f32[16,24,576]{2,1,0:T(8,128)} %broadcast_in_dim.10), calls=%async_computation.1 | async-start | bytes 1966080 | tf_op jit(solution)/shard_map/all_to_all | solution.py:78
  51.4 0.7 fusion.37
  52.1 22.1 %all-to-all-done.1 = f32[16,24,576]{2,1,0:T(8,128)S(1)} async-done(((f32[16,24,576]{2,1,0:T(8,128)}), f32[16,24,576]{2,1,0:T(8,128)S(1)}, u32[]{:S(2)}, u32[]{:S(2)}) %all-to-all-start.1) | async-done | bytes 884768 | tf_op jit(solution)/shard_map/all_to_all | solution.py:78
  74.2 0.9 fusion.58
  75.1 0.9 copy.39
  76.1 1.2 slice.91
  77.3 0.9 copy.37
  78.2 1.2 slice.87
  79.8 1.4 pad_maximum_fusion
  81.1 2.7 %stack.57 = f32[1,2,12,96,96]{4,3,2,1,0:T(8,128)} reshape(f32[24,9216]{1,0:T(8,128)} %get-tuple-element.45) | data formatting | bytes 1769472 | tf_op jit(solution)/shard_map/stack | solution.py:93
  83.8 2.7 stack.56
  86.5 3.8 %fusion.10 = f32[2,12,96,2,96,1]{4,2,5,3,1,0:T(8,128)S(1)} fusion(f32[1,96,2,96]{3,1,2,0:T(8,128)} %get-tuple-element.37, f32[1,96,2,96]{3,1,2,0:T(8,128)} %get-tuple-element.40, f32[1,2,12,96,96]{4,3,2,1,0:T(8,128)} %stack.57, f32[1,2,12,96,96]{4,3,2,1,0:T(8,128)} %stack.56), kind=kOutput, calls=%fused_computation.12 | convolution fusion | flops 1019695104 | bytes 3686400 | tf_op jit(solution)/shard_map/akbz,pbxyz->paxyk/dot_general | solution.py:52
  90.3 5.5 %fusion.15 = f32[2,2,12,96,96]{3,4,1,2,0:T(8,128)} fusion(f32[2,12,96,2,96,1]{4,2,5,3,1,0:T(8,128)S(1)} %fusion.10, f32[1,96,2,96]{3,1,2,0:T(8,128)S(1)} %copy-done.11, f32[1,96,2,96]{3,1,2,0:T(8,128)S(1)} %copy-done.13), kind=kOutput, calls=%fused_computation.15 | convolution fusion | flops 1019252736 | bytes 3686400 | tf_op jit(solution)/shard_map/akby,pbxyz->paxkz/dot_general | solution.py:52
  95.7 3.1 %copy.44 = f32[2,2,12,96,96]{4,3,2,1,0:T(8,128)} copy(f32[2,2,12,96,96]{3,4,1,2,0:T(8,128)} %fusion.15) | data formatting | bytes 3538944 | tf_op jit(solution)/shard_map/akby,pbxyz->paxkz/transpose | solution.py:52
  98.8 3.0 %reshape.203 = f32[2,24,8,1152]{3,2,1,0:T(8,128)} reshape(f32[2,2,12,96,96]{4,3,2,1,0:T(8,128)} %copy.44) | data formatting | bytes 3538944 | tf_op jit(solution)/shard_map/reshape | solution.py:97
  101.8 3.1 %copy.45 = f32[8,2,24,1152]{3,2,1,0:T(8,128)} copy(f32[8,2,24,1152]{3,0,2,1:T(8,128)} %bitcast.153) | data formatting | bytes 3538944 | tf_op jit(solution)/shard_map/transpose | solution.py:97
  104.9 6.8 %all-to-all-start.2 = ((f32[8,2,24,1152]{3,2,1,0:T(8,128)}), f32[8,2,24,1152]{3,2,1,0:T(8,128)}, u32[]{:S(2)}, u32[]{:S(2)}) async-start(f32[8,2,24,1152]{3,2,1,0:T(8,128)} %copy.45), calls=%async_computation.2 | async-start | bytes 3538944 | tf_op jit(solution)/shard_map/all_to_all | solution.py:81
  111.9 3.1 %fusion.27 = f32[96,12,96]{0,2,1:T(8,128)} fusion(f32[96]{0:T(128)S(1)} %get-tuple-element.43, f32[96,12]{0,1:T(8,128)S(1)} %broadcast_add_fusion), kind=kLoop, calls=%fused_computation.31 | loop fusion | flops 995328 | bytes 447360 | tf_op jit(solution)/shard_map/mul | solution.py:75
  114.9 21.9 %all-to-all-done.2 = f32[8,2,24,1152]{3,2,1,0:T(8,128)} async-done(((f32[8,2,24,1152]{3,2,1,0:T(8,128)}), f32[8,2,24,1152]{3,2,1,0:T(8,128)}, u32[]{:S(2)}, u32[]{:S(2)}) %all-to-all-start.2) | async-done | bytes 1769504 | tf_op jit(solution)/shard_map/all_to_all | solution.py:81
  136.8 4.0 %reshape.204 = f32[8,2,2,12,12,96]{5,4,3,2,1,0:T(8,128)} reshape(f32[8,2,24,1152]{3,2,1,0:T(8,128)} %all-to-all-done.2) | data formatting | bytes 3538944 | tf_op jit(solution)/shard_map/reshape | solution.py:99
  140.9 3.8 %copy.46 = f32[2,2,8,12,12,96]{5,1,4,3,2,0:T(2,128)S(1)} copy(f32[2,2,8,12,12,96]{5,4,3,1,0,2:T(8,128)} %bitcast.149) | data formatting | bytes 3538944 | tf_op jit(solution)/shard_map/transpose | solution.py:99
  144.7 4.0 %fusion.8 = f32[2,12,96,2,96,1]{4,2,5,3,1,0:T(8,128)S(1)} fusion(f32[2,2,96,12,96,1]{4,1,3,2,0,5:T(2,128)S(1)} %bitcast.150, f32[1,96,2,96]{3,1,2,0:T(8,128)S(1)} %copy-done.12, f32[1,96,2,96]{3,1,2,0:T(8,128)S(1)} %copy-done.14), kind=kOutput, calls=%fused_computation.10 | convolution fusion | flops 1019252736 | bytes 3686400 | tf_op jit(solution)/shard_map/akbx,pbxyz->pakyz/dot_general | solution.py:52
  148.7 3.5 %fusion.12 = f32[2,2,96,12,96]{2,4,1,3,0:T(8,128)} fusion(f32[2,12,96,2,96,1]{4,2,5,3,1,0:T(8,128)S(1)} %fusion.8, f32[96,12,96]{0,2,1:T(8,128)S(1)} %copy-done.6, f32[1,96,2,96]{3,1,2,0:T(8,128)S(1)} %get-tuple-element.41, f32[1,96,2,96]{3,1,2,0:T(8,128)S(1)} %get-tuple-element.36), kind=kOutput, calls=%fused_computation.14 | convolution fusion | flops 1019695104 | bytes 4128768 | tf_op jit(solution)/shard_map/akbx,pbxyz->pakyz/dot_general | solution.py:52
  152.2 4.7 %copy.48 = f32[2,2,96,12,96]{4,3,1,2,0:T(8,128)} copy(f32[2,2,96,12,96]{2,4,1,3,0:T(8,128)} %fusion.12) | data formatting | bytes 3538944 | tf_op jit(solution)/shard_map/akbx,pbxyz->pakyz/transpose | solution.py:52
  156.9 4.6 %reshape.206 = f32[2,2,8,12,1152]{4,1,3,2,0:T(2,128)} reshape(f32[2,2,96,12,96]{4,3,1,2,0:T(8,128)} %copy.48) | data formatting | bytes 3538944 | tf_op jit(solution)/shard_map/reshape | solution.py:103
  161.5 1.8 copy.49
  163.4 1.5 copy.50
  164.9 4.3 %all-to-all-start.3 = ((f32[8,2,24,1152]{3,2,1,0:T(8,128)}), f32[8,2,24,1152]{3,2,1,0:T(8,128)}, u32[]{:S(2)}, u32[]{:S(2)}) async-start(f32[8,2,24,1152]{3,2,1,0:T(8,128)} %copy.50), calls=%async_computation.3 | async-start | bytes 3538944 | tf_op jit(solution)/shard_map/all_to_all | solution.py:81
  169.2 1.1 fusion.57
  170.3 2.0 slice.107
  172.3 2.0 slice.105
  174.4 19.9 %all-to-all-done.3 = f32[8,2,24,1152]{3,2,1,0:T(8,128)} async-done(((f32[8,2,24,1152]{3,2,1,0:T(8,128)}), f32[8,2,24,1152]{3,2,1,0:T(8,128)}, u32[]{:S(2)}, u32[]{:S(2)}) %all-to-all-start.3) | async-done | bytes 1769504 | tf_op jit(solution)/shard_map/all_to_all | solution.py:81
  194.3 3.3 %copy.51 = f32[2,24,8,1152]{3,2,1,0:T(8,128)} copy(f32[2,24,8,1152]{3,1,0,2:T(8,128)} %bitcast.36) | data formatting | bytes 3538944 | tf_op jit(solution)/shard_map/transpose | solution.py:105
  197.6 3.3 %reshape.208 = f32[2,2,12,96,96]{4,3,2,1,0:T(8,128)} reshape(f32[2,24,8,1152]{3,2,1,0:T(8,128)} %copy.51) | data formatting | bytes 3538944 | tf_op jit(solution)/shard_map/reshape | solution.py:105
  200.9 5.8 %fusion.6 = f32[2,12,96,2,96,1]{4,2,5,3,1,0:T(8,128)S(1)} fusion(f32[1,96,2,96]{3,1,2,0:T(8,128)S(1)} %get-tuple-element.41, f32[1,96,2,96]{3,1,2,0:T(8,128)S(1)} %get-tuple-element.36, f32[2,2,12,96,96]{4,3,2,1,0:T(8,128)} %reshape.208), kind=kOutput, calls=%fused_computation.8 | convolution fusion | flops 1019252736 | bytes 3686400 | tf_op jit(solution)/shard_map/akby,pbxyz->paxkz/dot_general | solution.py:52
  206.7 4.0 %fusion.18 = f32[2,2,12,96,96]{4,3,1,2,0:T(8,128)S(1)} fusion(f32[2,12,96,2,96,1]{4,2,5,3,1,0:T(8,128)S(1)} %fusion.6, f32[1,96,2,96]{3,1,2,0:T(8,128)S(1)} %get-tuple-element.41, f32[1,96,2,96]{3,1,2,0:T(8,128)S(1)} %get-tuple-element.36), kind=kOutput, calls=%fused_computation.16 | convolution fusion | flops 1019252736 | bytes 3686400 | tf_op jit(solution)/shard_map/akbz,pbxyz->paxyk/dot_general | solution.py:52
  210.7 1.2 fusion.56
  211.9 1.2 slice.99
  213.1 1.0 slice.106
  214.1 1.2 slice.97
  215.3 1.0 slice.104
  216.3 2.3 slice.103
  218.6 2.2 slice.101
  220.9 3.2 %multiply_add_fusion = (f32[12,9216]{1,0:T(8,128)}, f32[12,9216]{1,0:T(8,128)}, f32[12,9216]{1,0:T(8,128)}, f32[12,9216]{1,0:T(8,128)}, f32[12,9216]{1,0:T(8,128)}, /*index=5*/f32[12,9216]{1,0:T(8,128)}) fusion(f32[12,9216]{1,0:T(8,128)} %slice.103, f32[12,9216]{1,0:T(8,128)} %slice.101, f32[24,9216]{1,0:T(8,128)S(1)} %collective-permute-done, ...), kind=kLoop, calls=%fused_computation.43 | loop fusion | flops 1990656 | bytes 6193152 | tf_op jit(solution)/shard_map/add | solution.py:58
  224.1 1.4 concatenate.32
  225.4 1.2 concatenate.31
  227.0 1.3 copy.54
  228.3 6.5 %all-to-all-start.4 = ((f32[16,24,576]{2,1,0:T(8,128)}), f32[16,24,576]{2,1,0:T(8,128)S(1)}, u32[]{:S(2)}, u32[]{:S(2)}) async-start(f32[16,24,576]{2,1,0:T(8,128)} %copy.54), calls=%async_computation.4 | async-start | bytes 1966080 | tf_op jit(solution)/shard_map/all_to_all | solution.py:78
  234.8 2.1 pad_maximum_fusion.2
  236.9 1.1 collective-permute-start.1
  238.0 20.3 %all-to-all-done.4 = f32[16,24,576]{2,1,0:T(8,128)S(1)} async-done(((f32[16,24,576]{2,1,0:T(8,128)}), f32[16,24,576]{2,1,0:T(8,128)S(1)}, u32[]{:S(2)}, u32[]{:S(2)}) %all-to-all-start.4) | async-done | bytes 884768 | tf_op jit(solution)/shard_map/all_to_all | solution.py:78
  258.4 2.8 %collective-permute-start.2 = (f32[24,288]{1,0:T(8,128)S(1)}, f32[24,288]{1,0:T(8,128)S(1)}, u32[]{:S(2)}, u32[]{:S(2)}) collective-permute-start(f32[24,288]{1,0:T(8,128)S(1)} %constant_dynamic-slice_fusion), channel_id=1, source_target_pairs={{0,8},{8,0},{16,24},{24,16},{32,40},{40,32},{48,56},{56,48},{64,72... | collective-permute-start | bytes 82952 | tf_op jit(solution)/shard_map/ppermute | solution.py:119
  261.2 0.9 copy-done.15
  262.2 1.3 fusion.23
  263.6 1.6 copy.55
  265.3 0.7 copy.56
  (55 shorter events, 2.2 us)
Async XLA Ops:
  0.6 4.9 %copy-start.16 = (s32[32]{0:T(128)S(1)}, s32[32]{0:T(128)}, u32[]{:S(2)}) copy-start(s32[32]{0:T(128)} %param.3) | copy-start | bytes 388
  2.2 5.9 %collective-permute-start = (f32[24,9216]{1,0:T(8,128)S(1)}, f32[24,9216]{1,0:T(8,128)S(1)}, u32[]{:S(2)}, u32[]{:S(2)}) collective-permute-start(f32[24,9216]{1,0:T(8,128)S(1)} %reshape.201), channel_id=1, source_target_pairs={{0,8},{8,0},{16,24},{24,16},{32,40},{40,32},{48,56},{56,48},{64,72... | collective-permute-start | bytes 2654216 | tf_op jit(solution)/shard_map/ppermute | solution.py:84
  11.9 31.6 %all-to-all-start = ((f32[16,24,576]{2,1,0:T(8,128)}), f32[16,24,576]{2,1,0:T(8,128)S(1)}, u32[]{:S(2)}, u32[]{:S(2)}) async-start(f32[16,24,576]{2,1,0:T(8,128)} %bitcast.155), calls=%async_computation | async-start | bytes 1966080 | tf_op jit(solution)/shard_map/all_to_all | solution.py:78
  44.5 29.7 %all-to-all-start.1 = ((f32[16,24,576]{2,1,0:T(8,128)}), f32[16,24,576]{2,1,0:T(8,128)S(1)}, u32[]{:S(2)}, u32[]{:S(2)}) async-start(f32[16,24,576]{2,1,0:T(8,128)} %broadcast_in_dim.10), calls=%async_computation.1 | async-start | bytes 1966080 | tf_op jit(solution)/shard_map/all_to_all | solution.py:78
  75.1 2.2 copy-start
  86.4 3.8 %copy-start.11 = (f32[1,96,2,96]{3,1,2,0:T(8,128)S(1)}, f32[1,96,2,96]{3,1,2,0:T(8,128)}, u32[]{:S(2)}) copy-start(f32[1,96,2,96]{3,1,2,0:T(8,128)} %get-tuple-element.37) | copy-start | bytes 221188
  86.5 3.8 %copy-start.13 = (f32[1,96,2,96]{3,1,2,0:T(8,128)S(1)}, f32[1,96,2,96]{3,1,2,0:T(8,128)}, u32[]{:S(2)}) copy-start(f32[1,96,2,96]{3,1,2,0:T(8,128)} %get-tuple-element.40) | copy-start | bytes 221188
  104.9 31.9 %all-to-all-start.2 = ((f32[8,2,24,1152]{3,2,1,0:T(8,128)}), f32[8,2,24,1152]{3,2,1,0:T(8,128)}, u32[]{:S(2)}, u32[]{:S(2)}) async-start(f32[8,2,24,1152]{3,2,1,0:T(8,128)} %copy.45), calls=%async_computation.2 | async-start | bytes 3538944 | tf_op jit(solution)/shard_map/all_to_all | solution.py:81
  140.9 3.8 %copy-start.12 = (f32[1,96,2,96]{3,1,2,0:T(8,128)S(1)}, f32[1,96,2,96]{3,1,2,0:T(8,128)}, u32[]{:S(2)}) copy-start(f32[1,96,2,96]{3,1,2,0:T(8,128)} %get-tuple-element.37) | copy-start | bytes 221188
  140.9 3.8 %copy-start.14 = (f32[1,96,2,96]{3,1,2,0:T(8,128)S(1)}, f32[1,96,2,96]{3,1,2,0:T(8,128)}, u32[]{:S(2)}) copy-start(f32[1,96,2,96]{3,1,2,0:T(8,128)} %get-tuple-element.40) | copy-start | bytes 221188
  144.6 4.1 %copy-start.6 = (f32[96,12,96]{0,2,1:T(8,128)S(1)}, f32[96,12,96]{0,2,1:T(8,128)}, u32[]{:S(2)}) copy-start(f32[96,12,96]{0,2,1:T(8,128)} %fusion.27) | copy-start | bytes 1327108
  164.9 29.4 %all-to-all-start.3 = ((f32[8,2,24,1152]{3,2,1,0:T(8,128)}), f32[8,2,24,1152]{3,2,1,0:T(8,128)}, u32[]{:S(2)}, u32[]{:S(2)}) async-start(f32[8,2,24,1152]{3,2,1,0:T(8,128)} %copy.50), calls=%async_computation.3 | async-start | bytes 3538944 | tf_op jit(solution)/shard_map/all_to_all | solution.py:81
  214.1 6.7 %copy-start.1 = (f32[12,9216]{1,0:T(8,128)S(1)}, f32[12,9216]{1,0:T(8,128)}, u32[]{:S(2)}) copy-start(f32[12,9216]{1,0:T(8,128)} %slice.99) | copy-start | bytes 1327108
  216.3 4.5 %copy-start.2 = (f32[12,9216]{1,0:T(8,128)S(1)}, f32[12,9216]{1,0:T(8,128)}, u32[]{:S(2)}) copy-start(f32[12,9216]{1,0:T(8,128)} %slice.97) | copy-start | bytes 1327108
  224.0 2.7 copy-start.7
  224.0 2.7 copy-start.8
  224.0 2.7 %copy-start.9 = (f32[12,16,576]{2,1,0:T(8,128)S(1)}, f32[12,16,576]{2,1,0:T(8,128)}, u32[]{:S(2)}) copy-start(f32[12,16,576]{2,1,0:T(8,128)} %slice.106) | copy-start | bytes 1327108
  224.0 2.7 %copy-start.10 = (f32[12,16,576]{2,1,0:T(8,128)S(1)}, f32[12,16,576]{2,1,0:T(8,128)}, u32[]{:S(2)}) copy-start(f32[12,16,576]{2,1,0:T(8,128)} %slice.104) | copy-start | bytes 1327108
  227.0 7.8 %copy-start.5 = (f32[12,9216]{1,0:T(8,128)S(1)}, f32[12,9216]{1,0:T(8,128)}, u32[]{:S(2)}) copy-start(f32[12,9216]{1,0:T(8,128)} %get-tuple-element.24) | copy-start | bytes 1327108
  228.3 33.9 %copy-start.3 = (f32[12,9216]{1,0:T(8,128)S(1)}, f32[12,9216]{1,0:T(8,128)}, u32[]{:S(2)}) copy-start(f32[12,9216]{1,0:T(8,128)} %get-tuple-element.26) | copy-start | bytes 1327108
  228.3 33.9 %copy-start.4 = (f32[12,9216]{1,0:T(8,128)S(1)}, f32[12,9216]{1,0:T(8,128)}, u32[]{:S(2)}) copy-start(f32[12,9216]{1,0:T(8,128)} %get-tuple-element.27) | copy-start | bytes 1327108
  228.3 30.0 %all-to-all-start.4 = ((f32[16,24,576]{2,1,0:T(8,128)}), f32[16,24,576]{2,1,0:T(8,128)S(1)}, u32[]{:S(2)}, u32[]{:S(2)}) async-start(f32[16,24,576]{2,1,0:T(8,128)} %copy.54), calls=%async_computation.4 | async-start | bytes 1966080 | tf_op jit(solution)/shard_map/all_to_all | solution.py:78
  236.9 24.4 %collective-permute-start.1 = (f32[24,9216]{1,0:T(8,128)}, f32[24,9216]{1,0:T(8,128)S(1)}, u32[]{:S(2)}, u32[]{:S(2)}) collective-permute-start(f32[24,9216]{1,0:T(8,128)} %pad_maximum_fusion.2), channel_id=1, source_target_pairs={{0,8},{8,0},{16,24},{24,16},{32,40},{40,32},{48,56},{56,48},{64,72... | collective-permute-start | bytes 2654216 | tf_op jit(solution)/shard_map/ppermute | solution.py:110
  258.4 6.7 %collective-permute-start.2 = (f32[24,288]{1,0:T(8,128)S(1)}, f32[24,288]{1,0:T(8,128)S(1)}, u32[]{:S(2)}, u32[]{:S(2)}) collective-permute-start(f32[24,288]{1,0:T(8,128)S(1)} %constant_dynamic-slice_fusion), channel_id=1, source_target_pairs={{0,8},{8,0},{16,24},{24,16},{32,40},{40,32},{48,56},{56,48},{64,72... | collective-permute-start | bytes 82952 | tf_op jit(solution)/shard_map/ppermute | solution.py:119
  261.2 0.9 copy-start.15

commit v2 on v1

v2 whole, which is shorter than its diff:
```python
import functools
import math

import jax
import jax.numpy as jnp
import ml_dtypes
import numpy as np
from jax import lax
from jax.experimental import pallas as pl
from jax.experimental.pallas import tpu as pltpu
from jax.sharding import PartitionSpec as P

NX = 96
NY = 96
NZ = 96
SERVE = 2
CHIPS = 16
PARTS = 8
ROWS = 24
PLANE = NY * NZ
BLOCK = PLANE // PARTS
CHUNK = 112
HALF = PLANE // CHIPS // 2
VMEM = 48 * 1024 * 1024

cell_side = 41.04
mixing = 0.25


def frequencies(count):
    signed = (jnp.arange(count, dtype=jnp.int32) + count // 2) % count - count // 2
    return signed.astype(jnp.float32) * (2.0 * math.pi / cell_side)


def kernel_columns(start, width):
    freq_x = frequencies(NX)
    freq_y = lax.dynamic_slice_in_dim(frequencies(NY), start, width)
    freq_z = frequencies(NZ)
    freq_y = jnp.broadcast_to(freq_y[:, None], (width, NZ)).reshape(-1)
    freq_z = jnp.broadcast_to(freq_z[None], (width, NZ)).reshape(-1)
    squared = freq_x[:, None] ** 2 + freq_y[None] ** 2 + freq_z[None] ** 2
    radius = cell_side * (3.0 / (4.0 * math.pi)) ** (1.0 / 3.0)
    safe_square = jnp.where(squared > 0, squared, 1.0)
    general = 4.0 * math.pi * (1.0 - jnp.cos(jnp.sqrt(safe_square) * radius)) / safe_square
    return jnp.where(squared > 0, general, 2.0 * math.pi * radius * radius)


def split_table(table):
    high = table.astype(ml_dtypes.bfloat16)
    low = (table - high.astype(np.float64)).astype(ml_dtypes.bfloat16)
    return high, low


def angle_tables(sign):
    index = np.arange(96)
    angles = 2.0 * np.pi * (np.outer(index, index) % 96) / 96
    return np.cos(angles), sign * np.sin(angles)


def lane_table(sign):
    cosine, sine = angle_tables(sign)
    table = np.zeros((256, 256))
    table[:96, :96] = cosine
    table[128:224, 128:224] = cosine
    table[:96, 128:224] = sine
    table[128:224, :96] = -sine
    return split_table(table)


def slab_order():
    part = np.array([0] * 8 + [1] * 8 + [0] * 4 + [1] * 4)
    plane = np.array(list(range(8)) * 2 + list(range(8, 12)) * 2)
    part = np.tile(part, PARTS)
    plane = np.concatenate([plane + 12 * f for f in range(PARTS)])
    return part * 96 + plane


def row_tables():
    order = slab_order()
    cosine, sine = angle_tables(-1.0)
    forward = np.block([[cosine, -sine], [sine, cosine]])[:, order]
    cosine, sine = angle_tables(1.0)
    inverse = np.block([[cosine, -sine], [sine, cosine]])[order]
    return split_table(forward) + split_table(inverse)


def const_times(value, angle, count):
    re, im = value
    angle %= count
    if angle == 0:
        return value
    if 2 * angle == count:
        return (-re, -im)
    if 4 * angle == count:
        return (-im, re)
    if 4 * angle == 3 * count:
        return (im, -re)
    c = math.cos(2 * math.pi * angle / count)
    s = math.sin(2 * math.pi * angle / count)
    if (8 * angle) % count == 0:
        r = math.sqrt(0.5)
        c = math.copysign(1.0, c)
        s = math.copysign(1.0, s)
        a = re * (c * r)
        b = im * (c * r)
        return (a - b, a + b) if c == s else (a + b, b - a)
    return (re * c - im * s, re * s + im * c)


def add(a, b):
    return (a[0] + b[0], a[1] + b[1])


def sub(a, b):
    return (a[0] - b[0], a[1] - b[1])


def small_dft(x, sign):
    n = len(x)
    if n == 2:
        return [add(x[0], x[1]), sub(x[0], x[1])]
    if n == 3:
        total = add(x[1], x[2])
        diff = sub(x[1], x[2])
        r = sign * math.sqrt(0.75)
        mid = (x[0][0] - 0.5 * total[0], x[0][1] - 0.5 * total[1])
        turn = (-r * diff[1], r * diff[0])
        return [add(x[0], total), add(mid, turn), sub(mid, turn)]
    if n == 4:
        a, b = add(x[0], x[2]), sub(x[0], x[2])
        c, d = add(x[1], x[3]), sub(x[1], x[3])
        d = const_times(d, sign, 4)
        return [add(a, c), add(b, d), sub(a, c), sub(b, d)]
    inner = 4
    outer = n // inner
    out = [None] * n
    columns = []
    for low in range(outer):
        column = small_dft([x[outer * i + low] for i in range(inner)], sign)
        columns.append([const_times(v, sign * low * k, n) for k, v in enumerate(column)])
    for k in range(inner):
        row = small_dft([columns[low][k] for low in range(outer)], sign)
        for j in range(outer):
            out[k + inner * j] = row[j]
    return out


def leading_dft(field, sign):
    def tile(t, carry):
        rows = pl.ds(pl.multiple_of(t * 8, 8), 8)

        def load(y):
            return (field[y, rows, 0:128], field[y, rows, 128:256])

        def save(y, v):
            field[y, rows, 0:128] = v[0]
            field[y, rows, 128:256] = v[1]

        for low in range(8):
            column = small_dft([load(8 * i + low) for i in range(12)], sign)
            for k, v in enumerate(column):
                save(8 * k + low, const_times(v, sign * low * k, 96))
        return carry

    lax.fori_loop(0, 3, tile, 0)


def second_pass(field, k, rows, sign):
    values = [
        (field[8 * k + low, rows, 0:128], field[8 * k + low, rows, 128:256]) for low in range(8)
    ]
    return small_dft(values, sign)


def whole_dft(source, target, sign):
    leading_dft(source, sign)

    def tile(t, carry):
        rows = pl.ds(pl.multiple_of(t * 8, 8), 8)
        for k in range(12):
            for j, v in enumerate(second_pass(source, k, rows, sign)):
                target[k + 12 * j, rows, 0:128] = v[0]
                target[k + 12 * j, rows, 128:256] = v[1]
        return carry

    lax.fori_loop(0, 3, tile, 0)


def lanes():
    return lax.broadcasted_iota(jnp.int32, (8, 128), 1)


def unpack(wide):
    lane = lanes()
    out = []
    for q in range(3):
        a, b, c = (wide[:, 128 * (3 * q + i) : 128 * (3 * q + i + 1)] for i in range(3))
        out.append(a)
        out.append(jnp.where(lane < 32, pltpu.roll(a, 32, 1), pltpu.roll(b, 32, 1)))
        out.append(jnp.where(lane < 64, pltpu.roll(b, 64, 1), pltpu.roll(c, 64, 1)))
        out.append(pltpu.roll(c, 96, 1))
    return out


def pack(tiles):
    lane = lanes()
    out = []
    for q in range(3):
        a, b, c, d = tiles[4 * q : 4 * q + 4]
        b = pltpu.roll(b, 96, 1)
        c = pltpu.roll(c, 64, 1)
        d = pltpu.roll(d, 32, 1)
        out.append(jnp.where(lane < 96, a, b))
        out.append(jnp.where(lane < 64, b, c))
        out.append(jnp.where(lane < 32, c, d))
    return jnp.concatenate(out, axis=1)


def flip(x):
    return pltpu.roll(x, 4, 0)


def top(x):
    return lax.broadcasted_iota(jnp.int32, x.shape, 0) < 4


def split_dot(x, high, low):
    x_high = x.astype(jnp.bfloat16)
    x_low = (x - x_high.astype(jnp.float32)).astype(jnp.bfloat16)
    dot = functools.partial(jnp.dot, preferred_element_type=jnp.float32)
    return dot(x_high, high) + (dot(x_high, low) + dot(x_low, high))


def dot_split(high, low, x):
    x_high = x.astype(jnp.bfloat16)
    x_low = (x - x_high.astype(jnp.float32)).astype(jnp.bfloat16)
    dot = functools.partial(jnp.dot, preferred_element_type=jnp.float32)
    return dot(high, x_high) + (dot(low, x_high) + dot(high, x_low))


def tile_rows(ref, r, g):
    start = pl.multiple_of(8 * (72 * r + 9 * g), 8)
    x = ref[pl.ds(start, 72), :]
    return jnp.concatenate([x[8 * i : 8 * i + 8] for i in range(9)], axis=1)


def orbital_rows(ref, g):
    cols = pl.ds(pl.multiple_of(g * BLOCK, 128), BLOCK)
    rest = jnp.concatenate([ref[0, 8:12, cols], ref[1, 8:12, cols]], axis=0)
    return ref[0, 0:8, cols], ref[1, 0:8, cols], rest


def candidate_kernel(own_ref, mine, other, out):
    def copy(ref):
        for l in range(72):
            cols = slice(128 * l, 128 * l + 128)
            out[8 * l : 8 * l + 8, :] = ref[0, 0:8, cols]
            out[8 * (72 + l) : 8 * (72 + l) + 8, :] = ref[1, 0:8, cols]
            out[8 * (144 + l) : 8 * (144 + l) + 8, :] = jnp.concatenate(
                [ref[0, 8:12, cols], ref[1, 8:12, cols]], axis=0
            )

    out[1728:1792, :] = jnp.zeros((64, 128), jnp.float32)

    @pl.when(own_ref[0] == 1)
    def _():
        copy(mine)

    @pl.when(own_ref[0] == 0)
    def _():
        copy(other)


def forward_kernel(served, mine, other, high, low, out, line, field, spectrum):
    def block(g, carry):
        s0, s1, s2 = (tile_rows(served, r, g) for r in range(3))
        parts = []
        rests = []
        for ref in (mine, other):
            re, im, rest = orbital_rows(ref, g)
            parts.append((s0 * re + s1 * im, s0 * im - s1 * re))
            same = s2 * rest
            cross = s2 * flip(rest)
            rests.append((same + flip(same), cross - flip(cross)))
        upper = top(s2)
        parts.append(
            (jnp.where(upper, rests[0][0], rests[1][0]), jnp.where(upper, rests[0][1], -rests[1][1]))
        )
        for t, (re, im) in enumerate(parts):
            for y, (a, b) in enumerate(zip(unpack(re), unpack(im))):
                line[24 * y + 8 * t : 24 * y + 8 * t + 8, 0:128] = a
                line[24 * y + 8 * t : 24 * y + 8 * t + 8, 128:256] = b
        result = split_dot(line[...], high[...], low[...])
        field[pl.ds(g * 12, 12)] = result.reshape(12, 24, 256)
        return carry

    lax.fori_loop(0, PARTS, block, 0)
    whole_dft(field, spectrum, -1)

    def send(g, carry):
        packed = []
        for t in range(3):
            rows = slice(8 * t, 8 * t + 8)
            packed.append(
                tuple(
                    pack([spectrum[g * 12 + y, rows, c : c + 128] for y in range(12)])
                    for c in (0, 128)
                )
            )
        re, im = packed[2]
        upper = top(re)
        for p, rest in enumerate(
            (jnp.where(upper, re, flip(im)), jnp.where(upper, flip(re), im))
        ):
            out[g, p, 0:8, :] = packed[p][0]
            out[g, p, 8:16, :] = packed[p][1]
            out[g, p, 16:24, :] = rest
        return carry

    lax.fori_loop(0, PARTS, send, 0)


def column_kernel(blocks, coulomb, fh, fl, ih, il, out):
    x = blocks[:, 0].reshape(8 * ROWS, BLOCK)
    x = dot_split(fh[...], fl[...], x)
    k = coulomb[...]
    x = jnp.concatenate([x[:96] * k, x[96:] * k], axis=0)
    x = dot_split(ih[...], il[...], x)
    out[:, 0] = x.reshape(8, ROWS, BLOCK)


def backward_kernel(blocks, served, mine, other, high, low, own, away, terms, line, field, spectrum):
    def receive(g, carry):
        rests = [blocks[g, p, 16:24, :] for p in range(2)]
        upper = top(rests[0])
        parts = [(blocks[g, p, 0:8, :], blocks[g, p, 8:16, :]) for p in range(2)]
        parts.append(
            (
                jnp.where(upper, rests[0], flip(rests[1])),
                jnp.where(upper, flip(rests[0]), rests[1]),
            )
        )
        for t, (re, im) in enumerate(parts):
            rows = slice(8 * t, 8 * t + 8)
            for y, (a, b) in enumerate(zip(unpack(re), unpack(im))):
                spectrum[g * 12 + y, rows, 0:128] = a
                spectrum[g * 12 + y, rows, 128:256] = b
        return carry

    lax.fori_loop(0, PARTS, receive, 0)
    whole_dft(spectrum, field, 1)

    def block(g, carry):
        x = field[pl.ds(g * 12, 12)].reshape(288, 256)
        line[...] = split_dot(x, high[...], low[...])
        packed = []
        for t in range(3):
            packed.append(
                tuple(
                    pack([line[24 * y + 8 * t : 24 * y + 8 * t + 8, c : c + 128] for y in range(12)])
                    for c in (0, 128)
                )
            )
        re, im = packed[2]
        upper = top(re)
        rests = (jnp.where(upper, re, flip(im)), jnp.where(upper, flip(re), im))
        s0, s1, s2 = (tile_rows(served, r, g) for r in range(3))
        cols = pl.ds(pl.multiple_of(g * BLOCK, 128), BLOCK)
        sums = None
        for p, (ref, result) in enumerate(((mine, own), (other, away))):
            vr, vi = packed[p]
            v2 = rests[p]
            result[0, 0:8, cols] = s0 * vr - s1 * vi
            result[1, 0:8, cols] = s0 * vi + s1 * vr
            same = s2 * v2
            cross = s2 * flip(v2)
            result[0, 8:12, cols] = (same - flip(same))[0:4]
            result[1, 8:12, cols] = (cross + flip(cross))[0:4]
            ore, oim, rest = orbital_rows(ref, g)
            same = v2 * rest
            cross = v2 * flip(rest)
            turned = flip(cross)
            both = (
                vr * ore + vi * oim,
                vr * oim - vi * ore,
                jnp.where(upper, same + flip(same), turned - cross),
            )
            sums = both if sums is None else tuple(a + b for a, b in zip(sums, both))
        lane = lanes()
        for odd in range(2):
            start = pl.multiple_of((2 * g + odd) * CHUNK, 8)
            for r in range(3):
                for l in range(4):
                    c = 128 * (l + 5 * odd)
                    terms[pl.ds(start + 8 * (4 * r + l), 8), :] = sums[r][:, c : c + 128]
            h0, h1, h2 = (x[:, 512:640] for x in sums)
            if odd:
                h0, h2 = pltpu.roll(h0, 64, 1), pltpu.roll(h2, 64, 1)
            else:
                h1 = pltpu.roll(h1, 64, 1)
            terms[pl.ds(start + 96, 8), :] = jnp.where(lane < 64, h0, h1)
            terms[pl.ds(start + 104, 8), :] = h2
        return carry

    lax.fori_loop(0, PARTS, block, 0)


def finish_kernel(place, blocks, keep, give):
    lane = lanes()
    odd = place[1] == 1
    first_core = place[0] == 0
    tiles = []
    for i in range(14):
        x = [blocks[CHUNK * q + 8 * i : CHUNK * q + 8 * i + 8, :] for q in range(CHIPS)]
        while len(x) > 1:
            x = [x[2 * j] + x[2 * j + 1] for j in range(len(x) // 2)]
        tiles.append(x[0])
    halves = (tiles[12], pltpu.roll(tiles[12], 64, 1), tiles[13])
    for r in range(3):
        f = tiles[4 * r : 4 * r + 4]
        h = halves[r]
        s = [pltpu.roll(x, 64, 1) for x in f]
        wide = [
            jnp.where(odd, jnp.where(lane < 64, a, b), c)
            for a, b, c in zip([h] + s, s + [s[3]], f + [h])
        ]
        s = [pltpu.roll(x, 96, 1) for x in wide[2:]]
        second = [jnp.where(lane < 96, s[0], s[1]), jnp.where(lane < 96, s[1], s[2]), s[2]]
        first = wide[:3]
        for ref, cond in ((keep, first_core), (give, jnp.logical_not(first_core))):
            for i in range(3):
                x = jnp.where(cond, first[i], second[i])
                if i == 2:
                    x = x[:, :32]
                cols = slice(128 * i, 128 * i + x.shape[1])
                if r < 2:
                    ref[r, 0:8, cols] = x
                else:
                    ref[0, 8:12, cols] = x[0:4]
                    ref[1, 8:12, cols] = x[4:8]


def f32(*shape):
    return jax.ShapeDtypeStruct(shape, jnp.float32)


def shards(orbitals, serve_order):
    rank_fft = lax.axis_index("fft")
    rank_band = lax.axis_index("band")
    core = rank_band % 2
    chip = rank_band // 2
    swap = [(i, i ^ 1) for i in range(32)]
    same_core = [[2 * i + c for i in range(CHIPS)] for c in range(2)]
    scale = -mixing / (NX * NY * NZ)
    coulomb = kernel_columns(rank_fft * 12, 12) * scale
    params = pltpu.CompilerParams(vmem_limit_bytes=VMEM)
    scalars = pl.BlockSpec(memory_space=pltpu.SMEM)
    whole = pl.BlockSpec(memory_space=pltpu.VMEM)

    def chips_exchange(blocks):
        return lax.all_to_all(blocks, "band", 0, 0, axis_index_groups=same_core, tiled=True)

    def fft_exchange(blocks):
        return lax.all_to_all(blocks, "fft", 0, 0, tiled=True)

    mine = orbitals.reshape(2, 12, PLANE)
    other = lax.ppermute(mine, "band", swap)
    serving = serve_order[core]
    own = (serving % 2 == core).astype(jnp.int32).reshape(1)
    blocks = pl.pallas_call(
        candidate_kernel,
        out_shape=f32(CHIPS * CHUNK, 128),
        in_specs=[scalars, whole, whole],
        out_specs=whole,
        compiler_params=params,
        name="candidate",
    )(own, mine, other)
    blocks = chips_exchange(blocks.reshape(CHIPS, CHUNK, 128))
    block = lax.dynamic_index_in_dim(blocks, serving // 2, 0, keepdims=True)
    served = chips_exchange(jnp.broadcast_to(block, blocks.shape)).reshape(CHIPS * CHUNK, 128)

    scratch = [
        pltpu.VMEM((288, 256), jnp.float32),
        pltpu.VMEM((NY, ROWS, 256), jnp.float32),
        pltpu.VMEM((NY, ROWS, 256), jnp.float32),
    ]
    high, low = lane_table(-1.0)
    blocks = pl.pallas_call(
        forward_kernel,
        out_shape=f32(PARTS, 2, ROWS, BLOCK),
        in_specs=[whole] * 5,
        out_specs=whole,
        scratch_shapes=scratch,
        compiler_params=params,
        name="forward",
    )(served, mine, other, jnp.asarray(high), jnp.asarray(low))
    blocks = fft_exchange(blocks)
    tables = [jnp.asarray(t) for t in row_tables()]
    fixed = pl.BlockSpec((192, 192), lambda p: (0, 0))
    pair = pl.BlockSpec((PARTS, 1, ROWS, BLOCK), lambda p: (0, p, 0, 0))
    blocks = pl.pallas_call(
        column_kernel,
        out_shape=f32(PARTS, 2, ROWS, BLOCK),
        grid=(2,),
        in_specs=[pair, pl.BlockSpec((NX, BLOCK), lambda p: (0, 0))] + [fixed] * 4,
        out_specs=pair,
        compiler_params=params,
        name="columns",
    )(blocks, coulomb, *tables)
    blocks = fft_exchange(blocks)
    high, low = lane_table(1.0)
    own, away, terms = pl.pallas_call(
        backward_kernel,
        out_shape=(f32(2, 12, PLANE), f32(2, 12, PLANE), f32(CHIPS * CHUNK, 128)),
        in_specs=[whole] * 6,
        out_specs=(whole,) * 3,
        scratch_shapes=scratch,
        compiler_params=params,
        name="backward",
    )(blocks, served, mine, other, jnp.asarray(high), jnp.asarray(low))
    applied = own + lax.ppermute(away, "band", swap)
    blocks = chips_exchange(terms.reshape(CHIPS, CHUNK, 128)).reshape(CHIPS * CHUNK, 128)
    place = jnp.stack([core, chip % 2]).astype(jnp.int32)
    keep, give = pl.pallas_call(
        finish_kernel,
        out_shape=(f32(2, 12, HALF), f32(2, 12, HALF)),
        in_specs=[scalars, whole],
        out_specs=(whole, whole),
        compiler_params=params,
        name="finish",
    )(place, blocks)
    got = lax.ppermute(give, "band", swap)
    first = jnp.where(core == 0, keep, got)
    second = jnp.where(core == 0, got, keep)
    serving_exchange = jnp.stack([first, second])
    return (applied.reshape(1, 2, 12, PLANE), serving_exchange)


def solution(mesh):
    return jax.shard_map(
        shards,
        mesh=mesh,
        in_specs=(P("band", None, "fft", None), P()),
        out_specs=(P("band", None, "fft", None), P(None, None, "fft", "band")),
        check_vma=False,
    )
```

time: 270 us -> 183 us (0.68); the launches traced: 266 us -> 182 us
  local copies, waits for them, and re-layouts: 75.3 us -> 11.4 us
  blocking collectives: 0 us -> 56.2 us
  waiting for transfers between devices: 108 us -> 62.9 us
  matrix products: 26.6 us -> 0 us
  Pallas kernels: 0 us -> 18 us
  other arithmetic: 14 us -> 2.33 us
  starting transfers between devices: 38.9 us -> 28.1 us
    all_to_all x0 -> x2, blocking collectives: none -> 56.2 us  [the longest x1 28.6 us: chips_exchange(): lax.all_to_all(blocks, 'band', 0, 0, axis_index_groups=same_core, tiled=T...]
    dot_general x6 -> x0, matrix products: 26.6 us -> none  [transform(): jnp.einsum(einsum_form, table, field, precision=lax.Precision.HIGHEST)]
    all_to_all x3 -> x2, waiting for transfers between devices: 65.8 us -> 39.8 us  [chips_exchange(): lax.all_to_all(blocks, 'band', 0, 0, axis_index_groups=same_core, tiled=T...]
    transpose x7 -> x0, local copies, waits for them, and re-layouts: 21 us -> none  [the longest x2 7.78 us: transform(): jnp.einsum(einsum_form, table, field, precision=lax.Precision.HIGHEST)]
    slice x15 -> x0, local copies, waits for them, and re-layouts: 20.5 us -> none  [the longest x7 10.1 us: times(): rr, ri = (right[:12], right[12:])]
    reshape x9 -> x1, local copies, waits for them, and re-layouts: 19.5 us -> 0.68 us  [shards(): mine = orbitals.reshape(2, 12, PLANE)]
    all_to_all x2 -> x1, waiting for transfers between devices: 41.8 us -> 23.1 us  [fft_exchange(): return lax.all_to_all(blocks, 'fft', 0, 0, tiled=True)]
    pallas_call x0 -> x5, Pallas kernels: none -> 18 us  [the longest x1 7.42 us: shards(): pl.pallas_call(backward_kernel, out_shape=(f32(2, 12, PLANE), f32(2, 12,...]
  transfers between devices with their start and end apart: 8 -> 6, of which waited for: 5 -> 3; matrix products, arithmetic and copies ran while one was open for 6% -> 3% of each run, Pallas kernels for 0% -> 0%
where the time goes in v2:
time: 183 us; the launch traced here: 182 us
  waiting for transfers between devices  62.9 us (34%)
  blocking collectives  56.2 us (31%)
  starting transfers between devices  28.1 us (15%)
  Pallas kernels  18 us (10%)
  local copies, waits for them, and re-layouts  11.4 us (6%)
  between operations  3.46 us (2%)
  other arithmetic  2.33 us (1%)
    all_to_all x2, waiting for transfers between devices, chips_exchange(): lax.all_to_all(blocks, 'band', 0, 0, axis_index_groups=same_core, tiled=T...  39.8 us
    all_to_all x1, blocking collectives, chips_exchange(): lax.all_to_all(blocks, 'band', 0, 0, axis_index_groups=same_core, tiled=T...  28.6 us
    all_to_all x1, blocking collectives, fft_exchange(): return lax.all_to_all(blocks, 'fft', 0, 0, tiled=True)  27.6 us
    all_to_all x1, waiting for transfers between devices, fft_exchange(): return lax.all_to_all(blocks, 'fft', 0, 0, tiled=True)  23.1 us
    all_to_all x2, starting transfers between devices, chips_exchange(): lax.all_to_all(blocks, 'band', 0, 0, axis_index_groups=same_core, tiled=T...  12.9 us
    unnamed x35, local copies, waits for them, and re-layouts  7.97 us
    pallas_call x1, Pallas kernels, shards(): pl.pallas_call(backward_kernel, out_shape=(f32(2, 12, PLANE), f32(2, 12,...  7.42 us
    all_to_all x1, starting transfers between devices, fft_exchange(): return lax.all_to_all(blocks, 'fft', 0, 0, tiled=True)  6.5 us
  transfers between devices with their start and end apart: 6, of which 3 were waited for; matrix products, arithmetic and copies ran while one was open for 3% of the time, Pallas kernels for 0%

profile of v2, /device:TPU:1, one launch (start us, length us, event | category | flops | bytes accessed | tf_op | source)
XLA Modules:
  0.0 182.3 jit_solution(12493135128728885665)
XLA Ops:
  0.6 1.4 copy.28
  2.1 0.0 copy-start.15
  2.1 0.7 copy.16
  2.8 3.3 %collective-permute-start = (f32[2,12,9216]{2,0,1:T(2,128)S(1)}, f32[2,12,9216]{2,0,1:T(2,128)S(1)}, u32[]{:S(2)}, u32[]{:S(2)}) collective-permute-start(f32[2,12,9216]{2,0,1:T(2,128)S(1)} %copy.16), channel_id=1, source_target_pairs={{0,8},{8,0},{16,24},{24,16},{32,40},{40,32},{48,56},{56,48},{64,72... | collective-permute-start | bytes 2654216 | tf_op jit(solution)/shard_map/ppermute | solution.py:467
  6.1 0.0 copy-done.15
  6.1 0.6 dynamic_slice.10
  8.6 0.0 collective-permute-done
  8.7 0.3 copy.17.other
  8.9 0.0 copy-start
  8.9 1.1 candidate.1
  10.1 7.6 %all-to-all-start = ((f32[16,112,128]{2,1,0:T(8,128)}), f32[16,112,128]{2,1,0:T(8,128)S(1)}, u32[]{:S(2)}, u32[]{:S(2)}) async-start(f32[16,112,128]{2,1,0:T(8,128)} %bitcast.3), calls=%async_computation | async-start | bytes 1835008 | tf_op jit(solution)/shard_map/all_to_all | solution.py:461
  18.3 22.1 %all-to-all-done = f32[16,112,128]{2,1,0:T(8,128)S(1)} async-done(((f32[16,112,128]{2,1,0:T(8,128)}), f32[16,112,128]{2,1,0:T(8,128)S(1)}, u32[]{:S(2)}, u32[]{:S(2)}) %all-to-all-start) | async-done | bytes 917536 | tf_op jit(solution)/shard_map/all_to_all | solution.py:461
  40.4 0.0 copy-start.9
  40.4 0.1 broadcast_in_dim.26
  40.5 28.6 %all_to_all.25 = f32[16,112,128]{2,1,0:T(8,128)S(1)} all-to-all(f32[16,112,128]{2,1,0:T(8,128)S(1)} %broadcast_in_dim.26), channel_id=1, replica_groups={{0,16,32,48,64,80,96,112,128,144,160,176,192,208,224,240},{8,24,40,56,7..., dimensions={0} | all-to-all | bytes 1835008 | tf_op jit(solution)/shard_map/all_to_all | solution.py:461
  69.1 0.0 copy-done
  69.1 0.0 copy-done.9
  69.1 0.0 copy-done.10
  69.1 4.7 %forward.1 = f32[8,2,24,1152]{3,2,1,0:T(8,128)S(1)} custom-call(f32[1792,128]{1,0:T(8,128)S(1)} %bitcast.23, f32[2,12,9216]{2,1,0:T(8,128)S(1)} %bitcast.21, f32[2,12,9216]{2,1,0:T(8,128)S(1)} %copy.17.other, bf16[256,256]{1,0:T(8,128)(2,1)S(1)} %copy-done.10, bf16[256,256]{1,0:T(8,128)(2,1)S(1)} %copy-done.9), custom_call_target="tpu_custom_call" | custom-call | tf_op jit(solution)/shard_map/forward/pallas_call | solution.py:488
  73.8 0.0 copy-start.1
  73.8 1.2 copy-done.1
  75.0 0.0 copy-start.11
  75.0 0.0 copy-start.12
  75.0 0.0 copy-start.13
  75.0 0.0 copy-start.14
  75.0 6.5 %all-to-all-start.2 = ((f32[8,2,24,1152]{3,2,1,0:T(8,128)}), f32[8,2,24,1152]{3,2,1,0:T(8,128)}, u32[]{:S(2)}, u32[]{:S(2)}) async-start(f32[8,2,24,1152]{3,2,1,0:T(8,128)} %copy-done.1), calls=%async_computation.2 | async-start | bytes 3538944 | tf_op jit(solution)/shard_map/all_to_all | solution.py:464
  81.5 0.1 dynamic-slice_multiply_fusion
  81.6 0.1 broadcast_in_dim.27
  81.7 0.1 integer_pow.34
  81.8 0.1 integer_pow.35
  81.9 1.7 fusion.1.coulomb
  83.6 23.1 %all-to-all-done.2.blocks = f32[8,2,24,1152]{3,2,1,0:T(8,128)} async-done(((f32[8,2,24,1152]{3,2,1,0:T(8,128)}), f32[8,2,24,1152]{3,2,1,0:T(8,128)}, u32[]{:S(2)}, u32[]{:S(2)}) %all-to-all-start.2) | async-done | bytes 1769504 | tf_op jit(solution)/shard_map/all_to_all | solution.py:464
  106.7 0.0 copy-done.11
  106.7 0.0 copy-done.12
  106.7 0.0 copy-done.13
  106.7 0.0 copy-done.14
  106.7 4.0 %columns.1 = f32[8,2,24,1152]{3,2,1,0:T(8,128)S(1)} custom-call(f32[8,2,24,1152]{3,2,1,0:T(8,128)} %all-to-all-done.2.blocks, f32[96,1152]{1,0:T(8,128)S(1)} %fusion.1.coulomb, bf16[192,192]{1,0:T(8,128)(2,1)S(1)} %copy-done.14, bf16[192,192]{1,0:T(8,128)(2,1)S(1)} %copy-done.13, bf16[192,192]{1,0:T(8,128)(2,1)S(1)} %copy-done.12, ...), custom_call_target="tpu_custom_call" | custom-call | tf_op jit(solution)/shard_map/columns/pallas_call | solution.py:501
  110.7 0.0 copy-start.7
  110.7 0.0 copy-start.8
  110.7 27.6 %all_to_all.26.blocks = f32[8,2,24,1152]{3,2,1,0:T(8,128)} all-to-all(f32[8,2,24,1152]{3,2,1,0:T(8,128)S(1)} %columns.1), channel_id=1, replica_groups=mesh['band'=32,'fft'=8] {'fft'}, dimensions={0} | all-to-all | bytes 3538944 | tf_op jit(solution)/shard_map/all_to_all | solution.py:464
  138.3 0.0 copy-done.7
  138.3 0.0 copy-done.8
  138.3 7.4 %backward.1 = (f32[2,12,9216]{2,1,0:T(8,128)S(1)}, f32[2,12,9216]{2,1,0:T(8,128)S(1)}, f32[1792,128]{1,0:T(8,128)S(1)}) custom-call(f32[8,2,24,1152]{3,2,1,0:T(8,128)} %all_to_all.26.blocks, f32[1792,128]{1,0:T(8,128)S(1)} %bitcast.24, f32[2,12,9216]{2,1,0:T(8,128)S(1)} %bitcast.22, f32[2,12,9216]{2,1,0:T(8,128)} %copy-done, bf16[256,256]{1,0:T(8,128)(2,1)S(1)} %copy-done.8, ...), custom_call_target="tpu_custom_call" | custom-call | tf_op jit(solution)/shard_map/backward/pallas_call | solution.py:512
  145.8 0.0 copy-start.2
  145.8 1.1 copy-done.2
  146.8 0.0 copy-start.4
  146.8 1.0 copy-done.4
  147.8 0.0 copy-start.6
  147.8 0.9 copy-done.6
  148.8 5.3 %all-to-all-start.4 = ((f32[16,112,128]{2,1,0:T(8,128)}), f32[16,112,128]{2,1,0:T(8,128)S(1)}, u32[]{:S(2)}, u32[]{:S(2)}) async-start(f32[16,112,128]{2,1,0:T(8,128)} %bitcast.26), calls=%async_computation.4 | async-start | bytes 1835008 | tf_op jit(solution)/shard_map/all_to_all | solution.py:461
  154.1 0.0 copy-done.5
  154.1 0.0 copy-start.3
  154.1 1.6 copy.20
  155.7 1.9 %collective-permute-start.1 = (f32[2,12,9216]{2,0,1:T(2,128)}, f32[2,12,9216]{2,0,1:T(2,128)S(1)}, u32[]{:S(2)}, u32[]{:S(2)}) collective-permute-start(f32[2,12,9216]{2,0,1:T(2,128)} %copy.20), channel_id=1, source_target_pairs={{0,8},{8,0},{16,24},{24,16},{32,40},{40,32},{48,56},{56,48},{64,72... | collective-permute-start | bytes 2654216 | tf_op jit(solution)/shard_map/ppermute | solution.py:521
  157.6 0.1 pad_add_fusion.place
  157.7 17.7 %all-to-all-done.4 = f32[16,112,128]{2,1,0:T(8,128)S(1)} async-done(((f32[16,112,128]{2,1,0:T(8,128)}), f32[16,112,128]{2,1,0:T(8,128)S(1)}, u32[]{:S(2)}, u32[]{:S(2)}) %all-to-all-start.4) | async-done | bytes 917536 | tf_op jit(solution)/shard_map/all_to_all | solution.py:461
  175.4 0.7 finish.1
  176.1 3.5 %collective-permute-start.2 = (f32[2,12,288]{2,1,0:T(8,128)S(1)}, f32[2,12,288]{2,1,0:T(8,128)S(1)}, u32[]{:S(2)}, u32[]{:S(2)}) collective-permute-start(f32[2,12,288]{2,1,0:T(8,128)S(1)} %get-tuple-element.11), channel_id=1, source_target_pairs={{0,8},{8,0},{16,24},{24,16},{32,40},{40,32},{48,56},{56,48},{64,72... | collective-permute-start | bytes 82952 | tf_op jit(solution)/shard_map/ppermute | solution.py:532
  179.6 0.0 collective-permute-done.1
  179.6 0.0 copy-done.3
  179.6 0.4 fusion
  180.0 1.6 copy.22
  181.6 0.0 collective-permute-done.2
  181.7 0.7 copy.23
  (8 shorter events, 0.1 us)
Async XLA Ops:
  2.1 4.0 %copy-start.15 = (s32[32]{0:T(128)S(1)}, s32[32]{0:T(128)}, u32[]{:S(2)}) copy-start(s32[32]{0:T(128)} %param.11) | copy-start | bytes 388
  2.8 5.9 %collective-permute-start = (f32[2,12,9216]{2,0,1:T(2,128)S(1)}, f32[2,12,9216]{2,0,1:T(2,128)S(1)}, u32[]{:S(2)}, u32[]{:S(2)}) collective-permute-start(f32[2,12,9216]{2,0,1:T(2,128)S(1)} %copy.16), channel_id=1, source_target_pairs={{0,8},{8,0},{16,24},{24,16},{32,40},{40,32},{48,56},{56,48},{64,72... | collective-permute-start | bytes 2654216 | tf_op jit(solution)/shard_map/ppermute | solution.py:467
  8.9 60.1 %copy-start = (f32[2,12,9216]{2,1,0:T(8,128)}, f32[2,12,9216]{2,1,0:T(8,128)S(1)}, u32[]{:S(2)}) copy-start(f32[2,12,9216]{2,1,0:T(8,128)S(1)} %copy.17.other) | copy-start | bytes 2654212
  10.1 30.3 %all-to-all-start = ((f32[16,112,128]{2,1,0:T(8,128)}), f32[16,112,128]{2,1,0:T(8,128)S(1)}, u32[]{:S(2)}, u32[]{:S(2)}) async-start(f32[16,112,128]{2,1,0:T(8,128)} %bitcast.3), calls=%async_computation | async-start | bytes 1835008 | tf_op jit(solution)/shard_map/all_to_all | solution.py:461
  40.4 28.7 %copy-start.9 = (bf16[256,256]{1,0:T(8,128)(2,1)S(1)}, bf16[256,256]{1,0:T(8,128)(2,1)}, u32[]{:S(2)}) copy-start(bf16[256,256]{1,0:T(8,128)(2,1)} %constant.111.clone.low) | copy-start | bytes 393220
  40.4 28.7 %copy-start.10 = (bf16[256,256]{1,0:T(8,128)(2,1)S(1)}, bf16[256,256]{1,0:T(8,128)(2,1)}, u32[]{:S(2)}) copy-start(bf16[256,256]{1,0:T(8,128)(2,1)} %constant.110.clone.high) | copy-start | bytes 393220
  73.8 1.2 copy-start.1
  75.0 31.6 %copy-start.11 = (bf16[192,192]{1,0:T(8,128)(2,1)S(1)}, bf16[192,192]{1,0:T(8,128)(2,1)}, u32[]{:S(2)}) copy-start(bf16[192,192]{1,0:T(8,128)(2,1)} %constant.115.clone.il) | copy-start | bytes 221188
  75.0 31.6 %copy-start.12 = (bf16[192,192]{1,0:T(8,128)(2,1)S(1)}, bf16[192,192]{1,0:T(8,128)(2,1)}, u32[]{:S(2)}) copy-start(bf16[192,192]{1,0:T(8,128)(2,1)} %constant.114.clone.ih) | copy-start | bytes 221188
  75.0 31.6 %copy-start.13 = (bf16[192,192]{1,0:T(8,128)(2,1)S(1)}, bf16[192,192]{1,0:T(8,128)(2,1)}, u32[]{:S(2)}) copy-start(bf16[192,192]{1,0:T(8,128)(2,1)} %constant.113.clone.fl) | copy-start | bytes 221188
  75.0 31.7 %copy-start.14 = (bf16[192,192]{1,0:T(8,128)(2,1)S(1)}, bf16[192,192]{1,0:T(8,128)(2,1)}, u32[]{:S(2)}) copy-start(bf16[192,192]{1,0:T(8,128)(2,1)} %constant.112.clone.fh) | copy-start | bytes 221188
  75.0 31.6 %all-to-all-start.2 = ((f32[8,2,24,1152]{3,2,1,0:T(8,128)}), f32[8,2,24,1152]{3,2,1,0:T(8,128)}, u32[]{:S(2)}, u32[]{:S(2)}) async-start(f32[8,2,24,1152]{3,2,1,0:T(8,128)} %copy-done.1), calls=%async_computation.2 | async-start | bytes 3538944 | tf_op jit(solution)/shard_map/all_to_all | solution.py:464
  110.7 27.6 %copy-start.7 = (bf16[256,256]{1,0:T(8,128)(2,1)S(1)}, bf16[256,256]{1,0:T(8,128)(2,1)}, u32[]{:S(2)}) copy-start(bf16[256,256]{1,0:T(8,128)(2,1)} %constant.117.clone.low) | copy-start | bytes 393220
  110.7 27.6 %copy-start.8 = (bf16[256,256]{1,0:T(8,128)(2,1)S(1)}, bf16[256,256]{1,0:T(8,128)(2,1)}, u32[]{:S(2)}) copy-start(bf16[256,256]{1,0:T(8,128)(2,1)} %constant.116.clone.high) | copy-start | bytes 393220
  145.8 1.1 copy-start.2
  146.8 1.0 copy-start.4
  147.8 0.9 copy-start.6
  148.8 5.3 %copy-start.5 = (f32[2,12,9216]{2,1,0:T(8,128)S(1)}, f32[2,12,9216]{2,1,0:T(8,128)}, u32[]{:S(2)}) copy-start(f32[2,12,9216]{2,1,0:T(8,128)} %copy-done.4) | copy-start | bytes 2654212
  148.8 26.6 %all-to-all-start.4 = ((f32[16,112,128]{2,1,0:T(8,128)}), f32[16,112,128]{2,1,0:T(8,128)S(1)}, u32[]{:S(2)}, u32[]{:S(2)}) async-start(f32[16,112,128]{2,1,0:T(8,128)} %bitcast.26), calls=%async_computation.4 | async-start | bytes 1835008 | tf_op jit(solution)/shard_map/all_to_all | solution.py:461
  154.1 25.5 %copy-start.3 = (f32[2,12,9216]{2,1,0:T(8,128)S(1)}, f32[2,12,9216]{2,1,0:T(8,128)}, u32[]{:S(2)}) copy-start(f32[2,12,9216]{2,1,0:T(8,128)} %copy-done.2) | copy-start | bytes 2654212
  155.7 23.9 %collective-permute-start.1 = (f32[2,12,9216]{2,0,1:T(2,128)}, f32[2,12,9216]{2,0,1:T(2,128)S(1)}, u32[]{:S(2)}, u32[]{:S(2)}) collective-permute-start(f32[2,12,9216]{2,0,1:T(2,128)} %copy.20), channel_id=1, source_target_pairs={{0,8},{8,0},{16,24},{24,16},{32,40},{40,32},{48,56},{56,48},{64,72... | collective-permute-start | bytes 2654216 | tf_op jit(solution)/shard_map/ppermute | solution.py:521
  176.1 5.5 %collective-permute-start.2 = (f32[2,12,288]{2,1,0:T(8,128)S(1)}, f32[2,12,288]{2,1,0:T(8,128)S(1)}, u32[]{:S(2)}, u32[]{:S(2)}) collective-permute-start(f32[2,12,288]{2,1,0:T(8,128)S(1)} %get-tuple-element.11), channel_id=1, source_target_pairs={{0,8},{8,0},{16,24},{24,16},{32,40},{40,32},{48,56},{56,48},{64,72... | collective-permute-start | bytes 82952 | tf_op jit(solution)/shard_map/ppermute | solution.py:532

commit v3 on v2

v3 whole, which is shorter than its diff:
```python
import functools
import math

import jax
import jax.numpy as jnp
import ml_dtypes
import numpy as np
from jax import lax
from jax.experimental import pallas as pl
from jax.experimental.pallas import tpu as pltpu
from jax.sharding import PartitionSpec as P

NX = 96
NY = 96
NZ = 96
SERVE = 2
CHIPS = 16
PARTS = 8
ROWS = 24
PLANE = NY * NZ
BLOCK = PLANE // PARTS
CHUNK = 112
LIST = 8 * CHUNK
TILES = 108 * 8
HALF = PLANE // CHIPS // 2
UNROLL = True
VMEM = 48 * 1024 * 1024

cell_side = 41.04
mixing = 0.25


def frequencies(count):
    signed = (jnp.arange(count, dtype=jnp.int32) + count // 2) % count - count // 2
    return signed.astype(jnp.float32) * (2.0 * math.pi / cell_side)


def kernel_columns(start, width):
    freq_x = frequencies(NX)
    freq_y = lax.dynamic_slice_in_dim(frequencies(NY), start, width)
    freq_z = frequencies(NZ)
    freq_y = jnp.broadcast_to(freq_y[:, None], (width, NZ)).reshape(-1)
    freq_z = jnp.broadcast_to(freq_z[None], (width, NZ)).reshape(-1)
    squared = freq_x[:, None] ** 2 + freq_y[None] ** 2 + freq_z[None] ** 2
    radius = cell_side * (3.0 / (4.0 * math.pi)) ** (1.0 / 3.0)
    safe_square = jnp.where(squared > 0, squared, 1.0)
    general = 4.0 * math.pi * (1.0 - jnp.cos(jnp.sqrt(safe_square) * radius)) / safe_square
    return jnp.where(squared > 0, general, 2.0 * math.pi * radius * radius)


def split_table(table):
    high = table.astype(ml_dtypes.bfloat16)
    low = (table - high.astype(np.float64)).astype(ml_dtypes.bfloat16)
    return high, low


def angle_tables(sign):
    index = np.arange(96)
    angles = 2.0 * np.pi * (np.outer(index, index) % 96) / 96
    return np.cos(angles), sign * np.sin(angles)


def lane_table(sign):
    cosine, sine = angle_tables(sign)
    table = np.zeros((256, 256))
    table[:96, :96] = cosine
    table[128:224, 128:224] = cosine
    table[:96, 128:224] = sine
    table[128:224, :96] = -sine
    return split_table(table)


def slab_order():
    part = np.array([0] * 8 + [1] * 8 + [0] * 4 + [1] * 4)
    virtual = np.array(list(range(8)) * 2 + list(range(8, 12)) * 2)
    slot = np.array([0, 0, 0, 0, 1, 1, 1, 1, 0, 0, 1, 1])[virtual]
    local = np.array([0, 1, 2, 3, 0, 1, 2, 3, 4, 5, 4, 5])[virtual]
    planes = np.array([[0, 1, 2, 3, 8, 9], [4, 5, 6, 7, 10, 11]])
    places = [
        slot * 192 + part * 96 + 12 * f + planes[half][local] for half in range(2) for f in range(PARTS)
    ]
    return np.concatenate(places)


def row_tables():
    order = slab_order()
    cosine, sine = angle_tables(-1.0)
    single = np.block([[cosine, -sine], [sine, cosine]])
    forward = np.kron(np.eye(2), single)[:, order]
    cosine, sine = angle_tables(1.0)
    single = np.block([[cosine, -sine], [sine, cosine]])
    inverse = np.kron(np.eye(2), single)[order]
    return split_table(forward) + split_table(inverse)


def const_times(value, angle, count):
    re, im = value
    angle %= count
    if angle == 0:
        return value
    if 2 * angle == count:
        return (-re, -im)
    if 4 * angle == count:
        return (-im, re)
    if 4 * angle == 3 * count:
        return (im, -re)
    c = math.cos(2 * math.pi * angle / count)
    s = math.sin(2 * math.pi * angle / count)
    if (8 * angle) % count == 0:
        r = math.sqrt(0.5)
        c = math.copysign(1.0, c)
        s = math.copysign(1.0, s)
        a = re * (c * r)
        b = im * (c * r)
        return (a - b, a + b) if c == s else (a + b, b - a)
    return (re * c - im * s, re * s + im * c)


def add(a, b):
    return (a[0] + b[0], a[1] + b[1])


def sub(a, b):
    return (a[0] - b[0], a[1] - b[1])


def small_dft(x, sign):
    n = len(x)
    if n == 2:
        return [add(x[0], x[1]), sub(x[0], x[1])]
    if n == 3:
        total = add(x[1], x[2])
        diff = sub(x[1], x[2])
        r = sign * math.sqrt(0.75)
        mid = (x[0][0] - 0.5 * total[0], x[0][1] - 0.5 * total[1])
        turn = (-r * diff[1], r * diff[0])
        return [add(x[0], total), add(mid, turn), sub(mid, turn)]
    if n == 4:
        a, b = add(x[0], x[2]), sub(x[0], x[2])
        c, d = add(x[1], x[3]), sub(x[1], x[3])
        d = const_times(d, sign, 4)
        return [add(a, c), add(b, d), sub(a, c), sub(b, d)]
    inner = 4
    outer = n // inner
    out = [None] * n
    columns = []
    for low in range(outer):
        column = small_dft([x[outer * i + low] for i in range(inner)], sign)
        columns.append([const_times(v, sign * low * k, n) for k, v in enumerate(column)])
    for k in range(inner):
        row = small_dft([columns[low][k] for low in range(outer)], sign)
        for j in range(outer):
            out[k + inner * j] = row[j]
    return out


def leading_dft(field, sign):
    def tile(t, carry):
        rows = pl.ds(pl.multiple_of(t * 8, 8), 8)

        def load(y):
            return (field[y, rows, 0:128], field[y, rows, 128:256])

        def save(y, v):
            field[y, rows, 0:128] = v[0]
            field[y, rows, 128:256] = v[1]

        for low in range(8):
            column = small_dft([load(8 * i + low) for i in range(12)], sign)
            for k, v in enumerate(column):
                save(8 * k + low, const_times(v, sign * low * k, 96))
        return carry

    lax.fori_loop(0, 3, tile, 0, unroll=UNROLL)


def second_pass(field, k, rows, sign):
    values = [
        (field[8 * k + low, rows, 0:128], field[8 * k + low, rows, 128:256]) for low in range(8)
    ]
    return small_dft(values, sign)


def whole_dft(source, target, sign):
    leading_dft(source, sign)

    def tile(t, carry):
        rows = pl.ds(pl.multiple_of(t * 8, 8), 8)
        for k in range(12):
            for j, v in enumerate(second_pass(source, k, rows, sign)):
                target[k + 12 * j, rows, 0:128] = v[0]
                target[k + 12 * j, rows, 128:256] = v[1]
        return carry

    lax.fori_loop(0, 3, tile, 0, unroll=UNROLL)


def lanes():
    return lax.broadcasted_iota(jnp.int32, (8, 128), 1)


def unpack(wide):
    lane = lanes()
    out = []
    for q in range(3):
        a, b, c = (wide[:, 128 * (3 * q + i) : 128 * (3 * q + i + 1)] for i in range(3))
        out.append(a)
        out.append(jnp.where(lane < 32, pltpu.roll(a, 32, 1), pltpu.roll(b, 32, 1)))
        out.append(jnp.where(lane < 64, pltpu.roll(b, 64, 1), pltpu.roll(c, 64, 1)))
        out.append(pltpu.roll(c, 96, 1))
    return out


def pack(tiles):
    lane = lanes()
    out = []
    for q in range(3):
        a, b, c, d = tiles[4 * q : 4 * q + 4]
        b = pltpu.roll(b, 96, 1)
        c = pltpu.roll(c, 64, 1)
        d = pltpu.roll(d, 32, 1)
        out.append(jnp.where(lane < 96, a, b))
        out.append(jnp.where(lane < 64, b, c))
        out.append(jnp.where(lane < 32, c, d))
    return jnp.concatenate(out, axis=1)


def flip(x):
    return pltpu.roll(x, 4, 0)


def top(x):
    return lax.broadcasted_iota(jnp.int32, x.shape, 0) < 4


def split_dot(x, high, low):
    x_high = x.astype(jnp.bfloat16)
    x_low = (x - x_high.astype(jnp.float32)).astype(jnp.bfloat16)
    dot = functools.partial(jnp.dot, preferred_element_type=jnp.float32)
    return dot(x_high, high) + (dot(x_high, low) + dot(x_low, high))


def dot_split(high, low, x):
    x_high = x.astype(jnp.bfloat16)
    x_low = (x - x_high.astype(jnp.float32)).astype(jnp.bfloat16)
    dot = functools.partial(jnp.dot, preferred_element_type=jnp.float32)
    return dot(high, x_high) + (dot(low, x_high) + dot(high, x_low))


def row_index(x):
    return lax.broadcasted_iota(jnp.int32, x.shape, 0)


def combine(a0, a1, b0, b1):
    upper = top(a0)
    row = row_index(b0)
    rest = jnp.where(
        row < 2,
        b0,
        jnp.where(
            row < 4,
            pltpu.roll(b1, 2, 0),
            jnp.where(row < 6, pltpu.roll(b0, 2, 0), pltpu.roll(b1, 4, 0)),
        ),
    )
    return jnp.where(upper, a0, flip(a1)), jnp.where(upper, flip(a0), a1), rest


def split(t0, t1, t2):
    upper = top(t0)
    low = row_index(t2) < 2
    back = pltpu.roll(t2, 6, 0)
    return (
        jnp.where(upper, t0, flip(t1)),
        jnp.where(upper, flip(t0), t1),
        jnp.where(low, t2, back),
        jnp.where(low, back, flip(t2)),
    )


def list_load(ref, start):
    x = ref[pl.ds(pl.multiple_of(start, 8), 72), :]
    return jnp.concatenate([x[8 * i : 8 * i + 8] for i in range(9)], axis=1)


def list_save(ref, start, x):
    for i in range(9):
        ref[pl.ds(pl.multiple_of(start + 8 * i, 8), 8), :] = x[:, 128 * i : 128 * i + 128]


def second_start(g):
    return 8 * (72 + 9 * lax.rem(g, 4))


def half_load(ref, g):
    b = list_load(ref, second_start(g))
    return list_load(ref, 72 * g), jnp.where(g >= 4, flip(b), b)


def half_save(ref, g, a, b):
    list_save(ref, 72 * g, a)
    old = list_load(ref, second_start(g))
    upper = top(b)
    b = jnp.where(upper, b, flip(b))
    b = jnp.where(g < 4, jnp.where(upper, b, old), jnp.where(upper, old, b))
    list_save(ref, second_start(g), b)


def block_columns(g):
    return pl.ds(pl.multiple_of(g * BLOCK, 128), BLOCK)


def slab_rows(ref, g):
    cols = block_columns(g)
    rest = jnp.concatenate([ref[0, 8:12, cols], ref[1, 8:12, cols]], axis=0)
    return ref[0, 0:8, cols], ref[1, 0:8, cols], rest


def orbital_rows(ref, g):
    cols = block_columns(g)
    return ref[0:8, cols], ref[8:16, cols], ref[16:24, cols]


def halves_kernel(place, orbital, keep, send):
    first = place[2] == 0

    def block(g, carry):
        a0, a1, b0, b1 = split(*slab_rows(orbital, g))
        half_save(keep, g, jnp.where(first, a0, a1), jnp.where(first, b0, b1))
        half_save(send, g, jnp.where(first, a1, a0), jnp.where(first, b1, b0))
        return carry

    lax.fori_loop(0, PARTS, block, 0, unroll=UNROLL)
    for ref in (keep, send):
        ref[TILES:LIST, :] = jnp.zeros((LIST - TILES, 128), jnp.float32)


def assemble_kernel(place, keep, recv, keep_other, recv_other, mine, other):
    first = place[2] == 0

    def block(g, carry):
        cols = block_columns(g)
        for own, far, out in ((keep, recv, mine), (keep_other, recv_other, other)):
            (a0, b0), (a1, b1) = half_load(own, g), half_load(far, g)
            rows = combine(
                jnp.where(first, a0, a1),
                jnp.where(first, a1, a0),
                jnp.where(first, b0, b1),
                jnp.where(first, b1, b0),
            )
            for r in range(3):
                out[8 * r : 8 * r + 8, cols] = rows[r]
        return carry

    lax.fori_loop(0, PARTS, block, 0, unroll=UNROLL)


def applied_kernel(place, near, got, far, out):
    first = place[2] == 0

    def block(g, carry):
        cols = block_columns(g)
        a0, b0 = half_load(near, g)
        a1, b1 = half_load(got, g)
        a0, b0 = a0 + a1, b0 + b1
        a1, b1 = half_load(far, g)
        t0, t1, t2 = combine(
            jnp.where(first, a0, a1),
            jnp.where(first, a1, a0),
            jnp.where(first, b0, b1),
            jnp.where(first, b1, b0),
        )
        out[0, 0:8, cols] = t0
        out[1, 0:8, cols] = t1
        out[0, 8:12, cols] = t2[0:4]
        out[1, 8:12, cols] = t2[4:8]
        return carry

    lax.fori_loop(0, PARTS, block, 0, unroll=UNROLL)


def served_rows(ref, g):
    a, b = half_load(ref, g)
    return combine(a, a, b, b)


def forward_kernel(place, served, mine, other, table, out, line, field, spectrum):
    def block(g, carry):
        s0, s1, s2 = served_rows(served, g)
        parts = []
        rests = []
        for ref in (mine, other):
            re, im, rest = orbital_rows(ref, g)
            parts.append((s0 * re + s1 * im, s0 * im - s1 * re))
            same = s2 * rest
            cross = s2 * flip(rest)
            rests.append((same + flip(same), cross - flip(cross)))
        upper = top(s2)
        parts.append(
            (jnp.where(upper, rests[0][0], rests[1][0]), jnp.where(upper, rests[0][1], -rests[1][1]))
        )
        for t, (re, im) in enumerate(parts):
            for y, (a, b) in enumerate(zip(unpack(re), unpack(im))):
                line[24 * y + 8 * t : 24 * y + 8 * t + 8, 0:128] = a
                line[24 * y + 8 * t : 24 * y + 8 * t + 8, 128:256] = b
        result = split_dot(line[...], table[0:256], table[256:512])
        field[pl.ds(g * 12, 12)] = result.reshape(12, 24, 256)
        return carry

    lax.fori_loop(0, PARTS, block, 0, unroll=UNROLL)
    whole_dft(field, spectrum, -1)

    def send(g, carry):
        packed = []
        for t in range(3):
            rows = slice(8 * t, 8 * t + 8)
            packed.append(
                tuple(
                    pack([spectrum[g * 12 + y, rows, c : c + 128] for y in range(12)])
                    for c in (0, 128)
                )
            )
        re, im = packed[2]
        upper = top(re)
        for p, rest in enumerate(
            (jnp.where(upper, re, flip(im)), jnp.where(upper, flip(re), im))
        ):
            out[p, g, 0:8, :] = packed[p][0]
            out[p, g, 8:16, :] = packed[p][1]
            out[p, g, 16:24, :] = rest
        return carry

    lax.fori_loop(0, PARTS, send, 0, unroll=UNROLL)


def column_kernel(blocks, coulomb, tables, out):
    lanes_here = blocks.shape[-1]
    x = blocks[...].reshape(16 * ROWS, lanes_here)
    x = dot_split(tables[0:384], tables[384:768], x)
    k = coulomb[...]
    x = jnp.concatenate([x[96 * i : 96 * i + 96] * k for i in range(4)], axis=0)
    x = dot_split(tables[768:1152], tables[1152:1536], x)
    out[...] = x.reshape(16, ROWS, lanes_here)


def backward_kernel(
    place, blocks, served, mine, other, table, own_near, own_far, away_near, away_far, terms,
    line, field, spectrum, total,
):
    first = place[2] == 0

    def receive(g, carry):
        rests = [blocks[p, g, 16:24, :] for p in range(2)]
        upper = top(rests[0])
        parts = [(blocks[p, g, 0:8, :], blocks[p, g, 8:16, :]) for p in range(2)]
        parts.append(
            (
                jnp.where(upper, rests[0], flip(rests[1])),
                jnp.where(upper, flip(rests[0]), rests[1]),
            )
        )
        for t, (re, im) in enumerate(parts):
            rows = slice(8 * t, 8 * t + 8)
            for y, (a, b) in enumerate(zip(unpack(re), unpack(im))):
                spectrum[g * 12 + y, rows, 0:128] = a
                spectrum[g * 12 + y, rows, 128:256] = b
        return carry

    lax.fori_loop(0, PARTS, receive, 0, unroll=UNROLL)
    whole_dft(spectrum, field, 1)

    def block(g, carry):
        x = field[pl.ds(g * 12, 12)].reshape(288, 256)
        line[...] = split_dot(x, table[0:256], table[256:512])
        packed = []
        for t in range(3):
            packed.append(
                tuple(
                    pack([line[24 * y + 8 * t : 24 * y + 8 * t + 8, c : c + 128] for y in range(12)])
                    for c in (0, 128)
                )
            )
        re, im = packed[2]
        upper = top(re)
        rests = (jnp.where(upper, re, flip(im)), jnp.where(upper, flip(re), im))
        s0, s1, s2 = served_rows(served, g)
        sums = None
        for p, (ref, near, far) in enumerate(
            ((mine, own_near, own_far), (other, away_near, away_far))
        ):
            vr, vi = packed[p]
            v2 = rests[p]
            same = s2 * v2
            cross = s2 * flip(v2)
            a0, a1, b0, b1 = split(
                s0 * vr - s1 * vi,
                s0 * vi + s1 * vr,
                jnp.where(upper, same - flip(same), cross + flip(cross)),
            )
            half_save(near, g, jnp.where(first, a0, a1), jnp.where(first, b0, b1))
            half_save(far, g, jnp.where(first, a1, a0), jnp.where(first, b1, b0))
            ore, oim, rest = orbital_rows(ref, g)
            same = v2 * rest
            cross = v2 * flip(rest)
            turned = flip(cross)
            both = (
                vr * ore + vi * oim,
                vr * oim - vi * ore,
                jnp.where(upper, same + flip(same), turned - cross),
            )
            sums = both if sums is None else tuple(a + b for a, b in zip(sums, both))
        a0, a1, b0, b1 = split(*sums)
        half_save(total, g, a0 + a1, b0 + b1)
        return carry

    lax.fori_loop(0, PARTS, block, 0, unroll=UNROLL)
    lane = lanes()

    def tile(l):
        return total[8 * l : 8 * l + 8, :]

    def turn(x):
        return pltpu.roll(x, 64, 1)

    for g in range(4):
        middle = 9 * g + 4
        for odd in range(2):
            begin = 9 * g + 5 * odd
            tiles = [tile(begin + i) for i in range(4)] + [tile(begin + 36 + i) for i in range(4)]
            a, b = tile(middle), tile(middle + 36)
            a, b = (turn(a), b) if odd else (a, turn(b))
            tiles.append(jnp.where(lane < 64, a, b))
            tiles += [tile(72 + begin + i) for i in range(4)]
            a = tile(72 + middle)
            tiles.append(turn(a) if odd else a)
            for i, x in enumerate(tiles):
                start = (2 * g + odd) * CHUNK + 8 * i
                terms[start : start + 8, :] = x


def finish_kernel(place, blocks, *pieces):
    lane = lanes()
    second_core = place[0] == 1
    odd = place[1] == 1
    second_half = place[2] == 1
    tiles = []
    for i in range(14):
        x = [blocks[CHUNK * q + 8 * i : CHUNK * q + 8 * i + 8, :] for q in range(8)]
        while len(x) > 1:
            x = [x[2 * j] + x[2 * j + 1] for j in range(len(x) // 2)]
        tiles.append(x[0])

    def widen(f, h):
        s = [pltpu.roll(x, 64, 1) for x in f]
        wide = [
            jnp.where(odd, jnp.where(lane < 64, a, b), c)
            for a, b, c in zip([h] + s, s + [s[3]], f + [h])
        ]
        s = [pltpu.roll(x, 96, 1) for x in wide[2:]]
        second = [jnp.where(lane < 96, s[0], s[1]), jnp.where(lane < 96, s[1], s[2]), s[2]]
        return wide[:3], second

    left = widen(tiles[0:4], tiles[8])
    right = widen(tiles[4:8], pltpu.roll(tiles[8], 64, 1))
    rest = widen(tiles[9:13], tiles[13])
    for piece, out in enumerate(pieces):
        half = second_half if piece < 2 else jnp.logical_not(second_half)
        core = second_core if piece % 2 == 0 else jnp.logical_not(second_core)
        for i in range(3):
            x = [jnp.where(core, y[1][i], y[0][i]) for y in (left, right, rest)]
            a = jnp.where(half, x[1], x[0])
            b = jnp.where(half, flip(x[2]), x[2])
            width = 128 if i < 2 else 32
            cols = slice(128 * i, 128 * i + width)
            out[0:8, cols] = a[:, :width]
            out[8:12, cols] = b[0:4, :width]


def serving_kernel(place, p00, p01, p10, p11, out):
    second_core = place[0] == 1
    second_half = place[2] == 1
    x = [[p00[...], p01[...]], [p10[...], p11[...]]]
    for member in range(2):
        swap = second_core if member == 0 else jnp.logical_not(second_core)
        near, far = (jnp.where(swap, x[i][1], x[i][0]) for i in range(2))
        h0 = jnp.where(second_half, far, near)
        h1 = jnp.where(second_half, near, far)
        for part in range(2):
            out[member, part, 0:4, :] = h0[4 * part : 4 * part + 4]
            out[member, part, 4:8, :] = h1[4 * part : 4 * part + 4]
            out[member, part, 8:10, :] = h0[8 + 2 * part : 10 + 2 * part]
            out[member, part, 10:12, :] = h1[8 + 2 * part : 10 + 2 * part]


def f32(*shape):
    return jax.ShapeDtypeStruct(shape, jnp.float32)


def shards(orbitals, serve_order):
    rank_fft = lax.axis_index("fft")
    rank_band = lax.axis_index("band")
    core = rank_band % 2
    line = rank_band // 2 % 8
    half = rank_band // 16
    place = jnp.stack([core, line % 2, half]).astype(jnp.int32)
    z_groups = [[y * 16 + 2 * z + c for z in range(8)] for y in range(2) for c in range(2)]
    plane_groups = [
        [(y * 16 + b) * PARTS + f for y in range(2) for f in range(PARTS)] for b in range(16)
    ]
    scale = -mixing / (NX * NY * NZ)

    coulomb = kernel_columns(rank_fft * 12, 12) * scale
    params = pltpu.CompilerParams(vmem_limit_bytes=VMEM)
    scalars = pl.BlockSpec(memory_space=pltpu.SMEM)
    whole = pl.BlockSpec(memory_space=pltpu.VMEM)

    def call(kernel, shapes, inputs, scratch=()):
        return pl.pallas_call(
            kernel,
            out_shape=shapes,
            in_specs=[scalars] + [whole] * len(inputs),
            out_specs=jax.tree.map(lambda _: whole, shapes),
            scratch_shapes=list(scratch),
            compiler_params=params,
        )(place, *inputs)

    def swap(x, bits):
        return lax.ppermute(x, "band", [(i, i ^ bits) for i in range(32)])

    def line_exchange(blocks):
        return lax.all_to_all(blocks, "band", 0, 0, axis_index_groups=z_groups, tiled=True)

    def plane_exchange(blocks):
        return lax.all_to_all(
            blocks, ("band", "fft"), 0, 0, axis_index_groups=plane_groups, tiled=True
        )

    lists = f32(LIST, 128)
    keep, send = call(halves_kernel, (lists, lists), (orbitals.reshape(2, 12, PLANE),))
    recv = swap(send, 16)
    keep_other = swap(keep, 1)
    recv_other = swap(recv, 1)
    serving = serve_order[core]
    near = serving // 16 == half
    same = serving % 2 == core
    candidate = jnp.where(
        same, jnp.where(near, keep, recv), jnp.where(near, keep_other, recv_other)
    )
    blocks = line_exchange(candidate.reshape(8, CHUNK, 128))
    block = lax.dynamic_index_in_dim(blocks, serving // 2 % 8, 0, keepdims=True)
    block, coulomb = lax.optimization_barrier((block, coulomb))
    served = line_exchange(jnp.broadcast_to(block, blocks.shape)).reshape(LIST, 128)
    rows = f32(ROWS, PLANE)
    mine, other = call(assemble_kernel, (rows, rows), (keep, recv, keep_other, recv_other))

    scratch = [
        pltpu.VMEM((288, 256), jnp.float32),
        pltpu.VMEM((NY, ROWS, 256), jnp.float32),
        pltpu.VMEM((NY, ROWS, 256), jnp.float32),
    ]
    table = jnp.asarray(np.concatenate(lane_table(-1.0)))
    blocks = call(
        forward_kernel, f32(2, PARTS, ROWS, BLOCK), (served, mine, other, table), scratch
    )
    blocks = plane_exchange(blocks.reshape(16, ROWS, BLOCK))
    tables = jnp.asarray(np.concatenate(row_tables()))
    fixed = pl.BlockSpec((4 * 384, 384), lambda i: (0, 0))
    piece = pl.BlockSpec((16, ROWS, BLOCK // 3), lambda i: (0, 0, i))
    blocks = pl.pallas_call(
        column_kernel,
        out_shape=f32(16, ROWS, BLOCK),
        grid=(3,),
        in_specs=[piece, pl.BlockSpec((NX, BLOCK // 3), lambda i: (0, i)), fixed],
        out_specs=piece,
        compiler_params=params,
    )(blocks, coulomb, tables)
    blocks = plane_exchange(blocks).reshape(2, PARTS, ROWS, BLOCK)
    table = jnp.asarray(np.concatenate(lane_table(1.0)))
    short = f32(TILES, 128)
    own_near, own_far, away_near, away_far, terms = call(
        backward_kernel,
        (short, short, short, short, lists),
        (blocks, served, mine, other, table),
        scratch + [pltpu.VMEM((TILES, 128), jnp.float32)],
    )
    far = swap(own_far + swap(away_far, 1), 16)
    got = swap(away_near, 1)
    applied = call(applied_kernel, f32(2, 12, PLANE), (own_near, got, far))
    blocks = line_exchange(terms.reshape(8, CHUNK, 128)).reshape(LIST, 128)
    blocks, applied = lax.optimization_barrier((blocks, applied))
    small = f32(12, HALF)
    pieces = call(finish_kernel, (small,) * 4, (blocks,))
    pieces = [pieces[0], swap(pieces[1], 1), swap(pieces[2], 16), swap(pieces[3], 17)]
    serving_exchange = call(serving_kernel, f32(SERVE, 2, 12, HALF), pieces)
    return (applied.reshape(1, 2, 12, PLANE), serving_exchange)


def solution(mesh):
    return jax.shard_map(
        shards,
        mesh=mesh,
        in_specs=(P("band", None, "fft", None), P()),
        out_specs=(P("band", None, "fft", None), P(None, None, "fft", "band")),
        check_vma=False,
    )
```

time: 183 us -> 168 us (0.918)
  waiting for transfers between devices: 62.9 us -> 50.9 us
  local copies, waits for them, and re-layouts: 11.4 us -> 8.15 us
  starting transfers between devices: 28.1 us -> 26.2 us
    all_to_all x3, waiting for transfers between devices: 62.9 us -> 31.7 us  [line_exchange(): lax.all_to_all(blocks, 'band', 0, 0, axis_index_groups=z_groups, tiled=True)]
    ppermute x3 -> x9, waiting for transfers between devices: 0.01 us -> 19.2 us  [swap(): return lax.ppermute(x, 'band', [(i, i ^ bits) for i in range(32)])]
    all_to_all x3, starting transfers between devices: 19.4 us -> 15.3 us  [line_exchange(): lax.all_to_all(blocks, 'band', 0, 0, axis_index_groups=z_groups, tiled=True)]
    ppermute x3 -> x9, starting transfers between devices: 8.71 us -> 10.9 us  [swap(): return lax.ppermute(x, 'band', [(i, i ^ bits) for i in range(32)])]
    unnamed x35 -> x23, local copies, waits for them, and re-layouts: 7.97 us -> 6.54 us
    pallas_call x5 -> x8, Pallas kernels: 18 us -> 17.1 us  [the longest x7 12.1 us: call(): pl.pallas_call(kernel, out_shape=shapes, in_specs=[scalars] + [whole] * l...]
  transfers between devices with their start and end apart: 6 -> 12, of which waited for: 3 -> 7; matrix products, arithmetic and copies ran while one was open for 3% -> 3% of each run, Pallas kernels for 0% -> 1%
where the time goes in v3:
time: 168 us; the launch traced here: 167 us
  blocking collectives  57.8 us (34%)
  waiting for transfers between devices  50.9 us (30%)
  starting transfers between devices  26.2 us (16%)
  Pallas kernels  17.1 us (10%)
  local copies, waits for them, and re-layouts  8.15 us (5%)
  other arithmetic  3.71 us (2%)
  between operations  3.55 us (2%)
    all_to_all x2, blocking collectives, plane_exchange(): lax.all_to_all(blocks, ('band', 'fft'), 0, 0, axis_index_groups=plane_gro...  57.8 us
    all_to_all x3, waiting for transfers between devices, line_exchange(): lax.all_to_all(blocks, 'band', 0, 0, axis_index_groups=z_groups, tiled=True)  31.7 us
    ppermute x9, waiting for transfers between devices, swap(): return lax.ppermute(x, 'band', [(i, i ^ bits) for i in range(32)])  19.2 us
    all_to_all x3, starting transfers between devices, line_exchange(): lax.all_to_all(blocks, 'band', 0, 0, axis_index_groups=z_groups, tiled=True)  15.3 us
    pallas_call x7, Pallas kernels, call(): pl.pallas_call(kernel, out_shape=shapes, in_specs=[scalars] + [whole] * l...  12.1 us
    ppermute x9, starting transfers between devices, swap(): return lax.ppermute(x, 'band', [(i, i ^ bits) for i in range(32)])  10.9 us
    unnamed x23, local copies, waits for them, and re-layouts  6.54 us
    pallas_call x1, Pallas kernels, shards(): pl.pallas_call(column_kernel, out_shape=f32(16, ROWS, BLOCK), grid=(3,),...  5.02 us
  transfers between devices with their start and end apart: 12, of which 7 were waited for; matrix products, arithmetic and copies ran while one was open for 3% of the time, Pallas kernels for 1%

profile of v3, /device:TPU:1, one launch (start us, length us, event | category | flops | bytes accessed | tf_op | source)
XLA Modules:
  0.0 167.4 jit_solution(8529487763551870212)
XLA Ops:
  0.6 0.0 copy-start.9
  0.7 1.4 copy.11
  2.2 0.1 pad_add_fusion.place
  2.2 0.7 shard_map.68
  3.0 2.2 %collective-permute-start = (f32[896,128]{1,0:T(8,128)S(1)}, f32[896,128]{1,0:T(8,128)S(1)}, u32[]{:S(2)}, u32[]{:S(2)}) collective-permute-start(f32[896,128]{1,0:T(8,128)S(1)} %get-tuple-element.20), channel_id=1, source_target_pairs={{0,128},{8,136},{16,144},{24,152},{32,160},{40,168},{48,176},{56,1... | collective-permute-start | bytes 1376264 | tf_op jit(solution)/shard_map/ppermute | solution.py:628
  5.2 1.2 collective-permute-start.1
  6.4 7.8 %collective-permute-done.recv = f32[896,128]{1,0:T(8,128)S(1)} collective-permute-done((f32[896,128]{1,0:T(8,128)S(1)}, f32[896,128]{1,0:T(8,128)S(1)}, u32[]{:S(2)}, u32[]{:S(2)}) %collective-permute-start) | collective-permute-done | bytes 458784 | tf_op jit(solution)/shard_map/ppermute | solution.py:628
  14.2 2.5 %collective-permute-start.2 = (f32[896,128]{1,0:T(8,128)S(1)}, f32[896,128]{1,0:T(8,128)S(1)}, u32[]{:S(2)}, u32[]{:S(2)}) collective-permute-start(f32[896,128]{1,0:T(8,128)S(1)} %collective-permute-done.recv), channel_id=1, source_target_pairs={{0,8},{8,0},{16,24},{24,16},{32,40},{40,32},{48,56},{56,48},{64,72... | collective-permute-start | bytes 1376264 | tf_op jit(solution)/shard_map/ppermute | solution.py:628
  16.7 0.0 copy-done.9
  16.7 0.6 dynamic_slice.10
  19.9 0.0 collective-permute-done.1.keep_other
  19.9 0.0 copy-start
  19.9 0.0 collective-permute-done.2.recv_other
  19.9 0.0 copy-start.2
  19.9 1.0 select_select_fusion
  20.9 8.3 %all-to-all-start = ((f32[8,112,128]{2,1,0:T(8,128)}), f32[8,112,128]{2,1,0:T(8,128)S(1)}, u32[]{:S(2)}, u32[]{:S(2)}) async-start(f32[8,112,128]{2,1,0:T(8,128)} %bitcast.5), calls=%async_computation | async-start | bytes 917504 | tf_op jit(solution)/shard_map/all_to_all | solution.py:631
  29.3 0.1 dynamic-slice_multiply_fusion
  29.3 0.1 broadcast_in_dim.13
  29.4 0.1 integer_pow.34
  29.5 0.1 integer_pow.35
  29.6 2.5 %fusion.coulomb = f32[96,1152]{1,0:T(8,128)} fusion(f32[1152]{0:T(1024)S(1)} %integer_pow.35, f32[1152]{0:T(1024)S(1)} %integer_pow.34, f32[96]{0:T(128)S(1)} %fusion.4), kind=kLoop, calls=%fused_computation.4 | loop fusion | flops 1105920 | bytes 451968 | tf_op jit(solution)/shard_map/mul | solution.py:612
  32.1 0.0 copy-done
  32.1 0.0 copy-done.2
  32.1 0.0 copy-start.7
  32.1 13.8 %all-to-all-done = f32[8,112,128]{2,1,0:T(8,128)S(1)} async-done(((f32[8,112,128]{2,1,0:T(8,128)}), f32[8,112,128]{2,1,0:T(8,128)S(1)}, u32[]{:S(2)}, u32[]{:S(2)}) %all-to-all-start) | async-done | bytes 458784 | tf_op jit(solution)/shard_map/all_to_all | solution.py:631
  45.9 0.8 broadcast_in_dim.29
  46.7 3.5 %all-to-all-start.1 = ((f32[8,112,128]{2,1,0:T(8,128)}), f32[8,112,128]{2,1,0:T(8,128)S(1)}, u32[]{:S(2)}, u32[]{:S(2)}) async-start(f32[8,112,128]{2,1,0:T(8,128)} %broadcast_in_dim.29), calls=%async_computation.1 | async-start | bytes 917504 | tf_op jit(solution)/shard_map/all_to_all | solution.py:631
  50.2 0.0 copy-start.1
  50.2 1.0 copy-done.1
  51.2 1.0 copy-done.3
  52.2 0.8 shard_map.69
  53.0 13.6 %all-to-all-done.1 = f32[8,112,128]{2,1,0:T(8,128)S(1)} async-done(((f32[8,112,128]{2,1,0:T(8,128)}), f32[8,112,128]{2,1,0:T(8,128)S(1)}, u32[]{:S(2)}, u32[]{:S(2)}) %all-to-all-start.1) | async-done | bytes 458784 | tf_op jit(solution)/shard_map/all_to_all | solution.py:631
  66.6 0.0 copy-done.7
  66.6 2.9 %shard_map.70 = f32[2,8,24,1152]{3,2,1,0:T(8,128)S(1)} custom-call(s32[3]{0:T(128)S(1)} %pad_add_fusion.place, f32[896,128]{1,0:T(8,128)S(1)} %bitcast.18, f32[24,9216]{1,0:T(8,128)S(1)} %get-tuple-element.22.mine, f32[24,9216]{1,0:T(8,128)S(1)} %get-tuple-element.23.other, bf16[512,256]{1,0:T(8,128)(2,1)S(1)} %copy-done.7), custom_call_target="tpu_custom_call" | custom-call | tf_op jit(solution)/shard_map/pallas_call | solution.py:618
  69.6 0.0 copy-start.4
  69.6 0.0 copy-start.5
  69.6 30.9 %all_to_all.25.blocks = f32[16,24,1152]{2,1,0:T(8,128)S(1)} all-to-all(f32[16,24,1152]{2,1,0:T(8,128)S(1)} %bitcast.15), channel_id=1, replica_groups={{0,1,2,3,4,5,6,7,128,129,130,131,132,133,134,135},{8,9,10,11,12,13,14,1..., dimensions={0} | all-to-all | bytes 3538944 | tf_op jit(solution)/shard_map/all_to_all | solution.py:634
  100.5 0.0 copy-done.4
  100.5 0.0 copy-done.5
  100.5 5.0 %shard_map.71 = f32[16,24,1152]{2,1,0:T(8,128)S(1)} custom-call(f32[16,24,1152]{2,1,0:T(8,128)S(1)} %all_to_all.25.blocks, f32[96,1152]{1,0:T(8,128)S(1)} %copy-done.4, bf16[1536,384]{1,0:T(8,128)(2,1)S(1)} %copy-done.5), custom_call_target="tpu_custom_call" | custom-call | tf_op jit(solution)/shard_map/pallas_call | solution.py:669
  105.5 0.0 copy-start.6
  105.5 26.9 %all_to_all.26 = f32[16,24,1152]{2,1,0:T(8,128)} all-to-all(f32[16,24,1152]{2,1,0:T(8,128)S(1)} %shard_map.71), channel_id=1, replica_groups={{0,1,2,3,4,5,6,7,128,129,130,131,132,133,134,135},{8,9,10,11,12,13,14,1..., dimensions={0} | all-to-all | bytes 3538944 | tf_op jit(solution)/shard_map/all_to_all | solution.py:634
  132.4 0.0 copy-done.6
  132.4 5.6 %shard_map.72 = (f32[864,128]{1,0:T(8,128)S(1)}, f32[864,128]{1,0:T(8,128)S(1)}, f32[864,128]{1,0:T(8,128)S(1)}, f32[864,128]{1,0:T(8,128)}, f32[896,128]{1,0:T(8,128)}) custom-call(s32[3]{0:T(128)S(1)} %pad_add_fusion.place, f32[2,8,24,1152]{3,2,1,0:T(8,128)} %bitcast.21, f32[896,128]{1,0:T(8,128)S(1)} %bitcast.19, f32[24,9216]{1,0:T(8,128)S(1)} %get-tuple-element.22.mine, ...), custom_call_target="tpu_custom_call" | custom-call | tf_op jit(solution)/shard_map/pallas_call | solution.py:618
  138.1 0.8 copy-done.8
  138.8 2.5 %collective-permute-start.4 = (f32[864,128]{1,0:T(8,128)}, f32[864,128]{1,0:T(8,128)S(1)}, u32[]{:S(2)}, u32[]{:S(2)}) collective-permute-start(f32[864,128]{1,0:T(8,128)} %get-tuple-element.29), channel_id=1, source_target_pairs={{0,8},{8,0},{16,24},{24,16},{32,40},{40,32},{48,56},{56,48},{64,72... | collective-permute-start | bytes 1327112 | tf_op jit(solution)/shard_map/ppermute | solution.py:628
  141.3 3.5 %all-to-all-start.4 = ((f32[8,112,128]{2,1,0:T(8,128)}), f32[8,112,128]{2,1,0:T(8,128)S(1)}, u32[]{:S(2)}, u32[]{:S(2)}) async-start(f32[8,112,128]{2,1,0:T(8,128)} %bitcast.10), calls=%async_computation.4 | async-start | bytes 917504 | tf_op jit(solution)/shard_map/all_to_all | solution.py:631
  144.8 0.1 collective-permute-start.3
  144.9 0.0 collective-permute-done.4
  145.0 0.1 collective-permute-start.5
  145.1 1.8 %collective-permute-done.3.got = f32[864,128]{1,0:T(8,128)S(1)} collective-permute-done((f32[864,128]{1,0:T(8,128)}, f32[864,128]{1,0:T(8,128)S(1)}, u32[]{:S(2)}, u32[]{:S(2)}) %collective-permute-start.3) | collective-permute-done | bytes 442400 | tf_op jit(solution)/shard_map/ppermute | solution.py:628
  146.9 9.4 %collective-permute-done.5.far = f32[864,128]{1,0:T(8,128)S(1)} collective-permute-done((f32[864,128]{1,0:T(8,128)S(1)}, f32[864,128]{1,0:T(8,128)S(1)}, u32[]{:S(2)}, u32[]{:S(2)}) %collective-permute-start.5) | collective-permute-done | bytes 442400 | tf_op jit(solution)/shard_map/ppermute | solution.py:628
  156.3 0.7 shard_map.73
  157.1 4.3 %all-to-all-done.4 = f32[8,112,128]{2,1,0:T(8,128)S(1)} async-done(((f32[8,112,128]{2,1,0:T(8,128)}), f32[8,112,128]{2,1,0:T(8,128)S(1)}, u32[]{:S(2)}, u32[]{:S(2)}) %all-to-all-start.4) | async-done | bytes 458784 | tf_op jit(solution)/shard_map/all_to_all | solution.py:631
  161.4 0.7 shard_map.74
  162.1 0.5 collective-permute-start.6
  162.6 0.0 collective-permute-start.7
  162.7 1.7 %collective-permute-start.8 = (f32[12,288]{1,0:T(8,128)S(1)}, f32[12,288]{1,0:T(8,128)S(1)}, u32[]{:S(2)}, u32[]{:S(2)}) collective-permute-start(f32[12,288]{1,0:T(8,128)S(1)} %get-tuple-element.35), channel_id=1, source_target_pairs={{0,136},{8,128},{16,152},{24,144},{32,168},{40,160},{48,184},{56,1... | collective-permute-start | bytes 41480 | tf_op jit(solution)/shard_map/ppermute | solution.py:628
  164.3 1.6 copy.8
  165.9 0.0 collective-permute-done.6.p01
  165.9 0.0 collective-permute-done.7.p10
  165.9 0.2 collective-permute-done.8.p11
  166.1 0.6 shard_map.75
  166.7 0.7 copy.9
  (7 shorter events, 0.1 us)
Async XLA Ops:
  0.6 16.0 %copy-start.9 = (s32[32]{0:T(128)S(1)}, s32[32]{0:T(128)}, u32[]{:S(2)}) copy-start(s32[32]{0:T(128)} %param.6) | copy-start | bytes 388
  3.0 11.2 %collective-permute-start = (f32[896,128]{1,0:T(8,128)S(1)}, f32[896,128]{1,0:T(8,128)S(1)}, u32[]{:S(2)}, u32[]{:S(2)}) collective-permute-start(f32[896,128]{1,0:T(8,128)S(1)} %get-tuple-element.20), channel_id=1, source_target_pairs={{0,128},{8,136},{16,144},{24,152},{32,160},{40,168},{48,176},{56,1... | collective-permute-start | bytes 1376264 | tf_op jit(solution)/shard_map/ppermute | solution.py:628
  5.2 14.7 %collective-permute-start.1 = (f32[896,128]{1,0:T(8,128)S(1)}, f32[896,128]{1,0:T(8,128)S(1)}, u32[]{:S(2)}, u32[]{:S(2)}) collective-permute-start(f32[896,128]{1,0:T(8,128)S(1)} %get-tuple-element.19.keep), channel_id=1, source_target_pairs={{0,8},{8,0},{16,24},{24,16},{32,40},{40,32},{48,56},{56,48},{64,72... | collective-permute-start | bytes 1376264 | tf_op jit(solution)/shard_map/ppermute | solution.py:628
  14.2 5.7 %collective-permute-start.2 = (f32[896,128]{1,0:T(8,128)S(1)}, f32[896,128]{1,0:T(8,128)S(1)}, u32[]{:S(2)}, u32[]{:S(2)}) collective-permute-start(f32[896,128]{1,0:T(8,128)S(1)} %collective-permute-done.recv), channel_id=1, source_target_pairs={{0,8},{8,0},{16,24},{24,16},{32,40},{40,32},{48,56},{56,48},{64,72... | collective-permute-start | bytes 1376264 | tf_op jit(solution)/shard_map/ppermute | solution.py:628
  19.9 12.2 %copy-start = (f32[896,128]{1,0:T(8,128)}, f32[896,128]{1,0:T(8,128)S(1)}, u32[]{:S(2)}) copy-start(f32[896,128]{1,0:T(8,128)S(1)} %collective-permute-done.1.keep_other) | copy-start | bytes 1376260
  19.9 12.2 %copy-start.2 = (f32[896,128]{1,0:T(8,128)}, f32[896,128]{1,0:T(8,128)S(1)}, u32[]{:S(2)}) copy-start(f32[896,128]{1,0:T(8,128)S(1)} %collective-permute-done.2.recv_other) | copy-start | bytes 1376260
  20.9 25.0 %all-to-all-start = ((f32[8,112,128]{2,1,0:T(8,128)}), f32[8,112,128]{2,1,0:T(8,128)S(1)}, u32[]{:S(2)}, u32[]{:S(2)}) async-start(f32[8,112,128]{2,1,0:T(8,128)} %bitcast.5), calls=%async_computation | async-start | bytes 917504 | tf_op jit(solution)/shard_map/all_to_all | solution.py:631
  32.1 34.5 %copy-start.7 = (bf16[512,256]{1,0:T(8,128)(2,1)S(1)}, bf16[512,256]{1,0:T(8,128)(2,1)}, u32[]{:S(2)}) copy-start(bf16[512,256]{1,0:T(8,128)(2,1)} %constant.131.clone.table) | copy-start | bytes 786436
  46.7 20.0 %all-to-all-start.1 = ((f32[8,112,128]{2,1,0:T(8,128)}), f32[8,112,128]{2,1,0:T(8,128)S(1)}, u32[]{:S(2)}, u32[]{:S(2)}) async-start(f32[8,112,128]{2,1,0:T(8,128)} %broadcast_in_dim.29), calls=%async_computation.1 | async-start | bytes 917504 | tf_op jit(solution)/shard_map/all_to_all | solution.py:631
  50.2 1.0 copy-start.1
  51.2 1.0 copy-start.3
  69.6 30.9 %copy-start.4 = (f32[96,1152]{1,0:T(8,128)S(1)}, f32[96,1152]{1,0:T(8,128)}, u32[]{:S(2)}) copy-start(f32[96,1152]{1,0:T(8,128)} %fusion.coulomb) | copy-start | bytes 1327108
  69.6 30.9 %copy-start.5 = (bf16[1536,384]{1,0:T(8,128)(2,1)S(1)}, bf16[1536,384]{1,0:T(8,128)(2,1)}, u32[]{:S(2)}) copy-start(bf16[1536,384]{1,0:T(8,128)(2,1)} %constant.132.clone.tables) | copy-start | bytes 3538948
  105.5 26.9 %copy-start.6 = (bf16[512,256]{1,0:T(8,128)(2,1)S(1)}, bf16[512,256]{1,0:T(8,128)(2,1)}, u32[]{:S(2)}) copy-start(bf16[512,256]{1,0:T(8,128)(2,1)} %constant.133.clone.table) | copy-start | bytes 786436
  138.1 0.8 copy-start.8
  138.8 6.1 %collective-permute-start.4 = (f32[864,128]{1,0:T(8,128)}, f32[864,128]{1,0:T(8,128)S(1)}, u32[]{:S(2)}, u32[]{:S(2)}) collective-permute-start(f32[864,128]{1,0:T(8,128)} %get-tuple-element.29), channel_id=1, source_target_pairs={{0,8},{8,0},{16,24},{24,16},{32,40},{40,32},{48,56},{56,48},{64,72... | collective-permute-start | bytes 1327112 | tf_op jit(solution)/shard_map/ppermute | solution.py:628
  141.3 20.0 %all-to-all-start.4 = ((f32[8,112,128]{2,1,0:T(8,128)}), f32[8,112,128]{2,1,0:T(8,128)S(1)}, u32[]{:S(2)}, u32[]{:S(2)}) async-start(f32[8,112,128]{2,1,0:T(8,128)} %bitcast.10), calls=%async_computation.4 | async-start | bytes 917504 | tf_op jit(solution)/shard_map/all_to_all | solution.py:631
  144.8 2.1 %collective-permute-start.3 = (f32[864,128]{1,0:T(8,128)}, f32[864,128]{1,0:T(8,128)S(1)}, u32[]{:S(2)}, u32[]{:S(2)}) collective-permute-start(f32[864,128]{1,0:T(8,128)} %copy-done.8), channel_id=1, source_target_pairs={{0,8},{8,0},{16,24},{24,16},{32,40},{40,32},{48,56},{56,48},{64,72... | collective-permute-start | bytes 1327112 | tf_op jit(solution)/shard_map/ppermute | solution.py:628
  145.0 11.3 %collective-permute-start.5 = (f32[864,128]{1,0:T(8,128)S(1)}, f32[864,128]{1,0:T(8,128)S(1)}, u32[]{:S(2)}, u32[]{:S(2)}) collective-permute-start(f32[864,128]{1,0:T(8,128)S(1)} %add.117), channel_id=1, source_target_pairs={{0,128},{8,136},{16,144},{24,152},{32,160},{40,168},{48,176},{56,1... | collective-permute-start | bytes 1327112 | tf_op jit(solution)/shard_map/ppermute | solution.py:628
  162.1 3.9 %collective-permute-start.6 = (f32[12,288]{1,0:T(8,128)S(1)}, f32[12,288]{1,0:T(8,128)S(1)}, u32[]{:S(2)}, u32[]{:S(2)}) collective-permute-start(f32[12,288]{1,0:T(8,128)S(1)} %get-tuple-element.33), channel_id=1, source_target_pairs={{0,8},{8,0},{16,24},{24,16},{32,40},{40,32},{48,56},{56,48},{64,72... | collective-permute-start | bytes 41480 | tf_op jit(solution)/shard_map/ppermute | solution.py:628
  162.6 3.3 %collective-permute-start.7 = (f32[12,288]{1,0:T(8,128)S(1)}, f32[12,288]{1,0:T(8,128)S(1)}, u32[]{:S(2)}, u32[]{:S(2)}) collective-permute-start(f32[12,288]{1,0:T(8,128)S(1)} %get-tuple-element.34), channel_id=1, source_target_pairs={{0,128},{8,136},{16,144},{24,152},{32,160},{40,168},{48,176},{56,1... | collective-permute-start | bytes 41480 | tf_op jit(solution)/shard_map/ppermute | solution.py:628
  162.7 3.5 %collective-permute-start.8 = (f32[12,288]{1,0:T(8,128)S(1)}, f32[12,288]{1,0:T(8,128)S(1)}, u32[]{:S(2)}, u32[]{:S(2)}) collective-permute-start(f32[12,288]{1,0:T(8,128)S(1)} %get-tuple-element.35), channel_id=1, source_target_pairs={{0,136},{8,128},{16,152},{24,144},{32,168},{40,160},{48,184},{56,1... | collective-permute-start | bytes 41480 | tf_op jit(solution)/shard_map/ppermute | solution.py:628

commit v4 on v3

--- a/solution.py
+++ b/solution.py
@@ -370,10 +370,10 @@
             jnp.where(first, b0, b1),
             jnp.where(first, b1, b0),
         )
-        out[0, 0:8, cols] = t0
-        out[1, 0:8, cols] = t1
-        out[0, 8:12, cols] = t2[0:4]
-        out[1, 8:12, cols] = t2[4:8]
+        for part, rows, rest in ((0, t0, t2[0:4]), (1, t1, t2[4:8])):
+            for x in range(12):
+                row = rows[x : x + 1] if x < 8 else rest[x - 8 : x - 7]
+                out[x, part : part + 1, cols] = row
         return carry
 
     lax.fori_loop(0, PARTS, block, 0, unroll=UNROLL)
@@ -434,13 +434,15 @@
 
 
 def column_kernel(blocks, coulomb, tables, out):
-    lanes_here = blocks.shape[-1]
-    x = blocks[...].reshape(16 * ROWS, lanes_here)
-    x = dot_split(tables[0:384], tables[384:768], x)
-    k = coulomb[...]
-    x = jnp.concatenate([x[96 * i : 96 * i + 96] * k for i in range(4)], axis=0)
-    x = dot_split(tables[768:1152], tables[1152:1536], x)
-    out[...] = x.reshape(16, ROWS, lanes_here)
+    width = BLOCK // 3
+    for i in range(3):
+        cols = slice(width * i, width * i + width)
+        x = blocks[:, :, cols].reshape(16 * ROWS, width)
+        x = dot_split(tables[0:384], tables[384:768], x)
+        k = coulomb[:, cols]
+        x = jnp.concatenate([x[96 * j : 96 * j + 96] * k for j in range(4)], axis=0)
+        x = dot_split(tables[768:1152], tables[1152:1536], x)
+        out[:, :, cols] = x.reshape(16, ROWS, width)
 
 
 def backward_kernel(
@@ -586,10 +588,10 @@
         h0 = jnp.where(second_half, far, near)
         h1 = jnp.where(second_half, near, far)
         for part in range(2):
-            out[member, part, 0:4, :] = h0[4 * part : 4 * part + 4]
-            out[member, part, 4:8, :] = h1[4 * part : 4 * part + 4]
-            out[member, part, 8:10, :] = h0[8 + 2 * part : 10 + 2 * part]
-            out[member, part, 10:12, :] = h1[8 + 2 * part : 10 + 2 * part]
+            for i in range(12):
+                source = h0 if i in (0, 1, 2, 3, 8, 9) else h1
+                j = i % 4 + 4 * part if i < 8 else 8 + i % 2 + 2 * part
+                out[member, i, part : part + 1, :] = source[j : j + 1]
 
 
 def f32(*shape):
@@ -648,10 +650,10 @@
     )
     blocks = line_exchange(candidate.reshape(8, CHUNK, 128))
     block = lax.dynamic_index_in_dim(blocks, serving // 2 % 8, 0, keepdims=True)
-    block, coulomb = lax.optimization_barrier((block, coulomb))
-    served = line_exchange(jnp.broadcast_to(block, blocks.shape)).reshape(LIST, 128)
     rows = f32(ROWS, PLANE)
     mine, other = call(assemble_kernel, (rows, rows), (keep, recv, keep_other, recv_other))
+    block, coulomb, mine, other = lax.optimization_barrier((block, coulomb, mine, other))
+    served = line_exchange(jnp.broadcast_to(block, blocks.shape)).reshape(LIST, 128)
 
     scratch = [
         pltpu.VMEM((288, 256), jnp.float32),
@@ -664,14 +666,11 @@
     )
     blocks = plane_exchange(blocks.reshape(16, ROWS, BLOCK))
     tables = jnp.asarray(np.concatenate(row_tables()))
-    fixed = pl.BlockSpec((4 * 384, 384), lambda i: (0, 0))
-    piece = pl.BlockSpec((16, ROWS, BLOCK // 3), lambda i: (0, 0, i))
     blocks = pl.pallas_call(
         column_kernel,
         out_shape=f32(16, ROWS, BLOCK),
-        grid=(3,),
-        in_specs=[piece, pl.BlockSpec((NX, BLOCK // 3), lambda i: (0, i)), fixed],
-        out_specs=piece,
+        in_specs=[whole] * 3,
+        out_specs=whole,
         compiler_params=params,
     )(blocks, coulomb, tables)
     blocks = plane_exchange(blocks).reshape(2, PARTS, ROWS, BLOCK)
@@ -685,14 +684,14 @@
     )
     far = swap(own_far + swap(away_far, 1), 16)
     got = swap(away_near, 1)
-    applied = call(applied_kernel, f32(2, 12, PLANE), (own_near, got, far))
+    applied = call(applied_kernel, f32(12, 2, PLANE), (own_near, got, far))
     blocks = line_exchange(terms.reshape(8, CHUNK, 128)).reshape(LIST, 128)
     blocks, applied = lax.optimization_barrier((blocks, applied))
     small = f32(12, HALF)
     pieces = call(finish_kernel, (small,) * 4, (blocks,))
     pieces = [pieces[0], swap(pieces[1], 1), swap(pieces[2], 16), swap(pieces[3], 17)]
-    serving_exchange = call(serving_kernel, f32(SERVE, 2, 12, HALF), pieces)
-    return (applied.reshape(1, 2, 12, PLANE), serving_exchange)
+    serving_exchange = call(serving_kernel, f32(SERVE, 12, 2, HALF), pieces)
+    return (applied.transpose(1, 0, 2)[None], serving_exchange.transpose(0, 2, 1, 3))
 
 
 def solution(mesh):

time: 168 us -> 165 us (0.982)
  blocking collectives: 57.8 us -> 76.5 us
  waiting for transfers between devices: 50.9 us -> 36 us
  local copies, waits for them, and re-layouts: 8.15 us -> 4.15 us
  starting transfers between devices: 26.2 us -> 22.8 us
    all_to_all x0 -> x1, blocking collectives: none -> 18.9 us  [line_exchange(): lax.all_to_all(blocks, 'band', 0, 0, axis_index_groups=z_groups, tiled=True)]
    all_to_all x3 -> x2, waiting for transfers between devices: 31.7 us -> 15.2 us  [line_exchange(): lax.all_to_all(blocks, 'band', 0, 0, axis_index_groups=z_groups, tiled=True)]
    unnamed x23 -> x15, local copies, waits for them, and re-layouts: 6.54 us -> 2.48 us
    all_to_all x3 -> x2, starting transfers between devices: 15.3 us -> 11.8 us  [line_exchange(): lax.all_to_all(blocks, 'band', 0, 0, axis_index_groups=z_groups, tiled=True)]
    pallas_call x7, Pallas kernels: 12.1 us -> 13.9 us  [call(): pl.pallas_call(kernel, out_shape=shapes, in_specs=[scalars] + [whole] * l...]
  transfers between devices with their start and end apart: 12 -> 11, of which waited for: 7 -> 7; matrix products, arithmetic and copies ran while one was open for 3% -> 2% of each run, Pallas kernels for 1% -> 2%
where the time goes in v4:
time: 165 us; the launch traced here: 164 us
  blocking collectives  76.5 us (46%)
  waiting for transfers between devices  36 us (22%)
  starting transfers between devices  22.8 us (14%)
  Pallas kernels  17.8 us (11%)
  local copies, waits for them, and re-layouts  4.15 us (3%)
  other arithmetic  3.67 us (2%)
  between operations  3.52 us (2%)
    all_to_all x2, blocking collectives, plane_exchange(): lax.all_to_all(blocks, ('band', 'fft'), 0, 0, axis_index_groups=plane_gro...  57.6 us
    ppermute x9, waiting for transfers between devices, swap(): return lax.ppermute(x, 'band', [(i, i ^ bits) for i in range(32)])  20.8 us
    all_to_all x1, blocking collectives, line_exchange(): lax.all_to_all(blocks, 'band', 0, 0, axis_index_groups=z_groups, tiled=True)  18.9 us
    all_to_all x2, waiting for transfers between devices, line_exchange(): lax.all_to_all(blocks, 'band', 0, 0, axis_index_groups=z_groups, tiled=True)  15.2 us
    pallas_call x7, Pallas kernels, call(): pl.pallas_call(kernel, out_shape=shapes, in_specs=[scalars] + [whole] * l...  13.9 us
    all_to_all x2, starting transfers between devices, line_exchange(): lax.all_to_all(blocks, 'band', 0, 0, axis_index_groups=z_groups, tiled=True)  11.8 us
    ppermute x9, starting transfers between devices, swap(): return lax.ppermute(x, 'band', [(i, i ^ bits) for i in range(32)])  10.9 us
    pallas_call x1, Pallas kernels, shards(): pl.pallas_call(column_kernel, out_shape=f32(16, ROWS, BLOCK), in_specs=[w...  3.92 us
  transfers between devices with their start and end apart: 11, of which 7 were waited for; matrix products, arithmetic and copies ran while one was open for 2% of the time, Pallas kernels for 2%

profile of v4, /device:TPU:1, one launch (start us, length us, event | category | flops | bytes accessed | tf_op | source)
XLA Modules:
  0.0 164.4 jit_solution(17101711235143631167)
XLA Ops:
  0.6 0.0 copy-start.6
  0.7 1.4 copy.9
  2.2 0.1 pad_add_fusion.place
  2.2 0.7 shard_map.68
  3.0 2.2 %collective-permute-start = (f32[896,128]{1,0:T(8,128)S(1)}, f32[896,128]{1,0:T(8,128)S(1)}, u32[]{:S(2)}, u32[]{:S(2)}) collective-permute-start(f32[896,128]{1,0:T(8,128)S(1)} %get-tuple-element.22), channel_id=1, source_target_pairs={{0,128},{8,136},{16,144},{24,152},{32,160},{40,168},{48,176},{56,1... | collective-permute-start | bytes 1376264 | tf_op jit(solution)/shard_map/ppermute | solution.py:630
  5.2 1.2 collective-permute-start.1
  6.4 7.8 %collective-permute-done.recv = f32[896,128]{1,0:T(8,128)S(1)} collective-permute-done((f32[896,128]{1,0:T(8,128)S(1)}, f32[896,128]{1,0:T(8,128)S(1)}, u32[]{:S(2)}, u32[]{:S(2)}) %collective-permute-start) | collective-permute-done | bytes 458784 | tf_op jit(solution)/shard_map/ppermute | solution.py:630
  14.2 2.5 %collective-permute-start.2 = (f32[896,128]{1,0:T(8,128)S(1)}, f32[896,128]{1,0:T(8,128)S(1)}, u32[]{:S(2)}, u32[]{:S(2)}) collective-permute-start(f32[896,128]{1,0:T(8,128)S(1)} %collective-permute-done.recv), channel_id=1, source_target_pairs={{0,8},{8,0},{16,24},{24,16},{32,40},{40,32},{48,56},{56,48},{64,72... | collective-permute-start | bytes 1376264 | tf_op jit(solution)/shard_map/ppermute | solution.py:630
  16.7 0.0 copy-done.6
  16.7 0.6 dynamic_slice.10
  19.9 0.0 collective-permute-done.1.keep_other
  19.9 0.0 collective-permute-done.2.recv_other
  19.9 0.0 copy-start
  19.9 0.9 select_select_fusion
  20.8 8.3 %all-to-all-start = ((f32[8,112,128]{2,1,0:T(8,128)}), f32[8,112,128]{2,1,0:T(8,128)}, u32[]{:S(2)}, u32[]{:S(2)}) async-start(f32[8,112,128]{2,1,0:T(8,128)} %bitcast.5), calls=%async_computation | async-start | bytes 917504 | tf_op jit(solution)/shard_map/all_to_all | solution.py:633
  29.2 0.1 dynamic-slice_multiply_fusion
  29.3 0.1 broadcast_in_dim.28
  29.3 0.1 integer_pow.34
  29.4 0.1 integer_pow.35
  29.5 0.0 copy-done
  29.5 2.5 %fusion.coulomb = f32[96,1152]{1,0:T(8,128)} fusion(f32[1152]{0:T(1024)S(1)} %integer_pow.35, f32[1152]{0:T(1024)S(1)} %integer_pow.34, f32[96]{0:T(128)S(1)} %fusion.4), kind=kLoop, calls=%fused_computation.4 | loop fusion | flops 1105920 | bytes 451968 | tf_op jit(solution)/shard_map/mul | solution.py:614
  32.1 0.0 copy-start.1
  32.1 1.0 copy-done.1
  33.1 0.0 copy-start.5
  33.1 0.8 shard_map.69
  33.9 12.0 %all-to-all-done = f32[8,112,128]{2,1,0:T(8,128)} async-done(((f32[8,112,128]{2,1,0:T(8,128)}), f32[8,112,128]{2,1,0:T(8,128)}, u32[]{:S(2)}, u32[]{:S(2)}) %all-to-all-start) | async-done | bytes 458784 | tf_op jit(solution)/shard_map/all_to_all | solution.py:633
  45.9 0.8 constant_dynamic-slice_fusion
  46.8 18.9 %all_to_all.25 = f32[8,112,128]{2,1,0:T(8,128)S(1)} all-to-all(f32[8,112,128]{2,1,0:T(8,128)S(1)} %broadcast_in_dim.32), channel_id=1, replica_groups={{0,16,32,48,64,80,96,112},{8,24,40,56,72,88,104,120},{128,144,160,176,1..., dimensions={0} | all-to-all | bytes 917504 | tf_op jit(solution)/shard_map/all_to_all | solution.py:633
  65.6 0.0 copy-done.5
  65.6 2.9 %shard_map.70 = f32[2,8,24,1152]{3,2,1,0:T(8,128)S(1)} custom-call(s32[3]{0:T(128)S(1)} %pad_add_fusion.place, f32[896,128]{1,0:T(8,128)S(1)} %bitcast.20, f32[24,9216]{1,0:T(8,128)S(1)} %get-tuple-element.26.mine, f32[24,9216]{1,0:T(8,128)S(1)} %get-tuple-element.27.other, bf16[512,256]{1,0:T(8,128)(2,1)S(1)} %copy-done.5), custom_call_target="tpu_custom_call" | custom-call | tf_op jit(solution)/shard_map/pallas_call | solution.py:620
  68.6 0.0 copy-start.2
  68.6 0.0 copy-start.3
  68.6 30.8 %all_to_all.26.blocks = f32[16,24,1152]{2,1,0:T(8,128)S(1)} all-to-all(f32[16,24,1152]{2,1,0:T(8,128)S(1)} %bitcast.18), channel_id=1, replica_groups={{0,1,2,3,4,5,6,7,128,129,130,131,132,133,134,135},{8,9,10,11,12,13,14,1..., dimensions={0} | all-to-all | bytes 3538944 | tf_op jit(solution)/shard_map/all_to_all | solution.py:636
  99.4 0.0 copy-done.2
  99.4 0.0 copy-done.3
  99.4 3.9 %shard_map.71 = f32[16,24,1152]{2,1,0:T(8,128)S(1)} custom-call(f32[16,24,1152]{2,1,0:T(8,128)S(1)} %all_to_all.26.blocks, f32[96,1152]{1,0:T(8,128)S(1)} %copy-done.2, bf16[1536,384]{1,0:T(8,128)(2,1)S(1)} %copy-done.3), custom_call_target="tpu_custom_call" | custom-call | tf_op jit(solution)/shard_map/pallas_call | solution.py:669
  103.3 0.0 copy-start.4
  103.3 26.8 %all_to_all.27 = f32[16,24,1152]{2,1,0:T(8,128)} all-to-all(f32[16,24,1152]{2,1,0:T(8,128)S(1)} %shard_map.71), channel_id=1, replica_groups={{0,1,2,3,4,5,6,7,128,129,130,131,132,133,134,135},{8,9,10,11,12,13,14,1..., dimensions={0} | all-to-all | bytes 3538944 | tf_op jit(solution)/shard_map/all_to_all | solution.py:636
  130.1 0.0 copy-done.4
  130.2 5.6 %shard_map.72 = (f32[864,128]{1,0:T(8,128)S(1)}, f32[864,128]{1,0:T(8,128)S(1)}, f32[864,128]{1,0:T(8,128)S(1)}, f32[864,128]{1,0:T(8,128)}, f32[896,128]{1,0:T(8,128)}) custom-call(s32[3]{0:T(128)S(1)} %pad_add_fusion.place, f32[2,8,24,1152]{3,2,1,0:T(8,128)} %bitcast.23, f32[896,128]{1,0:T(8,128)S(1)} %bitcast.21, f32[24,9216]{1,0:T(8,128)S(1)} %get-tuple-element.26.mine, ...), custom_call_target="tpu_custom_call" | custom-call | tf_op jit(solution)/shard_map/pallas_call | solution.py:620
  135.8 2.6 %collective-permute-start.4 = (f32[864,128]{1,0:T(8,128)}, f32[864,128]{1,0:T(8,128)S(1)}, u32[]{:S(2)}, u32[]{:S(2)}) collective-permute-start(f32[864,128]{1,0:T(8,128)} %get-tuple-element.33), channel_id=1, source_target_pairs={{0,8},{8,0},{16,24},{24,16},{32,40},{40,32},{48,56},{56,48},{64,72... | collective-permute-start | bytes 1327112 | tf_op jit(solution)/shard_map/ppermute | solution.py:630
  138.4 3.5 %all-to-all-start.4 = ((f32[8,112,128]{2,1,0:T(8,128)}), f32[8,112,128]{2,1,0:T(8,128)S(1)}, u32[]{:S(2)}, u32[]{:S(2)}) async-start(f32[8,112,128]{2,1,0:T(8,128)} %bitcast.10), calls=%async_computation.4 | async-start | bytes 917504 | tf_op jit(solution)/shard_map/all_to_all | solution.py:633
  141.9 0.1 collective-permute-start.3
  142.0 0.0 collective-permute-done.4
  142.0 0.1 collective-permute-start.5
  142.1 1.6 collective-permute-done.3.got
  143.7 9.6 %collective-permute-done.5.far = f32[864,128]{1,0:T(8,128)S(1)} collective-permute-done((f32[864,128]{1,0:T(8,128)S(1)}, f32[864,128]{1,0:T(8,128)S(1)}, u32[]{:S(2)}, u32[]{:S(2)}) %collective-permute-start.5) | collective-permute-done | bytes 442400 | tf_op jit(solution)/shard_map/ppermute | solution.py:630
  153.4 1.8 %shard_map.73 = f32[12,2,9216]{2,1,0:T(2,128)} custom-call(s32[3]{0:T(128)S(1)} %pad_add_fusion.place, f32[864,128]{1,0:T(8,128)S(1)} %get-tuple-element.30.near, f32[864,128]{1,0:T(8,128)S(1)} %collective-permute-done.3.got, f32[864,128]{1,0:T(8,128)S(1)} %collective-permute-done.5.far), custom_call_target="tpu_custom_call" | custom-call | tf_op jit(solution)/shard_map/pallas_call | solution.py:620
  155.2 3.2 %all-to-all-done.4 = f32[8,112,128]{2,1,0:T(8,128)S(1)} async-done(((f32[8,112,128]{2,1,0:T(8,128)}), f32[8,112,128]{2,1,0:T(8,128)S(1)}, u32[]{:S(2)}, u32[]{:S(2)}) %all-to-all-start.4) | async-done | bytes 458784 | tf_op jit(solution)/shard_map/all_to_all | solution.py:633
  158.4 0.7 shard_map.74
  159.1 0.5 collective-permute-start.6
  159.7 0.0 collective-permute-start.7
  159.7 1.7 %collective-permute-start.8 = (f32[12,288]{1,0:T(8,128)S(1)}, f32[12,288]{1,0:T(8,128)S(1)}, u32[]{:S(2)}, u32[]{:S(2)}) collective-permute-start(f32[12,288]{1,0:T(8,128)S(1)} %get-tuple-element.39), channel_id=1, source_target_pairs={{0,136},{8,128},{16,152},{24,144},{32,168},{40,160},{48,184},{56,1... | collective-permute-start | bytes 41480 | tf_op jit(solution)/shard_map/ppermute | solution.py:630
  161.4 0.0 collective-permute-done.6.p01
  161.4 1.0 collective-permute-done.7.p10
  162.4 0.8 collective-permute-done.8.p11
  163.2 1.2 shard_map.75
  (5 shorter events, 0.1 us)
Async XLA Ops:
  0.6 16.0 %copy-start.6 = (s32[32]{0:T(128)S(1)}, s32[32]{0:T(128)}, u32[]{:S(2)}) copy-start(s32[32]{0:T(128)} %param.6) | copy-start | bytes 388
  3.0 11.2 %collective-permute-start = (f32[896,128]{1,0:T(8,128)S(1)}, f32[896,128]{1,0:T(8,128)S(1)}, u32[]{:S(2)}, u32[]{:S(2)}) collective-permute-start(f32[896,128]{1,0:T(8,128)S(1)} %get-tuple-element.22), channel_id=1, source_target_pairs={{0,128},{8,136},{16,144},{24,152},{32,160},{40,168},{48,176},{56,1... | collective-permute-start | bytes 1376264 | tf_op jit(solution)/shard_map/ppermute | solution.py:630
  5.2 14.7 %collective-permute-start.1 = (f32[896,128]{1,0:T(8,128)S(1)}, f32[896,128]{1,0:T(8,128)S(1)}, u32[]{:S(2)}, u32[]{:S(2)}) collective-permute-start(f32[896,128]{1,0:T(8,128)S(1)} %get-tuple-element.21.keep), channel_id=1, source_target_pairs={{0,8},{8,0},{16,24},{24,16},{32,40},{40,32},{48,56},{56,48},{64,72... | collective-permute-start | bytes 1376264 | tf_op jit(solution)/shard_map/ppermute | solution.py:630
  14.2 5.7 %collective-permute-start.2 = (f32[896,128]{1,0:T(8,128)S(1)}, f32[896,128]{1,0:T(8,128)S(1)}, u32[]{:S(2)}, u32[]{:S(2)}) collective-permute-start(f32[896,128]{1,0:T(8,128)S(1)} %collective-permute-done.recv), channel_id=1, source_target_pairs={{0,8},{8,0},{16,24},{24,16},{32,40},{40,32},{48,56},{56,48},{64,72... | collective-permute-start | bytes 1376264 | tf_op jit(solution)/shard_map/ppermute | solution.py:630
  19.9 9.6 %copy-start = (f32[896,128]{1,0:T(8,128)}, f32[896,128]{1,0:T(8,128)S(1)}, u32[]{:S(2)}) copy-start(f32[896,128]{1,0:T(8,128)S(1)} %collective-permute-done.2.recv_other) | copy-start | bytes 1376260
  20.8 25.1 %all-to-all-start = ((f32[8,112,128]{2,1,0:T(8,128)}), f32[8,112,128]{2,1,0:T(8,128)}, u32[]{:S(2)}, u32[]{:S(2)}) async-start(f32[8,112,128]{2,1,0:T(8,128)} %bitcast.5), calls=%async_computation | async-start | bytes 917504 | tf_op jit(solution)/shard_map/all_to_all | solution.py:633
  32.1 1.0 copy-start.1
  33.1 32.6 %copy-start.5 = (bf16[512,256]{1,0:T(8,128)(2,1)S(1)}, bf16[512,256]{1,0:T(8,128)(2,1)}, u32[]{:S(2)}) copy-start(bf16[512,256]{1,0:T(8,128)(2,1)} %constant.131.clone.table) | copy-start | bytes 786436
  68.6 30.8 %copy-start.2 = (f32[96,1152]{1,0:T(8,128)S(1)}, f32[96,1152]{1,0:T(8,128)}, u32[]{:S(2)}) copy-start(f32[96,1152]{1,0:T(8,128)} %fusion.coulomb) | copy-start | bytes 1327108
  68.6 30.8 %copy-start.3 = (bf16[1536,384]{1,0:T(8,128)(2,1)S(1)}, bf16[1536,384]{1,0:T(8,128)(2,1)}, u32[]{:S(2)}) copy-start(bf16[1536,384]{1,0:T(8,128)(2,1)} %constant.132.clone.tables) | copy-start | bytes 3538948
  103.3 26.8 %copy-start.4 = (bf16[512,256]{1,0:T(8,128)(2,1)S(1)}, bf16[512,256]{1,0:T(8,128)(2,1)}, u32[]{:S(2)}) copy-start(bf16[512,256]{1,0:T(8,128)(2,1)} %constant.133.clone.table) | copy-start | bytes 786436
  135.8 6.2 %collective-permute-start.4 = (f32[864,128]{1,0:T(8,128)}, f32[864,128]{1,0:T(8,128)S(1)}, u32[]{:S(2)}, u32[]{:S(2)}) collective-permute-start(f32[864,128]{1,0:T(8,128)} %get-tuple-element.33), channel_id=1, source_target_pairs={{0,8},{8,0},{16,24},{24,16},{32,40},{40,32},{48,56},{56,48},{64,72... | collective-permute-start | bytes 1327112 | tf_op jit(solution)/shard_map/ppermute | solution.py:630
  138.4 20.0 %all-to-all-start.4 = ((f32[8,112,128]{2,1,0:T(8,128)}), f32[8,112,128]{2,1,0:T(8,128)S(1)}, u32[]{:S(2)}, u32[]{:S(2)}) async-start(f32[8,112,128]{2,1,0:T(8,128)} %bitcast.10), calls=%async_computation.4 | async-start | bytes 917504 | tf_op jit(solution)/shard_map/all_to_all | solution.py:633
  141.9 1.9 %collective-permute-start.3 = (f32[864,128]{1,0:T(8,128)S(1)}, f32[864,128]{1,0:T(8,128)S(1)}, u32[]{:S(2)}, u32[]{:S(2)}) collective-permute-start(f32[864,128]{1,0:T(8,128)S(1)} %get-tuple-element.31), channel_id=1, source_target_pairs={{0,8},{8,0},{16,24},{24,16},{32,40},{40,32},{48,56},{56,48},{64,72... | collective-permute-start | bytes 1327112 | tf_op jit(solution)/shard_map/ppermute | solution.py:630
  142.0 11.3 %collective-permute-start.5 = (f32[864,128]{1,0:T(8,128)S(1)}, f32[864,128]{1,0:T(8,128)S(1)}, u32[]{:S(2)}, u32[]{:S(2)}) collective-permute-start(f32[864,128]{1,0:T(8,128)S(1)} %add.117), channel_id=1, source_target_pairs={{0,128},{8,136},{16,144},{24,152},{32,160},{40,168},{48,176},{56,1... | collective-permute-start | bytes 1327112 | tf_op jit(solution)/shard_map/ppermute | solution.py:630
  159.1 2.3 %collective-permute-start.6 = (f32[12,288]{1,0:T(8,128)S(1)}, f32[12,288]{1,0:T(8,128)S(1)}, u32[]{:S(2)}, u32[]{:S(2)}) collective-permute-start(f32[12,288]{1,0:T(8,128)S(1)} %get-tuple-element.37), channel_id=1, source_target_pairs={{0,8},{8,0},{16,24},{24,16},{32,40},{40,32},{48,56},{56,48},{64,72... | collective-permute-start | bytes 41480 | tf_op jit(solution)/shard_map/ppermute | solution.py:630
  159.7 2.7 %collective-permute-start.7 = (f32[12,288]{1,0:T(8,128)S(1)}, f32[12,288]{1,0:T(8,128)S(1)}, u32[]{:S(2)}, u32[]{:S(2)}) collective-permute-start(f32[12,288]{1,0:T(8,128)S(1)} %get-tuple-element.38), channel_id=1, source_target_pairs={{0,128},{8,136},{16,144},{24,152},{32,160},{40,168},{48,176},{56,1... | collective-permute-start | bytes 41480 | tf_op jit(solution)/shard_map/ppermute | solution.py:630
  159.7 3.5 %collective-permute-start.8 = (f32[12,288]{1,0:T(8,128)S(1)}, f32[12,288]{1,0:T(8,128)S(1)}, u32[]{:S(2)}, u32[]{:S(2)}) collective-permute-start(f32[12,288]{1,0:T(8,128)S(1)} %get-tuple-element.39), channel_id=1, source_target_pairs={{0,136},{8,128},{16,152},{24,144},{32,168},{40,160},{48,184},{56,1... | collective-permute-start | bytes 41480 | tf_op jit(solution)/shard_map/ppermute | solution.py:630

commit v5 on v4

--- a/solution.py
+++ b/solution.py
@@ -335,26 +335,6 @@
         ref[TILES:LIST, :] = jnp.zeros((LIST - TILES, 128), jnp.float32)
 
 
-def assemble_kernel(place, keep, recv, keep_other, recv_other, mine, other):
-    first = place[2] == 0
-
-    def block(g, carry):
-        cols = block_columns(g)
-        for own, far, out in ((keep, recv, mine), (keep_other, recv_other, other)):
-            (a0, b0), (a1, b1) = half_load(own, g), half_load(far, g)
-            rows = combine(
-                jnp.where(first, a0, a1),
-                jnp.where(first, a1, a0),
-                jnp.where(first, b0, b1),
-                jnp.where(first, b1, b0),
-            )
-            for r in range(3):
-                out[8 * r : 8 * r + 8, cols] = rows[r]
-        return carry
-
-    lax.fori_loop(0, PARTS, block, 0, unroll=UNROLL)
-
-
 def applied_kernel(place, near, got, far, out):
     first = place[2] == 0
 
@@ -384,13 +364,26 @@
     return combine(a, a, b, b)
 
 
-def forward_kernel(place, served, mine, other, table, out, line, field, spectrum):
+def forward_kernel(
+    place, served, keep, recv, keep_other, recv_other, table, out, mine, other, line, field, spectrum
+):
+    first = place[2] == 0
+
     def block(g, carry):
         s0, s1, s2 = served_rows(served, g)
         parts = []
         rests = []
-        for ref in (mine, other):
-            re, im, rest = orbital_rows(ref, g)
+        cols = block_columns(g)
+        for own, far, ref in ((keep, recv, mine), (keep_other, recv_other, other)):
+            (a0, b0), (a1, b1) = half_load(own, g), half_load(far, g)
+            re, im, rest = combine(
+                jnp.where(first, a0, a1),
+                jnp.where(first, a1, a0),
+                jnp.where(first, b0, b1),
+                jnp.where(first, b1, b0),
+            )
+            for r, rows in enumerate((re, im, rest)):
+                ref[8 * r : 8 * r + 8, cols] = rows
             parts.append((s0 * re + s1 * im, s0 * im - s1 * re))
             same = s2 * rest
             cross = s2 * flip(rest)
@@ -639,7 +632,7 @@
 
     lists = f32(LIST, 128)
     keep, send = call(halves_kernel, (lists, lists), (orbitals.reshape(2, 12, PLANE),))
-    recv = swap(send, 16)
+    recv, coulomb = lax.optimization_barrier((swap(send, 16), coulomb))
     keep_other = swap(keep, 1)
     recv_other = swap(recv, 1)
     serving = serve_order[core]
@@ -650,9 +643,6 @@
     )
     blocks = line_exchange(candidate.reshape(8, CHUNK, 128))
     block = lax.dynamic_index_in_dim(blocks, serving // 2 % 8, 0, keepdims=True)
-    rows = f32(ROWS, PLANE)
-    mine, other = call(assemble_kernel, (rows, rows), (keep, recv, keep_other, recv_other))
-    block, coulomb, mine, other = lax.optimization_barrier((block, coulomb, mine, other))
     served = line_exchange(jnp.broadcast_to(block, blocks.shape)).reshape(LIST, 128)
 
     scratch = [
@@ -661,8 +651,12 @@
         pltpu.VMEM((NY, ROWS, 256), jnp.float32),
     ]
     table = jnp.asarray(np.concatenate(lane_table(-1.0)))
-    blocks = call(
-        forward_kernel, f32(2, PARTS, ROWS, BLOCK), (served, mine, other, table), scratch
+    rows = f32(ROWS, PLANE)
+    blocks, mine, other = call(
+        forward_kernel,
+        (f32(2, PARTS, ROWS, BLOCK), rows, rows),
+        (served, keep, recv, keep_other, recv_other, table),
+        scratch,
     )
     blocks = plane_exchange(blocks.reshape(16, ROWS, BLOCK))
     tables = jnp.asarray(np.concatenate(row_tables()))

time: 165 us -> 164 us (level)
  waiting for transfers between devices: 36 us -> 38.6 us
  local copies, waits for them, and re-layouts: 4.15 us -> 2.31 us
    all_to_all x2, waiting for transfers between devices: 15.2 us -> 19.9 us  [line_exchange(): lax.all_to_all(blocks, 'band', 0, 0, axis_index_groups=z_groups, tiled=True)]
    ppermute x9, waiting for transfers between devices: 20.8 us -> 18.7 us  [swap(): return lax.ppermute(x, 'band', [(i, i ^ bits) for i in range(32)])]
    pallas_call x7 -> x6, Pallas kernels: 13.9 us -> 13 us  [call(): pl.pallas_call(kernel, out_shape=shapes, in_specs=[scalars] + [whole] * l...]
  transfers between devices with their start and end apart: 11 -> 11, of which waited for: 7 -> 7; matrix products, arithmetic and copies ran while one was open for 2% -> 2% of each run, Pallas kernels for 2% -> 1%
where the time goes in v5:
time: 164 us
  blocking collectives  76.5 us (47%)
  waiting for transfers between devices  38.6 us (24%)
  starting transfers between devices  22.9 us (14%)
  Pallas kernels  17 us (10%)
  between operations  3.47 us (2%)
  other arithmetic  2.83 us (2%)
  local copies, waits for them, and re-layouts  2.31 us (1%)
    all_to_all x2, blocking collectives, plane_exchange(): lax.all_to_all(blocks, ('band', 'fft'), 0, 0, axis_index_groups=plane_gro...  57.6 us
    all_to_all x2, waiting for transfers between devices, line_exchange(): lax.all_to_all(blocks, 'band', 0, 0, axis_index_groups=z_groups, tiled=True)  19.9 us
    all_to_all x1, blocking collectives, line_exchange(): lax.all_to_all(blocks, 'band', 0, 0, axis_index_groups=z_groups, tiled=True)  18.9 us
    ppermute x9, waiting for transfers between devices, swap(): return lax.ppermute(x, 'band', [(i, i ^ bits) for i in range(32)])  18.7 us
    pallas_call x6, Pallas kernels, call(): pl.pallas_call(kernel, out_shape=shapes, in_specs=[scalars] + [whole] * l...  13 us
    all_to_all x2, starting transfers between devices, line_exchange(): lax.all_to_all(blocks, 'band', 0, 0, axis_index_groups=z_groups, tiled=True)  12 us
    ppermute x9, starting transfers between devices, swap(): return lax.ppermute(x, 'band', [(i, i ^ bits) for i in range(32)])  10.9 us
    pallas_call x1, Pallas kernels, shards(): pl.pallas_call(column_kernel, out_shape=f32(16, ROWS, BLOCK), in_specs=[w...  3.97 us
  transfers between devices with their start and end apart: 11, of which 7 were waited for; matrix products, arithmetic and copies ran while one was open for 2% of the time, Pallas kernels for 1%

profile of v5, /device:TPU:1, one launch (start us, length us, event | category | flops | bytes accessed | tf_op | source)
XLA Modules:
  0.0 163.6 jit_solution(16489238072010404608)
XLA Ops:
  0.7 0.0 copy-start.3
  0.7 1.4 copy.9
  2.2 0.1 pad_add_fusion.place
  2.2 0.7 shard_map.68
  3.0 2.2 %collective-permute-start = (f32[896,128]{1,0:T(8,128)S(1)}, f32[896,128]{1,0:T(8,128)S(1)}, u32[]{:S(2)}, u32[]{:S(2)}) collective-permute-start(f32[896,128]{1,0:T(8,128)S(1)} %get-tuple-element.21), channel_id=1, source_target_pairs={{0,128},{8,136},{16,144},{24,152},{32,160},{40,168},{48,176},{56,1... | collective-permute-start | bytes 1376264 | tf_op jit(solution)/shard_map/ppermute | solution.py:623
  5.2 1.2 collective-permute-start.1
  6.4 0.1 dynamic-slice_multiply_fusion
  6.5 0.1 broadcast_in_dim.28
  6.6 0.1 integer_pow.34
  6.7 0.1 integer_pow.35
  6.7 1.7 %fusion.coulomb = f32[96,1152]{1,0:T(8,128)S(1)} fusion(f32[1152]{0:T(1024)S(1)} %integer_pow.35, f32[1152]{0:T(1024)S(1)} %integer_pow.34, f32[96]{0:T(128)S(1)} %fusion.4), kind=kLoop, calls=%fused_computation.4 | loop fusion | flops 1105920 | bytes 451968 | tf_op jit(solution)/shard_map/mul | solution.py:607
  8.5 5.7 %collective-permute-done.recv = f32[896,128]{1,0:T(8,128)S(1)} collective-permute-done((f32[896,128]{1,0:T(8,128)S(1)}, f32[896,128]{1,0:T(8,128)S(1)}, u32[]{:S(2)}, u32[]{:S(2)}) %collective-permute-start) | collective-permute-done | bytes 458784 | tf_op jit(solution)/shard_map/ppermute | solution.py:623
  14.2 2.5 %collective-permute-start.2 = (f32[896,128]{1,0:T(8,128)S(1)}, f32[896,128]{1,0:T(8,128)S(1)}, u32[]{:S(2)}, u32[]{:S(2)}) collective-permute-start(f32[896,128]{1,0:T(8,128)S(1)} %collective-permute-done.recv), channel_id=1, source_target_pairs={{0,8},{8,0},{16,24},{24,16},{32,40},{40,32},{48,56},{56,48},{64,72... | collective-permute-start | bytes 1376264 | tf_op jit(solution)/shard_map/ppermute | solution.py:623
  16.7 0.0 copy-done.3
  16.7 0.6 dynamic_slice.10
  19.9 0.0 collective-permute-done.1.keep_other
  19.9 0.0 collective-permute-done.2.recv_other
  19.9 0.9 select_select_fusion
  20.7 0.0 copy-start.2
  20.7 8.5 %all-to-all-start = ((f32[8,112,128]{2,1,0:T(8,128)}), f32[8,112,128]{2,1,0:T(8,128)S(1)}, u32[]{:S(2)}, u32[]{:S(2)}) async-start(f32[8,112,128]{2,1,0:T(8,128)} %bitcast.5), calls=%async_computation | async-start | bytes 917504 | tf_op jit(solution)/shard_map/all_to_all | solution.py:626
  29.2 16.6 %all-to-all-done = f32[8,112,128]{2,1,0:T(8,128)S(1)} async-done(((f32[8,112,128]{2,1,0:T(8,128)}), f32[8,112,128]{2,1,0:T(8,128)S(1)}, u32[]{:S(2)}, u32[]{:S(2)}) %all-to-all-start) | async-done | bytes 458784 | tf_op jit(solution)/shard_map/all_to_all | solution.py:626
  45.9 18.9 %all_to_all.25 = f32[8,112,128]{2,1,0:T(8,128)S(1)} all-to-all(f32[8,112,128]{2,1,0:T(8,128)S(1)} %broadcast_in_dim.32), channel_id=1, replica_groups={{0,16,32,48,64,80,96,112},{8,24,40,56,72,88,104,120},{128,144,160,176,1..., dimensions={0} | all-to-all | bytes 917504 | tf_op jit(solution)/shard_map/all_to_all | solution.py:626
  64.8 0.0 copy-done.2
  64.8 3.1 %shard_map.69 = (f32[2,8,24,1152]{3,2,1,0:T(8,128)S(1)}, f32[24,9216]{1,0:T(8,128)S(1)}, f32[24,9216]{1,0:T(8,128)S(1)}) custom-call(s32[3]{0:T(128)S(1)} %pad_add_fusion.place, f32[896,128]{1,0:T(8,128)S(1)} %bitcast.20, f32[896,128]{1,0:T(8,128)S(1)} %get-tuple-element.20.keep, f32[896,128]{1,0:T(8,128)S(1)} %collective-permute-done.recv, ...), custom_call_target="tpu_custom_call" | custom-call | tf_op jit(solution)/shard_map/pallas_call | solution.py:613
  67.8 0.0 copy-start
  67.8 30.8 %all_to_all.26.blocks = f32[16,24,1152]{2,1,0:T(8,128)S(1)} all-to-all(f32[16,24,1152]{2,1,0:T(8,128)S(1)} %bitcast.23), channel_id=1, replica_groups={{0,1,2,3,4,5,6,7,128,129,130,131,132,133,134,135},{8,9,10,11,12,13,14,1..., dimensions={0} | all-to-all | bytes 3538944 | tf_op jit(solution)/shard_map/all_to_all | solution.py:629
  98.6 0.0 copy-done
  98.6 4.0 %shard_map.70 = f32[16,24,1152]{2,1,0:T(8,128)S(1)} custom-call(f32[16,24,1152]{2,1,0:T(8,128)S(1)} %all_to_all.26.blocks, f32[96,1152]{1,0:T(8,128)S(1)} %fusion.coulomb, bf16[1536,384]{1,0:T(8,128)(2,1)S(1)} %copy-done), custom_call_target="tpu_custom_call" | custom-call | tf_op jit(solution)/shard_map/pallas_call | solution.py:663
  102.6 0.0 copy-start.1
  102.6 26.8 %all_to_all.27 = f32[16,24,1152]{2,1,0:T(8,128)} all-to-all(f32[16,24,1152]{2,1,0:T(8,128)S(1)} %shard_map.70), channel_id=1, replica_groups={{0,1,2,3,4,5,6,7,128,129,130,131,132,133,134,135},{8,9,10,11,12,13,14,1..., dimensions={0} | all-to-all | bytes 3538944 | tf_op jit(solution)/shard_map/all_to_all | solution.py:629
  129.5 0.0 copy-done.1
  129.5 5.5 %shard_map.71 = (f32[864,128]{1,0:T(8,128)S(1)}, f32[864,128]{1,0:T(8,128)S(1)}, f32[864,128]{1,0:T(8,128)S(1)}, f32[864,128]{1,0:T(8,128)S(1)}, f32[896,128]{1,0:T(8,128)}) custom-call(s32[3]{0:T(128)S(1)} %pad_add_fusion.place, f32[2,8,24,1152]{3,2,1,0:T(8,128)} %bitcast.24, f32[896,128]{1,0:T(8,128)S(1)} %bitcast.21, ...), custom_call_target="tpu_custom_call" | custom-call | tf_op jit(solution)/shard_map/pallas_call | solution.py:613
  135.0 2.6 %collective-permute-start.4 = (f32[864,128]{1,0:T(8,128)S(1)}, f32[864,128]{1,0:T(8,128)S(1)}, u32[]{:S(2)}, u32[]{:S(2)}) collective-permute-start(f32[864,128]{1,0:T(8,128)S(1)} %get-tuple-element.31), channel_id=1, source_target_pairs={{0,8},{8,0},{16,24},{24,16},{32,40},{40,32},{48,56},{56,48},{64,72... | collective-permute-start | bytes 1327112 | tf_op jit(solution)/shard_map/ppermute | solution.py:623
  137.6 3.5 %all-to-all-start.4 = ((f32[8,112,128]{2,1,0:T(8,128)}), f32[8,112,128]{2,1,0:T(8,128)S(1)}, u32[]{:S(2)}, u32[]{:S(2)}) async-start(f32[8,112,128]{2,1,0:T(8,128)} %bitcast.10), calls=%async_computation.4 | async-start | bytes 917504 | tf_op jit(solution)/shard_map/all_to_all | solution.py:626
  141.0 0.1 collective-permute-start.3
  141.1 0.0 collective-permute-done.4
  141.1 0.1 add.117
  141.2 0.1 collective-permute-start.5
  141.3 1.6 collective-permute-done.3.got
  142.9 9.6 %collective-permute-done.5.far = f32[864,128]{1,0:T(8,128)S(1)} collective-permute-done((f32[864,128]{1,0:T(8,128)S(1)}, f32[864,128]{1,0:T(8,128)S(1)}, u32[]{:S(2)}, u32[]{:S(2)}) %collective-permute-start.5) | collective-permute-done | bytes 442400 | tf_op jit(solution)/shard_map/ppermute | solution.py:623
  152.6 1.8 %shard_map.72 = f32[12,2,9216]{2,1,0:T(2,128)} custom-call(s32[3]{0:T(128)S(1)} %pad_add_fusion.place, f32[864,128]{1,0:T(8,128)S(1)} %get-tuple-element.28.near, f32[864,128]{1,0:T(8,128)S(1)} %collective-permute-done.3.got, f32[864,128]{1,0:T(8,128)S(1)} %collective-permute-done.5.far), custom_call_target="tpu_custom_call" | custom-call | tf_op jit(solution)/shard_map/pallas_call | solution.py:613
  154.4 3.2 %all-to-all-done.4 = f32[8,112,128]{2,1,0:T(8,128)S(1)} async-done(((f32[8,112,128]{2,1,0:T(8,128)}), f32[8,112,128]{2,1,0:T(8,128)S(1)}, u32[]{:S(2)}, u32[]{:S(2)}) %all-to-all-start.4) | async-done | bytes 458784 | tf_op jit(solution)/shard_map/all_to_all | solution.py:626
  157.6 0.7 shard_map.73
  158.3 0.5 collective-permute-start.6
  158.8 0.0 collective-permute-start.7
  158.8 1.7 %collective-permute-start.8 = (f32[12,288]{1,0:T(8,128)S(1)}, f32[12,288]{1,0:T(8,128)S(1)}, u32[]{:S(2)}, u32[]{:S(2)}) collective-permute-start(f32[12,288]{1,0:T(8,128)S(1)} %get-tuple-element.37), channel_id=1, source_target_pairs={{0,136},{8,128},{16,152},{24,144},{32,168},{40,160},{48,184},{56,1... | collective-permute-start | bytes 41480 | tf_op jit(solution)/shard_map/ppermute | solution.py:623
  160.6 0.0 collective-permute-done.6.p01
  160.6 1.0 collective-permute-done.7.p10
  161.5 0.8 collective-permute-done.8.p11
  162.4 1.2 shard_map.74
  (5 shorter events, 0.1 us)
Async XLA Ops:
  0.7 16.0 %copy-start.3 = (s32[32]{0:T(128)S(1)}, s32[32]{0:T(128)}, u32[]{:S(2)}) copy-start(s32[32]{0:T(128)} %param.6) | copy-start | bytes 388
  3.0 11.2 %collective-permute-start = (f32[896,128]{1,0:T(8,128)S(1)}, f32[896,128]{1,0:T(8,128)S(1)}, u32[]{:S(2)}, u32[]{:S(2)}) collective-permute-start(f32[896,128]{1,0:T(8,128)S(1)} %get-tuple-element.21), channel_id=1, source_target_pairs={{0,128},{8,136},{16,144},{24,152},{32,160},{40,168},{48,176},{56,1... | collective-permute-start | bytes 1376264 | tf_op jit(solution)/shard_map/ppermute | solution.py:623
  5.2 14.7 %collective-permute-start.1 = (f32[896,128]{1,0:T(8,128)S(1)}, f32[896,128]{1,0:T(8,128)S(1)}, u32[]{:S(2)}, u32[]{:S(2)}) collective-permute-start(f32[896,128]{1,0:T(8,128)S(1)} %get-tuple-element.20.keep), channel_id=1, source_target_pairs={{0,8},{8,0},{16,24},{24,16},{32,40},{40,32},{48,56},{56,48},{64,72... | collective-permute-start | bytes 1376264 | tf_op jit(solution)/shard_map/ppermute | solution.py:623
  14.2 5.7 %collective-permute-start.2 = (f32[896,128]{1,0:T(8,128)S(1)}, f32[896,128]{1,0:T(8,128)S(1)}, u32[]{:S(2)}, u32[]{:S(2)}) collective-permute-start(f32[896,128]{1,0:T(8,128)S(1)} %collective-permute-done.recv), channel_id=1, source_target_pairs={{0,8},{8,0},{16,24},{24,16},{32,40},{40,32},{48,56},{56,48},{64,72... | collective-permute-start | bytes 1376264 | tf_op jit(solution)/shard_map/ppermute | solution.py:623
  20.7 44.0 %copy-start.2 = (bf16[512,256]{1,0:T(8,128)(2,1)S(1)}, bf16[512,256]{1,0:T(8,128)(2,1)}, u32[]{:S(2)}) copy-start(bf16[512,256]{1,0:T(8,128)(2,1)} %constant.131.clone.table) | copy-start | bytes 786436
  20.7 25.1 %all-to-all-start = ((f32[8,112,128]{2,1,0:T(8,128)}), f32[8,112,128]{2,1,0:T(8,128)S(1)}, u32[]{:S(2)}, u32[]{:S(2)}) async-start(f32[8,112,128]{2,1,0:T(8,128)} %bitcast.5), calls=%async_computation | async-start | bytes 917504 | tf_op jit(solution)/shard_map/all_to_all | solution.py:626
  67.8 30.8 %copy-start = (bf16[1536,384]{1,0:T(8,128)(2,1)S(1)}, bf16[1536,384]{1,0:T(8,128)(2,1)}, u32[]{:S(2)}) copy-start(bf16[1536,384]{1,0:T(8,128)(2,1)} %constant.132.clone.tables) | copy-start | bytes 3538948
  102.6 26.8 %copy-start.1 = (bf16[512,256]{1,0:T(8,128)(2,1)S(1)}, bf16[512,256]{1,0:T(8,128)(2,1)}, u32[]{:S(2)}) copy-start(bf16[512,256]{1,0:T(8,128)(2,1)} %constant.133.clone.table) | copy-start | bytes 786436
  135.0 6.2 %collective-permute-start.4 = (f32[864,128]{1,0:T(8,128)S(1)}, f32[864,128]{1,0:T(8,128)S(1)}, u32[]{:S(2)}, u32[]{:S(2)}) collective-permute-start(f32[864,128]{1,0:T(8,128)S(1)} %get-tuple-element.31), channel_id=1, source_target_pairs={{0,8},{8,0},{16,24},{24,16},{32,40},{40,32},{48,56},{56,48},{64,72... | collective-permute-start | bytes 1327112 | tf_op jit(solution)/shard_map/ppermute | solution.py:623
  137.6 20.0 %all-to-all-start.4 = ((f32[8,112,128]{2,1,0:T(8,128)}), f32[8,112,128]{2,1,0:T(8,128)S(1)}, u32[]{:S(2)}, u32[]{:S(2)}) async-start(f32[8,112,128]{2,1,0:T(8,128)} %bitcast.10), calls=%async_computation.4 | async-start | bytes 917504 | tf_op jit(solution)/shard_map/all_to_all | solution.py:626
  141.0 1.9 %collective-permute-start.3 = (f32[864,128]{1,0:T(8,128)S(1)}, f32[864,128]{1,0:T(8,128)S(1)}, u32[]{:S(2)}, u32[]{:S(2)}) collective-permute-start(f32[864,128]{1,0:T(8,128)S(1)} %get-tuple-element.29), channel_id=1, source_target_pairs={{0,8},{8,0},{16,24},{24,16},{32,40},{40,32},{48,56},{56,48},{64,72... | collective-permute-start | bytes 1327112 | tf_op jit(solution)/shard_map/ppermute | solution.py:623
  141.2 11.3 %collective-permute-start.5 = (f32[864,128]{1,0:T(8,128)S(1)}, f32[864,128]{1,0:T(8,128)S(1)}, u32[]{:S(2)}, u32[]{:S(2)}) collective-permute-start(f32[864,128]{1,0:T(8,128)S(1)} %add.117), channel_id=1, source_target_pairs={{0,128},{8,136},{16,144},{24,152},{32,160},{40,168},{48,176},{56,1... | collective-permute-start | bytes 1327112 | tf_op jit(solution)/shard_map/ppermute | solution.py:623
  158.3 2.3 %collective-permute-start.6 = (f32[12,288]{1,0:T(8,128)S(1)}, f32[12,288]{1,0:T(8,128)S(1)}, u32[]{:S(2)}, u32[]{:S(2)}) collective-permute-start(f32[12,288]{1,0:T(8,128)S(1)} %get-tuple-element.35), channel_id=1, source_target_pairs={{0,8},{8,0},{16,24},{24,16},{32,40},{40,32},{48,56},{56,48},{64,72... | collective-permute-start | bytes 41480 | tf_op jit(solution)/shard_map/ppermute | solution.py:623
  158.8 2.7 %collective-permute-start.7 = (f32[12,288]{1,0:T(8,128)S(1)}, f32[12,288]{1,0:T(8,128)S(1)}, u32[]{:S(2)}, u32[]{:S(2)}) collective-permute-start(f32[12,288]{1,0:T(8,128)S(1)} %get-tuple-element.36), channel_id=1, source_target_pairs={{0,128},{8,136},{16,144},{24,152},{32,160},{40,168},{48,176},{56,1... | collective-permute-start | bytes 41480 | tf_op jit(solution)/shard_map/ppermute | solution.py:623
  158.8 3.5 %collective-permute-start.8 = (f32[12,288]{1,0:T(8,128)S(1)}, f32[12,288]{1,0:T(8,128)S(1)}, u32[]{:S(2)}, u32[]{:S(2)}) collective-permute-start(f32[12,288]{1,0:T(8,128)S(1)} %get-tuple-element.37), channel_id=1, source_target_pairs={{0,136},{8,128},{16,152},{24,144},{32,168},{40,160},{48,184},{56,1... | collective-permute-start | bytes 41480 | tf_op jit(solution)/shard_map/ppermute | solution.py:623

commit v6 on v5

--- a/solution.py
+++ b/solution.py
@@ -77,7 +77,7 @@
     local = np.array([0, 1, 2, 3, 0, 1, 2, 3, 4, 5, 4, 5])[virtual]
     planes = np.array([[0, 1, 2, 3, 8, 9], [4, 5, 6, 7, 10, 11]])
     places = [
-        slot * 192 + part * 96 + 12 * f + planes[half][local] for half in range(2) for f in range(PARTS)
+        slot * 192 + part * 96 + 12 * f + planes[half][local] for f in range(PARTS) for half in range(2)
     ]
     return np.concatenate(places)
 
@@ -418,9 +418,9 @@
         for p, rest in enumerate(
             (jnp.where(upper, re, flip(im)), jnp.where(upper, flip(re), im))
         ):
-            out[p, g, 0:8, :] = packed[p][0]
-            out[p, g, 8:16, :] = packed[p][1]
-            out[p, g, 16:24, :] = rest
+            out[g, p, 0:8, :] = packed[p][0]
+            out[g, p, 8:16, :] = packed[p][1]
+            out[g, p, 16:24, :] = rest
         return carry
 
     lax.fori_loop(0, PARTS, send, 0, unroll=UNROLL)
@@ -445,9 +445,9 @@
     first = place[2] == 0
 
     def receive(g, carry):
-        rests = [blocks[p, g, 16:24, :] for p in range(2)]
+        rests = [blocks[g, p, 16:24, :] for p in range(2)]
         upper = top(rests[0])
-        parts = [(blocks[p, g, 0:8, :], blocks[p, g, 8:16, :]) for p in range(2)]
+        parts = [(blocks[g, p, 0:8, :], blocks[g, p, 8:16, :]) for p in range(2)]
         parts.append(
             (
                 jnp.where(upper, rests[0], flip(rests[1])),
@@ -600,7 +600,7 @@
     place = jnp.stack([core, line % 2, half]).astype(jnp.int32)
     z_groups = [[y * 16 + 2 * z + c for z in range(8)] for y in range(2) for c in range(2)]
     plane_groups = [
-        [(y * 16 + b) * PARTS + f for y in range(2) for f in range(PARTS)] for b in range(16)
+        [(y * 16 + b) * PARTS + f for f in range(PARTS) for y in range(2)] for b in range(16)
     ]
     scale = -mixing / (NX * NY * NZ)
 
@@ -632,9 +632,11 @@
 
     lists = f32(LIST, 128)
     keep, send = call(halves_kernel, (lists, lists), (orbitals.reshape(2, 12, PLANE),))
-    recv, coulomb = lax.optimization_barrier((swap(send, 16), coulomb))
+    upper, lower = swap(send[:576], 16), swap(send[576:], 16)
+    lower, coulomb = lax.optimization_barrier((lower, coulomb))
     keep_other = swap(keep, 1)
-    recv_other = swap(recv, 1)
+    recv = jnp.concatenate([upper, lower])
+    recv_other = jnp.concatenate([swap(upper, 1), swap(lower, 1)])
     serving = serve_order[core]
     near = serving // 16 == half
     same = serving % 2 == core
@@ -654,7 +656,7 @@
     rows = f32(ROWS, PLANE)
     blocks, mine, other = call(
         forward_kernel,
-        (f32(2, PARTS, ROWS, BLOCK), rows, rows),
+        (f32(PARTS, 2, ROWS, BLOCK), rows, rows),
         (served, keep, recv, keep_other, recv_other, table),
         scratch,
     )
@@ -667,7 +669,7 @@
         out_specs=whole,
         compiler_params=params,
     )(blocks, coulomb, tables)
-    blocks = plane_exchange(blocks).reshape(2, PARTS, ROWS, BLOCK)
+    blocks = plane_exchange(blocks).reshape(PARTS, 2, ROWS, BLOCK)
     table = jnp.asarray(np.concatenate(lane_table(1.0)))
     short = f32(TILES, 128)
     own_near, own_far, away_near, away_far, terms = call(

time: 164 us -> 167 us (1.018)
  starting transfers between devices: 22.9 us -> 25.4 us
    ppermute x9 -> x11, starting transfers between devices: 10.9 us -> 13.4 us  [swap(): return lax.ppermute(x, 'band', [(i, i ^ bits) for i in range(32)])]
    ppermute x9 -> x11, waiting for transfers between devices: 18.7 us -> 19.7 us  [swap(): return lax.ppermute(x, 'band', [(i, i ^ bits) for i in range(32)])]
  transfers between devices with their start and end apart: 11 -> 13, of which waited for: 7 -> 8; matrix products, arithmetic and copies ran while one was open for 2% -> 2% of each run, Pallas kernels for 1% -> 1%
where the time goes in v6:
time: 167 us
  blocking collectives  75.9 us (45%)
  waiting for transfers between devices  39.5 us (24%)
  starting transfers between devices  25.4 us (15%)
  Pallas kernels  17 us (10%)
  between operations  3.53 us (2%)
  other arithmetic  2.83 us (2%)
  local copies, waits for them, and re-layouts  2.41 us (1%)
    all_to_all x2, blocking collectives, plane_exchange(): lax.all_to_all(blocks, ('band', 'fft'), 0, 0, axis_index_groups=plane_gro...  57.1 us
    all_to_all x2, waiting for transfers between devices, line_exchange(): lax.all_to_all(blocks, 'band', 0, 0, axis_index_groups=z_groups, tiled=True)  19.8 us
    ppermute x11, waiting for transfers between devices, swap(): return lax.ppermute(x, 'band', [(i, i ^ bits) for i in range(32)])  19.7 us
    all_to_all x1, blocking collectives, line_exchange(): lax.all_to_all(blocks, 'band', 0, 0, axis_index_groups=z_groups, tiled=True)  18.8 us
    ppermute x11, starting transfers between devices, swap(): return lax.ppermute(x, 'band', [(i, i ^ bits) for i in range(32)])  13.4 us
    pallas_call x6, Pallas kernels, call(): pl.pallas_call(kernel, out_shape=shapes, in_specs=[scalars] + [whole] * l...  13 us
    all_to_all x2, starting transfers between devices, line_exchange(): lax.all_to_all(blocks, 'band', 0, 0, axis_index_groups=z_groups, tiled=True)  12 us
    pallas_call x1, Pallas kernels, shards(): pl.pallas_call(column_kernel, out_shape=f32(16, ROWS, BLOCK), in_specs=[w...  3.97 us
  transfers between devices with their start and end apart: 13, of which 8 were waited for; matrix products, arithmetic and copies ran while one was open for 2% of the time, Pallas kernels for 1%

profile of v6, /device:TPU:1, one launch (start us, length us, event | category | flops | bytes accessed | tf_op | source)
XLA Modules:
  0.0 166.6 jit_solution(4605323950616047443)
XLA Ops:
  0.7 1.4 copy.9
  2.1 0.0 copy-start.3
  2.2 0.1 pad_add_fusion.place
  2.2 0.7 shard_map.68
  3.0 2.2 %collective-permute-start.1 = (f32[320,128]{1,0:T(8,128)S(1)}, f32[320,128]{1,0:T(8,128)S(1)}, u32[]{:S(2)}, u32[]{:S(2)}) collective-permute-start(f32[320,128]{1,0:T(8,128)S(1)} %slice.7), channel_id=1, source_target_pairs={{0,128},{8,136},{16,144},{24,152},{32,160},{40,168},{48,176},{56,1... | collective-permute-start | bytes 491528 | tf_op jit(solution)/shard_map/ppermute | solution.py:623
  5.2 0.1 collective-permute-start
  5.3 3.1 %collective-permute-start.2 = (f32[896,128]{1,0:T(8,128)S(1)}, f32[896,128]{1,0:T(8,128)S(1)}, u32[]{:S(2)}, u32[]{:S(2)}) collective-permute-start(f32[896,128]{1,0:T(8,128)S(1)} %get-tuple-element.20.keep), channel_id=1, source_target_pairs={{0,8},{8,0},{16,24},{24,16},{32,40},{40,32},{48,56},{56,48},{64,72... | collective-permute-start | bytes 1376264 | tf_op jit(solution)/shard_map/ppermute | solution.py:623
  8.5 0.1 dynamic-slice_multiply_fusion
  8.5 0.1 broadcast_in_dim.28
  8.6 0.1 integer_pow.34
  8.7 0.1 integer_pow.35
  8.8 5.4 %collective-permute-done = f32[576,128]{1,0:T(8,128)S(1)} collective-permute-done((f32[576,128]{1,0:T(8,128)S(1)}, f32[576,128]{1,0:T(8,128)S(1)}, u32[]{:S(2)}, u32[]{:S(2)}) %collective-permute-start) | collective-permute-done | bytes 294944 | tf_op jit(solution)/shard_map/ppermute | solution.py:623
  14.2 2.5 %collective-permute-start.3 = (f32[576,128]{1,0:T(8,128)S(1)}, f32[576,128]{1,0:T(8,128)S(1)}, u32[]{:S(2)}, u32[]{:S(2)}) collective-permute-start(f32[576,128]{1,0:T(8,128)S(1)} %collective-permute-done), channel_id=1, source_target_pairs={{0,8},{8,0},{16,24},{24,16},{32,40},{40,32},{48,56},{56,48},{64,72... | collective-permute-start | bytes 884744 | tf_op jit(solution)/shard_map/ppermute | solution.py:623
  16.7 1.7 %fusion.coulomb = f32[96,1152]{1,0:T(8,128)S(1)} fusion(f32[1152]{0:T(1024)S(1)} %integer_pow.35, f32[1152]{0:T(1024)S(1)} %integer_pow.34, f32[96]{0:T(128)S(1)} %fusion.4), kind=kLoop, calls=%fused_computation.4 | loop fusion | flops 1105920 | bytes 451968 | tf_op jit(solution)/shard_map/mul | solution.py:607
  18.4 0.0 copy-done.3
  18.4 0.6 dynamic_slice.10
  21.6 0.0 collective-permute-done.1
  21.7 0.1 collective-permute-start.4
  21.8 0.0 collective-permute-done.3
  21.8 1.3 collective-permute-done.4
  23.2 0.0 collective-permute-done.2.keep_other
  23.2 0.9 select_select_fusion
  24.0 0.0 copy-start.2
  24.0 8.5 %all-to-all-start = ((f32[8,112,128]{2,1,0:T(8,128)}), f32[8,112,128]{2,1,0:T(8,128)S(1)}, u32[]{:S(2)}, u32[]{:S(2)}) async-start(f32[8,112,128]{2,1,0:T(8,128)} %bitcast.5), calls=%async_computation | async-start | bytes 917504 | tf_op jit(solution)/shard_map/all_to_all | solution.py:626
  32.5 16.6 %all-to-all-done = f32[8,112,128]{2,1,0:T(8,128)S(1)} async-done(((f32[8,112,128]{2,1,0:T(8,128)}), f32[8,112,128]{2,1,0:T(8,128)S(1)}, u32[]{:S(2)}, u32[]{:S(2)}) %all-to-all-start) | async-done | bytes 458784 | tf_op jit(solution)/shard_map/all_to_all | solution.py:626
  49.1 18.8 %all_to_all.25 = f32[8,112,128]{2,1,0:T(8,128)S(1)} all-to-all(f32[8,112,128]{2,1,0:T(8,128)S(1)} %broadcast_in_dim.32), channel_id=1, replica_groups={{0,16,32,48,64,80,96,112},{8,24,40,56,72,88,104,120},{128,144,160,176,1..., dimensions={0} | all-to-all | bytes 917504 | tf_op jit(solution)/shard_map/all_to_all | solution.py:626
  68.0 0.0 copy-done.2
  68.0 3.1 %shard_map.69 = (f32[8,2,24,1152]{3,2,1,0:T(8,128)S(1)}, f32[24,9216]{1,0:T(8,128)S(1)}, f32[24,9216]{1,0:T(8,128)S(1)}) custom-call(s32[3]{0:T(128)S(1)} %pad_add_fusion.place, f32[896,128]{1,0:T(8,128)S(1)} %bitcast.20, f32[896,128]{1,0:T(8,128)S(1)} %get-tuple-element.20.keep, f32[896,128]{1,0:T(8,128)S(1)} %constant_dynamic-update-slice_fusion.recv, ...), custom_call_target="tpu_custom_call" | custom-call | tf_op jit(solution)/shard_map/pallas_call | solution.py:613
  71.0 0.0 copy-start
  71.0 30.8 %all_to_all.26.blocks = f32[16,24,1152]{2,1,0:T(8,128)S(1)} all-to-all(f32[16,24,1152]{2,1,0:T(8,128)S(1)} %bitcast.23), channel_id=1, replica_groups={{0,128,1,129,2,130,3,131,4,132,5,133,6,134,7,135},{8,136,9,137,10,138,1..., dimensions={0} | all-to-all | bytes 3538944 | tf_op jit(solution)/shard_map/all_to_all | solution.py:629
  101.8 0.0 copy-done
  101.8 4.0 %shard_map.70 = f32[16,24,1152]{2,1,0:T(8,128)S(1)} custom-call(f32[16,24,1152]{2,1,0:T(8,128)S(1)} %all_to_all.26.blocks, f32[96,1152]{1,0:T(8,128)S(1)} %fusion.coulomb, bf16[1536,384]{1,0:T(8,128)(2,1)S(1)} %copy-done), custom_call_target="tpu_custom_call" | custom-call | tf_op jit(solution)/shard_map/pallas_call | solution.py:665
  105.8 0.0 copy-start.1
  105.8 26.3 %all_to_all.27 = f32[16,24,1152]{2,1,0:T(8,128)} all-to-all(f32[16,24,1152]{2,1,0:T(8,128)S(1)} %shard_map.70), channel_id=1, replica_groups={{0,128,1,129,2,130,3,131,4,132,5,133,6,134,7,135},{8,136,9,137,10,138,1..., dimensions={0} | all-to-all | bytes 3538944 | tf_op jit(solution)/shard_map/all_to_all | solution.py:629
  132.1 0.0 copy-done.1
  132.1 5.5 %shard_map.71 = (f32[864,128]{1,0:T(8,128)S(1)}, f32[864,128]{1,0:T(8,128)S(1)}, f32[864,128]{1,0:T(8,128)S(1)}, f32[864,128]{1,0:T(8,128)S(1)}, f32[896,128]{1,0:T(8,128)}) custom-call(s32[3]{0:T(128)S(1)} %pad_add_fusion.place, f32[8,2,24,1152]{3,2,1,0:T(8,128)} %bitcast.24, f32[896,128]{1,0:T(8,128)S(1)} %bitcast.21, ...), custom_call_target="tpu_custom_call" | custom-call | tf_op jit(solution)/shard_map/pallas_call | solution.py:613
  137.6 2.7 %collective-permute-start.6 = (f32[864,128]{1,0:T(8,128)S(1)}, f32[864,128]{1,0:T(8,128)S(1)}, u32[]{:S(2)}, u32[]{:S(2)}) collective-permute-start(f32[864,128]{1,0:T(8,128)S(1)} %get-tuple-element.31), channel_id=1, source_target_pairs={{0,8},{8,0},{16,24},{24,16},{32,40},{40,32},{48,56},{56,48},{64,72... | collective-permute-start | bytes 1327112 | tf_op jit(solution)/shard_map/ppermute | solution.py:623
  140.3 3.5 %all-to-all-start.4 = ((f32[8,112,128]{2,1,0:T(8,128)}), f32[8,112,128]{2,1,0:T(8,128)S(1)}, u32[]{:S(2)}, u32[]{:S(2)}) async-start(f32[8,112,128]{2,1,0:T(8,128)} %bitcast.10), calls=%async_computation.4 | async-start | bytes 917504 | tf_op jit(solution)/shard_map/all_to_all | solution.py:626
  143.8 0.1 collective-permute-start.5
  143.9 0.0 collective-permute-done.6
  143.9 0.1 add.117
  144.0 0.4 collective-permute-start.7
  144.3 1.3 collective-permute-done.5.got
  145.7 9.6 %collective-permute-done.7.far = f32[864,128]{1,0:T(8,128)S(1)} collective-permute-done((f32[864,128]{1,0:T(8,128)S(1)}, f32[864,128]{1,0:T(8,128)S(1)}, u32[]{:S(2)}, u32[]{:S(2)}) %collective-permute-start.7) | collective-permute-done | bytes 442400 | tf_op jit(solution)/shard_map/ppermute | solution.py:623
  155.3 1.8 %shard_map.72 = f32[12,2,9216]{2,1,0:T(2,128)} custom-call(s32[3]{0:T(128)S(1)} %pad_add_fusion.place, f32[864,128]{1,0:T(8,128)S(1)} %get-tuple-element.28.near, f32[864,128]{1,0:T(8,128)S(1)} %collective-permute-done.5.got, f32[864,128]{1,0:T(8,128)S(1)} %collective-permute-done.7.far), custom_call_target="tpu_custom_call" | custom-call | tf_op jit(solution)/shard_map/pallas_call | solution.py:613
  157.1 3.2 %all-to-all-done.4 = f32[8,112,128]{2,1,0:T(8,128)S(1)} async-done(((f32[8,112,128]{2,1,0:T(8,128)}), f32[8,112,128]{2,1,0:T(8,128)S(1)}, u32[]{:S(2)}, u32[]{:S(2)}) %all-to-all-start.4) | async-done | bytes 458784 | tf_op jit(solution)/shard_map/all_to_all | solution.py:626
  160.3 0.7 shard_map.73
  161.0 0.5 collective-permute-start.8
  161.6 0.3 collective-permute-start.9
  161.9 1.4 collective-permute-start.10
  163.3 0.0 collective-permute-done.8.p01
  163.3 1.0 collective-permute-done.9.p10
  164.3 1.1 collective-permute-done.10.p11
  165.4 1.2 shard_map.74
  (11 shorter events, 0.2 us)
Async XLA Ops:
  2.1 16.3 %copy-start.3 = (s32[32]{0:T(128)S(1)}, s32[32]{0:T(128)}, u32[]{:S(2)}) copy-start(s32[32]{0:T(128)} %param.6) | copy-start | bytes 388
  3.0 18.7 %collective-permute-start.1 = (f32[320,128]{1,0:T(8,128)S(1)}, f32[320,128]{1,0:T(8,128)S(1)}, u32[]{:S(2)}, u32[]{:S(2)}) collective-permute-start(f32[320,128]{1,0:T(8,128)S(1)} %slice.7), channel_id=1, source_target_pairs={{0,128},{8,136},{16,144},{24,152},{32,160},{40,168},{48,176},{56,1... | collective-permute-start | bytes 491528 | tf_op jit(solution)/shard_map/ppermute | solution.py:623
  5.2 9.0 %collective-permute-start = (f32[576,128]{1,0:T(8,128)S(1)}, f32[576,128]{1,0:T(8,128)S(1)}, u32[]{:S(2)}, u32[]{:S(2)}) collective-permute-start(f32[576,128]{1,0:T(8,128)S(1)} %slice.6), channel_id=1, source_target_pairs={{0,128},{8,136},{16,144},{24,152},{32,160},{40,168},{48,176},{56,1... | collective-permute-start | bytes 884744 | tf_op jit(solution)/shard_map/ppermute | solution.py:623
  5.3 17.8 %collective-permute-start.2 = (f32[896,128]{1,0:T(8,128)S(1)}, f32[896,128]{1,0:T(8,128)S(1)}, u32[]{:S(2)}, u32[]{:S(2)}) collective-permute-start(f32[896,128]{1,0:T(8,128)S(1)} %get-tuple-element.20.keep), channel_id=1, source_target_pairs={{0,8},{8,0},{16,24},{24,16},{32,40},{40,32},{48,56},{56,48},{64,72... | collective-permute-start | bytes 1376264 | tf_op jit(solution)/shard_map/ppermute | solution.py:623
  14.2 7.6 %collective-permute-start.3 = (f32[576,128]{1,0:T(8,128)S(1)}, f32[576,128]{1,0:T(8,128)S(1)}, u32[]{:S(2)}, u32[]{:S(2)}) collective-permute-start(f32[576,128]{1,0:T(8,128)S(1)} %collective-permute-done), channel_id=1, source_target_pairs={{0,8},{8,0},{16,24},{24,16},{32,40},{40,32},{48,56},{56,48},{64,72... | collective-permute-start | bytes 884744 | tf_op jit(solution)/shard_map/ppermute | solution.py:623
  21.7 1.5 collective-permute-start.4
  24.0 43.9 %copy-start.2 = (bf16[512,256]{1,0:T(8,128)(2,1)S(1)}, bf16[512,256]{1,0:T(8,128)(2,1)}, u32[]{:S(2)}) copy-start(bf16[512,256]{1,0:T(8,128)(2,1)} %constant.131.clone.table) | copy-start | bytes 786436
  24.0 25.0 %all-to-all-start = ((f32[8,112,128]{2,1,0:T(8,128)}), f32[8,112,128]{2,1,0:T(8,128)S(1)}, u32[]{:S(2)}, u32[]{:S(2)}) async-start(f32[8,112,128]{2,1,0:T(8,128)} %bitcast.5), calls=%async_computation | async-start | bytes 917504 | tf_op jit(solution)/shard_map/all_to_all | solution.py:626
  71.0 30.8 %copy-start = (bf16[1536,384]{1,0:T(8,128)(2,1)S(1)}, bf16[1536,384]{1,0:T(8,128)(2,1)}, u32[]{:S(2)}) copy-start(bf16[1536,384]{1,0:T(8,128)(2,1)} %constant.132.clone.tables) | copy-start | bytes 3538948
  105.8 26.3 %copy-start.1 = (bf16[512,256]{1,0:T(8,128)(2,1)S(1)}, bf16[512,256]{1,0:T(8,128)(2,1)}, u32[]{:S(2)}) copy-start(bf16[512,256]{1,0:T(8,128)(2,1)} %constant.133.clone.table) | copy-start | bytes 786436
  137.6 6.3 %collective-permute-start.6 = (f32[864,128]{1,0:T(8,128)S(1)}, f32[864,128]{1,0:T(8,128)S(1)}, u32[]{:S(2)}, u32[]{:S(2)}) collective-permute-start(f32[864,128]{1,0:T(8,128)S(1)} %get-tuple-element.31), channel_id=1, source_target_pairs={{0,8},{8,0},{16,24},{24,16},{32,40},{40,32},{48,56},{56,48},{64,72... | collective-permute-start | bytes 1327112 | tf_op jit(solution)/shard_map/ppermute | solution.py:623
  140.3 20.0 %all-to-all-start.4 = ((f32[8,112,128]{2,1,0:T(8,128)}), f32[8,112,128]{2,1,0:T(8,128)S(1)}, u32[]{:S(2)}, u32[]{:S(2)}) async-start(f32[8,112,128]{2,1,0:T(8,128)} %bitcast.10), calls=%async_computation.4 | async-start | bytes 917504 | tf_op jit(solution)/shard_map/all_to_all | solution.py:626
  143.8 1.9 %collective-permute-start.5 = (f32[864,128]{1,0:T(8,128)S(1)}, f32[864,128]{1,0:T(8,128)S(1)}, u32[]{:S(2)}, u32[]{:S(2)}) collective-permute-start(f32[864,128]{1,0:T(8,128)S(1)} %get-tuple-element.29), channel_id=1, source_target_pairs={{0,8},{8,0},{16,24},{24,16},{32,40},{40,32},{48,56},{56,48},{64,72... | collective-permute-start | bytes 1327112 | tf_op jit(solution)/shard_map/ppermute | solution.py:623
  144.0 11.3 %collective-permute-start.7 = (f32[864,128]{1,0:T(8,128)S(1)}, f32[864,128]{1,0:T(8,128)S(1)}, u32[]{:S(2)}, u32[]{:S(2)}) collective-permute-start(f32[864,128]{1,0:T(8,128)S(1)} %add.117), channel_id=1, source_target_pairs={{0,128},{8,136},{16,144},{24,152},{32,160},{40,168},{48,176},{56,1... | collective-permute-start | bytes 1327112 | tf_op jit(solution)/shard_map/ppermute | solution.py:623
  161.0 2.3 %collective-permute-start.8 = (f32[12,288]{1,0:T(8,128)S(1)}, f32[12,288]{1,0:T(8,128)S(1)}, u32[]{:S(2)}, u32[]{:S(2)}) collective-permute-start(f32[12,288]{1,0:T(8,128)S(1)} %get-tuple-element.35), channel_id=1, source_target_pairs={{0,8},{8,0},{16,24},{24,16},{32,40},{40,32},{48,56},{56,48},{64,72... | collective-permute-start | bytes 41480 | tf_op jit(solution)/shard_map/ppermute | solution.py:623
  161.6 2.7 %collective-permute-start.9 = (f32[12,288]{1,0:T(8,128)S(1)}, f32[12,288]{1,0:T(8,128)S(1)}, u32[]{:S(2)}, u32[]{:S(2)}) collective-permute-start(f32[12,288]{1,0:T(8,128)S(1)} %get-tuple-element.36), channel_id=1, source_target_pairs={{0,128},{8,136},{16,144},{24,152},{32,160},{40,168},{48,176},{56,1... | collective-permute-start | bytes 41480 | tf_op jit(solution)/shard_map/ppermute | solution.py:623
  161.9 3.5 %collective-permute-start.10 = (f32[12,288]{1,0:T(8,128)S(1)}, f32[12,288]{1,0:T(8,128)S(1)}, u32[]{:S(2)}, u32[]{:S(2)}) collective-permute-start(f32[12,288]{1,0:T(8,128)S(1)} %get-tuple-element.37), channel_id=1, source_target_pairs={{0,136},{8,128},{16,152},{24,144},{32,168},{40,160},{48,184},{56,1... | collective-permute-start | bytes 41480 | tf_op jit(solution)/shard_map/ppermute | solution.py:623

commit v7 on v6

--- a/solution.py
+++ b/solution.py
@@ -632,11 +632,9 @@
 
     lists = f32(LIST, 128)
     keep, send = call(halves_kernel, (lists, lists), (orbitals.reshape(2, 12, PLANE),))
-    upper, lower = swap(send[:576], 16), swap(send[576:], 16)
-    lower, coulomb = lax.optimization_barrier((lower, coulomb))
+    recv, coulomb = lax.optimization_barrier((swap(send, 16), coulomb))
     keep_other = swap(keep, 1)
-    recv = jnp.concatenate([upper, lower])
-    recv_other = jnp.concatenate([swap(upper, 1), swap(lower, 1)])
+    recv_other = swap(recv, 1)
     serving = serve_order[core]
     near = serving // 16 == half
     same = serving % 2 == core

time: 167 us -> 164 us (0.982)
  starting transfers between devices: 25.4 us -> 23.3 us
    ppermute x11 -> x9, starting transfers between devices: 13.4 us -> 11.3 us  [swap(): return lax.ppermute(x, 'band', [(i, i ^ bits) for i in range(32)])]
    ppermute x11 -> x9, waiting for transfers between devices: 19.7 us -> 18.7 us  [swap(): return lax.ppermute(x, 'band', [(i, i ^ bits) for i in range(32)])]
  transfers between devices with their start and end apart: 13 -> 11, of which waited for: 8 -> 7; matrix products, arithmetic and copies ran while one was open for 2% -> 2% of each run, Pallas kernels for 1% -> 1%
where the time goes in v7:
time: 164 us; the launch traced here: 163 us
  blocking collectives  76 us (46%)
  waiting for transfers between devices  38.6 us (24%)
  starting transfers between devices  23.3 us (14%)
  Pallas kernels  17 us (10%)
  between operations  3.46 us (2%)
  other arithmetic  2.83 us (2%)
  local copies, waits for them, and re-layouts  2.31 us (1%)
    all_to_all x2, blocking collectives, plane_exchange(): lax.all_to_all(blocks, ('band', 'fft'), 0, 0, axis_index_groups=plane_gro...  57.1 us
    all_to_all x2, waiting for transfers between devices, line_exchange(): lax.all_to_all(blocks, 'band', 0, 0, axis_index_groups=z_groups, tiled=True)  19.9 us
    all_to_all x1, blocking collectives, line_exchange(): lax.all_to_all(blocks, 'band', 0, 0, axis_index_groups=z_groups, tiled=True)  18.9 us
    ppermute x9, waiting for transfers between devices, swap(): return lax.ppermute(x, 'band', [(i, i ^ bits) for i in range(32)])  18.7 us
    pallas_call x6, Pallas kernels, call(): pl.pallas_call(kernel, out_shape=shapes, in_specs=[scalars] + [whole] * l...  13 us
    all_to_all x2, starting transfers between devices, line_exchange(): lax.all_to_all(blocks, 'band', 0, 0, axis_index_groups=z_groups, tiled=True)  12 us
    ppermute x9, starting transfers between devices, swap(): return lax.ppermute(x, 'band', [(i, i ^ bits) for i in range(32)])  11.3 us
    pallas_call x1, Pallas kernels, shards(): pl.pallas_call(column_kernel, out_shape=f32(16, ROWS, BLOCK), in_specs=[w...  3.97 us
  transfers between devices with their start and end apart: 11, of which 7 were waited for; matrix products, arithmetic and copies ran while one was open for 2% of the time, Pallas kernels for 1%

profile of v7, /device:TPU:1, one launch (start us, length us, event | category | flops | bytes accessed | tf_op | source)
XLA Modules:
  0.0 163.4 jit_solution(2113535050392874867)
XLA Ops:
  0.7 0.0 copy-start.3
  0.7 1.4 copy.9
  2.2 0.1 pad_add_fusion.place
  2.2 0.7 shard_map.68
  3.0 2.2 %collective-permute-start = (f32[896,128]{1,0:T(8,128)S(1)}, f32[896,128]{1,0:T(8,128)S(1)}, u32[]{:S(2)}, u32[]{:S(2)}) collective-permute-start(f32[896,128]{1,0:T(8,128)S(1)} %get-tuple-element.21), channel_id=1, source_target_pairs={{0,128},{8,136},{16,144},{24,152},{32,160},{40,168},{48,176},{56,1... | collective-permute-start | bytes 1376264 | tf_op jit(solution)/shard_map/ppermute | solution.py:623
  5.2 1.2 collective-permute-start.1
  6.4 0.1 dynamic-slice_multiply_fusion
  6.5 0.1 broadcast_in_dim.28
  6.6 0.1 integer_pow.34
  6.7 0.1 integer_pow.35
  6.7 1.7 %fusion.coulomb = f32[96,1152]{1,0:T(8,128)S(1)} fusion(f32[1152]{0:T(1024)S(1)} %integer_pow.35, f32[1152]{0:T(1024)S(1)} %integer_pow.34, f32[96]{0:T(128)S(1)} %fusion.4), kind=kLoop, calls=%fused_computation.4 | loop fusion | flops 1105920 | bytes 451968 | tf_op jit(solution)/shard_map/mul | solution.py:607
  8.5 5.7 %collective-permute-done.recv = f32[896,128]{1,0:T(8,128)S(1)} collective-permute-done((f32[896,128]{1,0:T(8,128)S(1)}, f32[896,128]{1,0:T(8,128)S(1)}, u32[]{:S(2)}, u32[]{:S(2)}) %collective-permute-start) | collective-permute-done | bytes 458784 | tf_op jit(solution)/shard_map/ppermute | solution.py:623
  14.2 2.5 %collective-permute-start.2 = (f32[896,128]{1,0:T(8,128)S(1)}, f32[896,128]{1,0:T(8,128)S(1)}, u32[]{:S(2)}, u32[]{:S(2)}) collective-permute-start(f32[896,128]{1,0:T(8,128)S(1)} %collective-permute-done.recv), channel_id=1, source_target_pairs={{0,8},{8,0},{16,24},{24,16},{32,40},{40,32},{48,56},{56,48},{64,72... | collective-permute-start | bytes 1376264 | tf_op jit(solution)/shard_map/ppermute | solution.py:623
  16.7 0.0 copy-done.3
  16.7 0.6 dynamic_slice.10
  19.9 0.0 collective-permute-done.1.keep_other
  19.9 0.0 collective-permute-done.2.recv_other
  19.9 0.9 select_select_fusion
  20.7 0.0 copy-start.2
  20.7 8.5 %all-to-all-start = ((f32[8,112,128]{2,1,0:T(8,128)}), f32[8,112,128]{2,1,0:T(8,128)S(1)}, u32[]{:S(2)}, u32[]{:S(2)}) async-start(f32[8,112,128]{2,1,0:T(8,128)} %bitcast.5), calls=%async_computation | async-start | bytes 917504 | tf_op jit(solution)/shard_map/all_to_all | solution.py:626
  29.2 16.6 %all-to-all-done = f32[8,112,128]{2,1,0:T(8,128)S(1)} async-done(((f32[8,112,128]{2,1,0:T(8,128)}), f32[8,112,128]{2,1,0:T(8,128)S(1)}, u32[]{:S(2)}, u32[]{:S(2)}) %all-to-all-start) | async-done | bytes 458784 | tf_op jit(solution)/shard_map/all_to_all | solution.py:626
  45.9 18.9 %all_to_all.25 = f32[8,112,128]{2,1,0:T(8,128)S(1)} all-to-all(f32[8,112,128]{2,1,0:T(8,128)S(1)} %broadcast_in_dim.32), channel_id=1, replica_groups={{0,16,32,48,64,80,96,112},{8,24,40,56,72,88,104,120},{128,144,160,176,1..., dimensions={0} | all-to-all | bytes 917504 | tf_op jit(solution)/shard_map/all_to_all | solution.py:626
  64.8 0.0 copy-done.2
  64.8 3.1 %shard_map.69 = (f32[8,2,24,1152]{3,2,1,0:T(8,128)S(1)}, f32[24,9216]{1,0:T(8,128)S(1)}, f32[24,9216]{1,0:T(8,128)S(1)}) custom-call(s32[3]{0:T(128)S(1)} %pad_add_fusion.place, f32[896,128]{1,0:T(8,128)S(1)} %bitcast.20, f32[896,128]{1,0:T(8,128)S(1)} %get-tuple-element.20.keep, f32[896,128]{1,0:T(8,128)S(1)} %collective-permute-done.recv, ...), custom_call_target="tpu_custom_call" | custom-call | tf_op jit(solution)/shard_map/pallas_call | solution.py:613
  67.8 0.0 copy-start
  67.8 30.8 %all_to_all.26.blocks = f32[16,24,1152]{2,1,0:T(8,128)S(1)} all-to-all(f32[16,24,1152]{2,1,0:T(8,128)S(1)} %bitcast.23), channel_id=1, replica_groups={{0,128,1,129,2,130,3,131,4,132,5,133,6,134,7,135},{8,136,9,137,10,138,1..., dimensions={0} | all-to-all | bytes 3538944 | tf_op jit(solution)/shard_map/all_to_all | solution.py:629
  98.6 0.0 copy-done
  98.6 4.0 %shard_map.70 = f32[16,24,1152]{2,1,0:T(8,128)S(1)} custom-call(f32[16,24,1152]{2,1,0:T(8,128)S(1)} %all_to_all.26.blocks, f32[96,1152]{1,0:T(8,128)S(1)} %fusion.coulomb, bf16[1536,384]{1,0:T(8,128)(2,1)S(1)} %copy-done), custom_call_target="tpu_custom_call" | custom-call | tf_op jit(solution)/shard_map/pallas_call | solution.py:663
  102.6 0.0 copy-start.1
  102.6 26.3 %all_to_all.27 = f32[16,24,1152]{2,1,0:T(8,128)} all-to-all(f32[16,24,1152]{2,1,0:T(8,128)S(1)} %shard_map.70), channel_id=1, replica_groups={{0,128,1,129,2,130,3,131,4,132,5,133,6,134,7,135},{8,136,9,137,10,138,1..., dimensions={0} | all-to-all | bytes 3538944 | tf_op jit(solution)/shard_map/all_to_all | solution.py:629
  128.9 0.0 copy-done.1
  128.9 5.5 %shard_map.71 = (f32[864,128]{1,0:T(8,128)S(1)}, f32[864,128]{1,0:T(8,128)S(1)}, f32[864,128]{1,0:T(8,128)S(1)}, f32[864,128]{1,0:T(8,128)S(1)}, f32[896,128]{1,0:T(8,128)}) custom-call(s32[3]{0:T(128)S(1)} %pad_add_fusion.place, f32[8,2,24,1152]{3,2,1,0:T(8,128)} %bitcast.24, f32[896,128]{1,0:T(8,128)S(1)} %bitcast.21, ...), custom_call_target="tpu_custom_call" | custom-call | tf_op jit(solution)/shard_map/pallas_call | solution.py:613
  134.4 2.7 %collective-permute-start.4 = (f32[864,128]{1,0:T(8,128)S(1)}, f32[864,128]{1,0:T(8,128)S(1)}, u32[]{:S(2)}, u32[]{:S(2)}) collective-permute-start(f32[864,128]{1,0:T(8,128)S(1)} %get-tuple-element.31), channel_id=1, source_target_pairs={{0,8},{8,0},{16,24},{24,16},{32,40},{40,32},{48,56},{56,48},{64,72... | collective-permute-start | bytes 1327112 | tf_op jit(solution)/shard_map/ppermute | solution.py:623
  137.1 3.5 %all-to-all-start.4 = ((f32[8,112,128]{2,1,0:T(8,128)}), f32[8,112,128]{2,1,0:T(8,128)S(1)}, u32[]{:S(2)}, u32[]{:S(2)}) async-start(f32[8,112,128]{2,1,0:T(8,128)} %bitcast.10), calls=%async_computation.4 | async-start | bytes 917504 | tf_op jit(solution)/shard_map/all_to_all | solution.py:626
  140.6 0.1 collective-permute-start.3
  140.7 0.0 collective-permute-done.4
  140.7 0.1 add.117
  140.8 0.4 collective-permute-start.5
  141.1 1.3 collective-permute-done.3.got
  142.5 9.6 %collective-permute-done.5.far = f32[864,128]{1,0:T(8,128)S(1)} collective-permute-done((f32[864,128]{1,0:T(8,128)S(1)}, f32[864,128]{1,0:T(8,128)S(1)}, u32[]{:S(2)}, u32[]{:S(2)}) %collective-permute-start.5) | collective-permute-done | bytes 442400 | tf_op jit(solution)/shard_map/ppermute | solution.py:623
  152.1 1.8 %shard_map.72 = f32[12,2,9216]{2,1,0:T(2,128)} custom-call(s32[3]{0:T(128)S(1)} %pad_add_fusion.place, f32[864,128]{1,0:T(8,128)S(1)} %get-tuple-element.28.near, f32[864,128]{1,0:T(8,128)S(1)} %collective-permute-done.3.got, f32[864,128]{1,0:T(8,128)S(1)} %collective-permute-done.5.far), custom_call_target="tpu_custom_call" | custom-call | tf_op jit(solution)/shard_map/pallas_call | solution.py:613
  153.9 3.2 %all-to-all-done.4 = f32[8,112,128]{2,1,0:T(8,128)S(1)} async-done(((f32[8,112,128]{2,1,0:T(8,128)}), f32[8,112,128]{2,1,0:T(8,128)S(1)}, u32[]{:S(2)}, u32[]{:S(2)}) %all-to-all-start.4) | async-done | bytes 458784 | tf_op jit(solution)/shard_map/all_to_all | solution.py:626
  157.2 0.7 shard_map.73
  157.9 0.5 collective-permute-start.6
  158.4 0.3 collective-permute-start.7
  158.7 1.4 collective-permute-start.8
  160.1 0.0 collective-permute-done.6.p01
  160.1 1.0 collective-permute-done.7.p10
  161.1 1.1 collective-permute-done.8.p11
  162.2 1.2 shard_map.74
  (5 shorter events, 0.1 us)
Async XLA Ops:
  0.7 16.0 %copy-start.3 = (s32[32]{0:T(128)S(1)}, s32[32]{0:T(128)}, u32[]{:S(2)}) copy-start(s32[32]{0:T(128)} %param.6) | copy-start | bytes 388
  3.0 11.2 %collective-permute-start = (f32[896,128]{1,0:T(8,128)S(1)}, f32[896,128]{1,0:T(8,128)S(1)}, u32[]{:S(2)}, u32[]{:S(2)}) collective-permute-start(f32[896,128]{1,0:T(8,128)S(1)} %get-tuple-element.21), channel_id=1, source_target_pairs={{0,128},{8,136},{16,144},{24,152},{32,160},{40,168},{48,176},{56,1... | collective-permute-start | bytes 1376264 | tf_op jit(solution)/shard_map/ppermute | solution.py:623
  5.2 14.7 %collective-permute-start.1 = (f32[896,128]{1,0:T(8,128)S(1)}, f32[896,128]{1,0:T(8,128)S(1)}, u32[]{:S(2)}, u32[]{:S(2)}) collective-permute-start(f32[896,128]{1,0:T(8,128)S(1)} %get-tuple-element.20.keep), channel_id=1, source_target_pairs={{0,8},{8,0},{16,24},{24,16},{32,40},{40,32},{48,56},{56,48},{64,72... | collective-permute-start | bytes 1376264 | tf_op jit(solution)/shard_map/ppermute | solution.py:623
  14.2 5.7 %collective-permute-start.2 = (f32[896,128]{1,0:T(8,128)S(1)}, f32[896,128]{1,0:T(8,128)S(1)}, u32[]{:S(2)}, u32[]{:S(2)}) collective-permute-start(f32[896,128]{1,0:T(8,128)S(1)} %collective-permute-done.recv), channel_id=1, source_target_pairs={{0,8},{8,0},{16,24},{24,16},{32,40},{40,32},{48,56},{56,48},{64,72... | collective-permute-start | bytes 1376264 | tf_op jit(solution)/shard_map/ppermute | solution.py:623
  20.7 44.0 %copy-start.2 = (bf16[512,256]{1,0:T(8,128)(2,1)S(1)}, bf16[512,256]{1,0:T(8,128)(2,1)}, u32[]{:S(2)}) copy-start(bf16[512,256]{1,0:T(8,128)(2,1)} %constant.131.clone.table) | copy-start | bytes 786436
  20.7 25.1 %all-to-all-start = ((f32[8,112,128]{2,1,0:T(8,128)}), f32[8,112,128]{2,1,0:T(8,128)S(1)}, u32[]{:S(2)}, u32[]{:S(2)}) async-start(f32[8,112,128]{2,1,0:T(8,128)} %bitcast.5), calls=%async_computation | async-start | bytes 917504 | tf_op jit(solution)/shard_map/all_to_all | solution.py:626
  67.8 30.8 %copy-start = (bf16[1536,384]{1,0:T(8,128)(2,1)S(1)}, bf16[1536,384]{1,0:T(8,128)(2,1)}, u32[]{:S(2)}) copy-start(bf16[1536,384]{1,0:T(8,128)(2,1)} %constant.132.clone.tables) | copy-start | bytes 3538948
  102.6 26.3 %copy-start.1 = (bf16[512,256]{1,0:T(8,128)(2,1)S(1)}, bf16[512,256]{1,0:T(8,128)(2,1)}, u32[]{:S(2)}) copy-start(bf16[512,256]{1,0:T(8,128)(2,1)} %constant.133.clone.table) | copy-start | bytes 786436
  134.4 6.3 %collective-permute-start.4 = (f32[864,128]{1,0:T(8,128)S(1)}, f32[864,128]{1,0:T(8,128)S(1)}, u32[]{:S(2)}, u32[]{:S(2)}) collective-permute-start(f32[864,128]{1,0:T(8,128)S(1)} %get-tuple-element.31), channel_id=1, source_target_pairs={{0,8},{8,0},{16,24},{24,16},{32,40},{40,32},{48,56},{56,48},{64,72... | collective-permute-start | bytes 1327112 | tf_op jit(solution)/shard_map/ppermute | solution.py:623
  137.1 20.0 %all-to-all-start.4 = ((f32[8,112,128]{2,1,0:T(8,128)}), f32[8,112,128]{2,1,0:T(8,128)S(1)}, u32[]{:S(2)}, u32[]{:S(2)}) async-start(f32[8,112,128]{2,1,0:T(8,128)} %bitcast.10), calls=%async_computation.4 | async-start | bytes 917504 | tf_op jit(solution)/shard_map/all_to_all | solution.py:626
  140.6 1.9 %collective-permute-start.3 = (f32[864,128]{1,0:T(8,128)S(1)}, f32[864,128]{1,0:T(8,128)S(1)}, u32[]{:S(2)}, u32[]{:S(2)}) collective-permute-start(f32[864,128]{1,0:T(8,128)S(1)} %get-tuple-element.29), channel_id=1, source_target_pairs={{0,8},{8,0},{16,24},{24,16},{32,40},{40,32},{48,56},{56,48},{64,72... | collective-permute-start | bytes 1327112 | tf_op jit(solution)/shard_map/ppermute | solution.py:623
  140.8 11.3 %collective-permute-start.5 = (f32[864,128]{1,0:T(8,128)S(1)}, f32[864,128]{1,0:T(8,128)S(1)}, u32[]{:S(2)}, u32[]{:S(2)}) collective-permute-start(f32[864,128]{1,0:T(8,128)S(1)} %add.117), channel_id=1, source_target_pairs={{0,128},{8,136},{16,144},{24,152},{32,160},{40,168},{48,176},{56,1... | collective-permute-start | bytes 1327112 | tf_op jit(solution)/shard_map/ppermute | solution.py:623
  157.9 2.3 %collective-permute-start.6 = (f32[12,288]{1,0:T(8,128)S(1)}, f32[12,288]{1,0:T(8,128)S(1)}, u32[]{:S(2)}, u32[]{:S(2)}) collective-permute-start(f32[12,288]{1,0:T(8,128)S(1)} %get-tuple-element.35), channel_id=1, source_target_pairs={{0,8},{8,0},{16,24},{24,16},{32,40},{40,32},{48,56},{56,48},{64,72... | collective-permute-start | bytes 41480 | tf_op jit(solution)/shard_map/ppermute | solution.py:623
  158.4 2.7 %collective-permute-start.7 = (f32[12,288]{1,0:T(8,128)S(1)}, f32[12,288]{1,0:T(8,128)S(1)}, u32[]{:S(2)}, u32[]{:S(2)}) collective-permute-start(f32[12,288]{1,0:T(8,128)S(1)} %get-tuple-element.36), channel_id=1, source_target_pairs={{0,128},{8,136},{16,144},{24,152},{32,160},{40,168},{48,176},{56,1... | collective-permute-start | bytes 41480 | tf_op jit(solution)/shard_map/ppermute | solution.py:623
  158.7 3.5 %collective-permute-start.8 = (f32[12,288]{1,0:T(8,128)S(1)}, f32[12,288]{1,0:T(8,128)S(1)}, u32[]{:S(2)}, u32[]{:S(2)}) collective-permute-start(f32[12,288]{1,0:T(8,128)S(1)} %get-tuple-element.37), channel_id=1, source_target_pairs={{0,136},{8,128},{16,152},{24,144},{32,168},{40,160},{48,184},{56,1... | collective-permute-start | bytes 41480 | tf_op jit(solution)/shard_map/ppermute | solution.py:623
